TPU v7x, 32 devices: a whole 2x2x4 slice. The times are simulated.
32 devices in a mesh: seq: 4 (over y, core), neur: 8 (over z, x).
Axes of the slice: x: 2, y: 2, z: 4, core: 2. Of those that a mesh axis runs over, the one named last changes fastest.
Arguments:
- inputs: bfloat16 [2048, 16384], P('neur', 'seq'), may hold values from -6 to 6
- weight_one: bfloat16 [2048, 2048], P('neur'), may hold values from -0.125 to 0.125
- weight_two: bfloat16 [2048, 2048], P('neur'), may hold values from -0.125 to 0.125
- gain_one: float32 [2048], P('neur'), may hold values from 0.5 to 1.5
- gain_two: float32 [2048], P('neur'), may hold values from 0.5 to 1.5
- bias_one: float32 [2048], P('neur'), may hold values from -3 to 3
- bias_two: float32 [2048], P('neur'), may hold values from -3 to 3
- decay_one: float32 [2048], P('neur'), may hold values from 0.95 to 0.9995
- decay_two: float32 [2048], P('neur'), may hold values from 0.95 to 0.9995
- lengths: int32 [4, 12], P('seq'), may hold values from 1 to 1024, 3584 in all within a row
- frame_mask: int32 [16384], P('seq'), may hold values 0 or 1
- out_grad: bfloat16 [2048, 16384], P('neur', 'seq'), may hold values from -6 to 6
Outputs:
- output: float32 [2048, 16384], P('neur', 'seq')
- input_grad: float32 [2048, 16384], P('neur', 'seq')
- weight_one_grad: float32 [2048, 2048], P('neur')
- gain_one_grad: float32 [2048], P('neur')
- bias_one_grad: float32 [2048], P('neur')
- decay_one_grad: float32 [2048], P('neur')
- weight_two_grad: float32 [2048, 2048], P('neur')
- gain_two_grad: float32 [2048], P('neur')
- bias_two_grad: float32 [2048], P('neur')
- decay_two_grad: float32 [2048], P('neur')
Inputs may be any that keep to these rules, and one draw needn't show every extreme that they name: `lengths`: row b lists the 12 sequences packed from the first slot of block b; each row sums to 3584 and holds one sequence of exactly 1024 frames.
All inputs are finite; a program needn't handle non-finite values. No bound on the sum of `frame_mask` on one device may be relied on, other than what follows from the above.
Results may differ from a plain program's by a relative error of at most 0.0065.
Values may be sent and summed in bfloat16 or wider, within the bound.
A program may use at most 256 MiB of HBM per device.

v0:
```python
import jax
import jax.numpy as jnp
from jax import lax
from jax.sharding import PartitionSpec as P

epsilon = 1e-05
block_span = 128


def frame_tables(lengths, frame_mask):
    positions = jnp.arange(frame_mask.shape[0], dtype=jnp.int32)
    offsets = jnp.cumsum(lengths[0]) - lengths[0]
    filled = jnp.sum(lengths[0])
    begins = jnp.any(positions[:, None] == offsets[None, :], axis=1)
    continues = jnp.where(begins, 0.0, 1.0).astype(jnp.float32)
    counted = jnp.where((positions < filled) & (frame_mask > 0), 1.0, 0.0).astype(jnp.float32)
    return (continues, counted)


def linear_scan(coef_rows, driving, backwards):
    row_count, length = driving.shape
    block_count = length // block_span
    factor = coef_rows.reshape(row_count, block_count, block_span)
    running = driving.reshape(row_count, block_count, block_span)
    places = jnp.arange(block_span, dtype=jnp.int32)
    step = 1
    while step < block_span:
        if backwards:
            mover = jnp.where(places[:, None] == places[None, :] + step, 1.0, 0.0).astype(
                jnp.float32
            )
            edge = jnp.where(places >= block_span - step, 1.0, 0.0).astype(jnp.float32)
        else:
            mover = jnp.where(places[:, None] == places[None, :] - step, 1.0, 0.0).astype(
                jnp.float32
            )
            edge = jnp.where(places < step, 1.0, 0.0).astype(jnp.float32)
        moved_factor = (
            jnp.dot(
                factor, mover, precision=lax.Precision.HIGHEST, preferred_element_type=jnp.float32
            )
            + edge
        )
        moved_running = jnp.dot(
            running, mover, precision=lax.Precision.HIGHEST, preferred_element_type=jnp.float32
        )
        running = factor * moved_running + running
        factor = factor * moved_factor
        step = step * 2
    end_place = 0 if backwards else block_span - 1
    total_factor = factor[:, :, end_place].T
    total_running = running[:, :, end_place].T

    def carry_step(carried, block_pair):
        return (block_pair[0] * carried + block_pair[1], carried)

    _, entering = lax.scan(
        carry_step,
        jnp.zeros((row_count,), jnp.float32),
        (total_factor, total_running),
        reverse=backwards,
    )
    result = running + factor * entering.T[:, :, None]
    return result.reshape(row_count, length)


def layer_forward(layer_input, weight, gain_row, bias_row, decay_rate, continues, counted):
    frames_in = lax.all_to_all(layer_input, "neur", split_axis=1, concat_axis=0, tiled=True)
    projected = jnp.dot(
        lax.all_gather(weight, "neur", axis=0, tiled=True),
        frames_in,
        preferred_element_type=jnp.float32,
    )
    neuron_proj = lax.all_to_all(
        projected.astype(jnp.bfloat16), "neur", split_axis=0, concat_axis=1, tiled=True
    ).astype(jnp.float32)
    sum_first = jnp.sum(counted[None, :] * neuron_proj, axis=1)
    sum_second = jnp.sum(counted[None, :] * neuron_proj * neuron_proj, axis=1)
    sum_first, sum_second, frames = lax.psum((sum_first, sum_second, jnp.sum(counted)), "seq")
    average = sum_first / frames
    inv_std = lax.rsqrt(sum_second / frames - average * average + epsilon)
    normed = (neuron_proj - average[:, None]) * inv_std[:, None]
    spread = jnp.sqrt(1.0 - decay_rate * decay_rate)
    states = linear_scan(
        decay_rate[:, None] * continues[None, :], (spread * gain_row)[:, None] * normed, False
    )
    layer_out = counted[None, :] * jax.nn.softplus(states + bias_row[:, None])
    return (layer_out, (frames_in, None, normed, inv_std, frames, states))


def layer_backward(
    upstream, weight, gain_row, bias_row, decay_rate, continues, counted, kept_state
):
    frames_in, full_weight, normed, inv_std, frames, states = kept_state
    local_grad = upstream * counted[None, :] * jax.nn.sigmoid(states + bias_row[:, None])
    following = jnp.concatenate([continues[1:], jnp.zeros((1,), jnp.float32)])
    coef_rows = decay_rate[:, None] * following[None, :]
    state_grad = linear_scan(coef_rows, local_grad, True)
    sum_rec, sum_rec_norm, sum_local = lax.psum(
        (
            jnp.sum(state_grad, axis=1),
            jnp.sum(state_grad * normed, axis=1),
            jnp.sum(local_grad, axis=1),
        ),
        "seq",
    )
    spread = jnp.sqrt(1.0 - decay_rate * decay_rate)
    gain_grad = spread * sum_rec_norm
    proj_grad = (spread * gain_row * inv_std)[:, None] * (
        state_grad - counted[None, :] * (sum_rec[:, None] + sum_rec_norm[:, None] * normed) / frames
    )
    driving = (spread * gain_row)[:, None] * normed
    decay_part = jnp.sum(state_grad * (states - driving), axis=1) / decay_rate
    grad_frames = lax.all_to_all(
        proj_grad.astype(jnp.bfloat16), "neur", split_axis=1, concat_axis=0, tiled=True
    )
    grad_rows = grad_frames
    input_frames = jnp.einsum(
        "ot,oi->it",
        grad_rows,
        lax.all_gather(weight, "neur", axis=0, tiled=True),
        preferred_element_type=jnp.float32,
    )
    input_grad = lax.all_to_all(
        input_frames.astype(jnp.bfloat16), "neur", split_axis=0, concat_axis=1, tiled=True
    ).astype(jnp.float32)
    grad_rows = grad_frames
    weight_rows = lax.psum_scatter(
        jnp.einsum("ot,it->oi", grad_rows, frames_in, preferred_element_type=jnp.float32),
        "neur",
        scatter_dimension=0,
        tiled=True,
    )
    weight_grad, decay_sum = lax.psum((weight_rows, decay_part), "seq")
    decay_grad = decay_sum - decay_rate / spread * gain_row * sum_rec_norm
    return (input_grad, weight_grad, gain_grad, sum_local, decay_grad)


def shards(
    inputs,
    weight_one,
    weight_two,
    gain_one,
    gain_two,
    bias_one,
    bias_two,
    decay_one,
    decay_two,
    lengths,
    frame_mask,
    out_grad,
):
    continues, counted = frame_tables(lengths, frame_mask)
    first_out, first_kept = layer_forward(
        inputs, weight_one, gain_one, bias_one, decay_one, continues, counted
    )
    second_out, second_kept = layer_forward(
        first_out.astype(jnp.bfloat16),
        weight_two,
        gain_two,
        bias_two,
        decay_two,
        continues,
        counted,
    )
    output = inputs.astype(jnp.float32) + second_out
    upstream = out_grad.astype(jnp.float32)
    middle_grad, weight_two_grad, gain_two_grad, bias_two_grad, decay_two_grad = layer_backward(
        upstream, weight_two, gain_two, bias_two, decay_two, continues, counted, second_kept
    )
    lower_grad, weight_one_grad, gain_one_grad, bias_one_grad, decay_one_grad = layer_backward(
        middle_grad, weight_one, gain_one, bias_one, decay_one, continues, counted, first_kept
    )
    return (
        output,
        upstream + lower_grad,
        weight_one_grad,
        gain_one_grad,
        bias_one_grad,
        decay_one_grad,
        weight_two_grad,
        gain_two_grad,
        bias_two_grad,
        decay_two_grad,
    )


def solution(mesh):
    placed = (
        P("neur", "seq"),
        P("neur", None),
        P("neur", None),
        P("neur"),
        P("neur"),
        P("neur"),
        P("neur"),
        P("neur"),
        P("neur"),
        P("seq", None),
        P("seq"),
        P("neur", "seq"),
    )
    return jax.shard_map(
        shards,
        mesh=mesh,
        in_specs=placed,
        out_specs=(
            P("neur", "seq"),
            P("neur", "seq"),
            P("neur", None),
            P("neur"),
            P("neur"),
            P("neur"),
            P("neur", None),
            P("neur"),
            P("neur"),
            P("neur"),
        ),
        check_vma=False,
    )
```

profile of v0, /device:TPU:0, one launch (start us, length us, event | category | flops | bytes accessed | tf_op | source)
XLA Modules:
  0.0 1497.7 jit_solution(10952052994673365580)
XLA Ops:
  12.0 7.3 all-to-all-start
  22.2 79.0 %all-to-all-done = bf16[256,8,512]{0,2,1:T(8,128)(2,1)S(1)} async-done(((bf16[256,8,512]{0,2,1:T(8,128)(2,1)}), bf16[256,8,512]{0,2,1:T(8,128)(2,1)S(1)}, u32[]{:S(2)}, u32[]{:S(2)}) %all-to-all-start) | async-done | bytes 2097184 | tf_op jit(solution)/shard_map/all_to_all | solution.py:68
  103.6 71.9 %all-gather.3.cloned.1.call-done = bf16[2048,2048]{1,0:T(8,128)(2,1)} async-done(((bf16[256,2048]{1,0:T(8,128)(2,1)}), bf16[2048,2048]{1,0:T(8,128)(2,1)}) %all-gather.3.cloned.1.call-update) | async-done | bytes 8388624 | tf_op jit(solution)/shard_map/all_gather | solution.py:70
  175.5 9.8 convolution_convert_fusion.3
  224.4 43.1 %all-to-all-done.1 = bf16[8,256,512]{2,1,0:T(8,128)(2,1)S(1)} async-done(((bf16[8,256,512]{2,1,0:T(8,128)(2,1)}), bf16[8,256,512]{2,1,0:T(8,128)(2,1)S(1)}, u32[]{:S(2)}, u32[]{:S(2)}) %all-to-all-start.1) | async-done | bytes 2097184 | tf_op jit(solution)/shard_map/all_to_all | solution.py:74
  270.1 5.4 copy.304
  276.4 8.0 all-reduce.3
  285.7 8.6 fusion.15
  299.7 9.8 multiply_add_fusion.30
  309.5 5.6 fusion.176
  315.1 9.8 multiply_add_fusion.28
  324.9 5.8 fusion.158
  330.8 9.9 multiply_add_fusion.26
  346.0 6.6 multiply_add_fusion.25
  358.0 6.1 fusion.19
  386.3 5.4 add_multiply_fusion.20
  398.6 5.7 add_multiply_fusion.12
  404.3 10.6 all-to-all-done.2
  414.8 10.0 fusion.24
  452.1 5.4 add_multiply_fusion.3
  468.8 12.1 all-to-all-done.3
  483.4 5.4 copy.315
  489.7 5.8 all-reduce.2
  496.3 8.7 fusion.14
  505.0 5.4 fusion.194
  510.5 9.7 multiply_add_fusion.23
  520.2 5.6 fusion.174
  525.8 9.8 multiply_add_fusion.21
  535.6 5.8 fusion.156
  541.4 9.9 multiply_add_fusion.19
  556.6 6.6 multiply_add_fusion.18
  563.2 5.6 copy.324
  568.8 7.7 fusion.501
  576.5 5.7 copy.337
  582.2 8.5 fusion.17
  596.1 9.4 multiply_add_fusion.16
  605.5 5.6 fusion.112
  611.2 9.8 multiply_add_fusion.14
  621.0 5.8 fusion.94
  626.8 9.9 multiply_add_fusion.12
  642.2 8.8 multiply_reduce_fusion.2
  656.3 6.6 all-reduce.1
  666.8 52.2 %all_to_all.119 = bf16[256,8,512]{2,0,1:T(8,128)(2,1)S(1)} all-to-all(bf16[256,8,512]{2,0,1:T(8,128)(2,1)S(1)} %multiply_convert_fusion.1), channel_id=1, replica_groups=mesh['seq'=4,'neur'=8] {'neur'}, dimensions={1} | all-to-all | bytes 4194304 | tf_op jit(solution)/shard_map/all_to_all | solution.py:114
  719.0 8.1 fusion.509
  727.2 9.1 fusion.25
  762.4 5.4 add_multiply_fusion.8
  779.0 62.9 %all-to-all-done.5 = bf16[8,256,512]{2,1,0:T(8,128)(2,1)S(1)} async-done(((bf16[8,256,512]{2,1,0:T(8,128)(2,1)}), bf16[8,256,512]{2,1,0:T(8,128)(2,1)S(1)}, u32[]{:S(2)}, u32[]{:S(2)}) %all-to-all-start.5) | async-done | bytes 2097184 | tf_op jit(solution)/shard_map/all_to_all | solution.py:124
  844.6 5.5 copy.348
  850.1 11.1 fusion.16
  868.6 12.3 multiply_add_fusion.9
  880.9 5.6 fusion.110
  886.6 9.9 multiply_add_fusion.7
  896.5 5.7 fusion.92
  902.2 10.0 multiply_add_fusion.5
  917.6 8.9 multiply_reduce_fusion.3
  926.5 5.4 copy.357
  936.3 6.4 all-reduce
  946.7 51.3 %all_to_all.120 = bf16[256,8,512]{2,0,1:T(8,128)(2,1)S(1)} all-to-all(bf16[256,8,512]{2,0,1:T(8,128)(2,1)S(1)} %multiply_convert_fusion), channel_id=1, replica_groups=mesh['seq'=4,'neur'=8] {'neur'}, dimensions={1} | all-to-all | bytes 4194304 | tf_op jit(solution)/shard_map/all_to_all | solution.py:114
  998.0 8.2 fusion.508
  1006.2 8.2 convolution_convert_fusion
  1019.7 92.9 %reduce-scatter.5.cloned.1.call-done = f32[256,2048]{1,0:T(8,128)} async-done(((f32[2048,2048]{1,0:T(8,128)}), f32[256,2048]{1,0:T(8,128)}) %reduce-scatter.5.cloned.1.call-update) | async-done | bytes 2097168 | tf_op jit(solution)/shard_map/reduce_scatter | solution.py:128
  1112.6 286.3 %reduce-scatter.3.cloned.1.call-done = f32[256,2048]{1,0:T(8,128)} async-done(((f32[2048,2048]{1,0:T(8,128)}), f32[256,2048]{1,0:T(8,128)}) %reduce-scatter.3.cloned.1.call-update) | async-done | bytes 2097168 | tf_op jit(solution)/shard_map/reduce_scatter | solution.py:128
  1402.6 5.9 copy.359
  1413.4 72.7 %all-reduce.7.cloned.1.call-done = (f32[256,2048]{1,0:T(8,128)}, f32[256,2048]{1,0:T(8,128)}) async-done(((f32[256,2048]{1,0:T(8,128)}, f32[256,2048]{1,0:T(8,128)}), (f32[256,2048]{1,0:T(8,128)}, f32[256,2048]{1,0:T(8,128)})) %all-reduce.7.cloned.1.call-update) | async-done | bytes 4194320 | tf_op jit(solution)/shard_map/psum | solution.py:134
  (679 shorter events, 254.4 us)
Async XLA Ops:
  7.2 168.3 %all-gather.3.cloned.1.call-start = ((), (), s32[]{:S(2)}) async-start(), calls=%async_computation.10 | async-start | bytes 9437184 | tf_op jit(solution)/shard_map/all_gather | solution.py:70
  7.9 12.1 copy-start.82
  7.9 13.0 copy-start.67
  12.0 89.2 %all-to-all-start = ((bf16[256,8,512]{0,2,1:T(8,128)(2,1)}), bf16[256,8,512]{0,2,1:T(8,128)(2,1)S(1)}, u32[]{:S(2)}, u32[]{:S(2)}) async-start(bf16[256,8,512]{0,2,1:T(8,128)(2,1)} %bitcast.326), calls=%async_computation | async-start | bytes 4194304 | tf_op jit(solution)/shard_map/all_to_all | solution.py:68
  19.3 385.0 %all-gather.5.cloned.1.call-start = ((), (), s32[]{:S(2)}) async-start(), calls=%async_computation.11 | async-start | bytes 9437184 | tf_op jit(solution)/shard_map/all_gather | solution.py:70
  185.3 82.1 %all-to-all-start.1 = ((bf16[8,256,512]{2,1,0:T(8,128)(2,1)}), bf16[8,256,512]{2,1,0:T(8,128)(2,1)S(1)}, u32[]{:S(2)}, u32[]{:S(2)}) async-start(bf16[8,256,512]{2,1,0:T(8,128)(2,1)} %bitcast.333), calls=%async_computation.1 | async-start | bytes 4194304 | tf_op jit(solution)/shard_map/all_to_all | solution.py:74
  208.0 5.4 copy-start.24
  267.4 8.1 copy-start.32
  270.1 14.3 copy-start.77
  285.7 8.6 copy-start.68
  285.7 8.6 copy-start.70
  285.7 8.6 copy-start.73
  294.3 5.4 copy-start.51
  294.3 5.4 copy-start.53
  309.5 5.6 copy-start.5
  309.5 5.6 copy-start.25
  324.9 5.8 copy-start.21
  324.9 5.8 copy-start.23
  352.6 5.4 copy-start.79
  358.0 10.0 copy-start.64
  364.1 50.7 %all-to-all-start.2 = ((bf16[256,8,512]{2,0,1:T(8,128)(2,1)}), bf16[256,8,512]{2,0,1:T(8,128)(2,1)S(1)}, u32[]{:S(2)}, u32[]{:S(2)}) async-start(bf16[256,8,512]{2,0,1:T(8,128)(2,1)} %fusion.19), calls=%async_computation.2 | async-start | bytes 4194304 | tf_op jit(solution)/shard_map/all_to_all | solution.py:68
  386.3 5.4 copy-start.18
  414.8 10.0 copy-start.61
  428.8 52.0 %all-to-all-start.3 = ((bf16[8,256,512]{2,1,0:T(8,128)(2,1)}), bf16[8,256,512]{2,1,0:T(8,128)(2,1)S(1)}, u32[]{:S(2)}, u32[]{:S(2)}) async-start(bf16[8,256,512]{2,1,0:T(8,128)(2,1)} %bitcast.323), calls=%async_computation.3 | async-start | bytes 4194304 | tf_op jit(solution)/shard_map/all_to_all | solution.py:74
  432.4 680.2 %reduce-scatter.5.cloned.1.call-start = ((), (), s32[]{:S(2)}) async-start(), calls=%async_computation.13 | async-start | bytes 18874368 | tf_op jit(solution)/shard_map/reduce_scatter | solution.py:128
  452.1 5.5 copy-start.12
  483.4 12.1 copy-start.75
  505.0 5.5 copy-start.47
  505.0 5.4 copy-start.49
  520.2 5.6 copy-start.3
  520.2 5.6 copy-start.19
  535.6 5.8 copy-start.15
  535.6 5.8 copy-start.17
  563.2 5.6 copy-start.81
  590.7 5.4 copy-start.43
  590.7 5.4 copy-start.45
  605.5 5.6 copy-start.1
  605.5 5.6 copy-start.13
  621.0 5.8 copy-start.9
  621.0 5.8 copy-start.11
  666.8 52.2 %copy-start.62 = (bf16[256,8,512]{2,0,1:T(8,128)(2,1)S(1)}, bf16[256,8,512]{2,0,1:T(8,128)(2,1)}, u32[]{:S(2)}) copy-start(bf16[256,8,512]{2,0,1:T(8,128)(2,1)} %copy-done.61) | copy-start | bytes 6291460
  736.3 7.8 copy-start.66
  740.2 101.7 %all-to-all-start.5 = ((bf16[8,256,512]{2,1,0:T(8,128)(2,1)}), bf16[8,256,512]{2,1,0:T(8,128)(2,1)S(1)}, u32[]{:S(2)}, u32[]{:S(2)}) async-start(bf16[8,256,512]{2,1,0:T(8,128)(2,1)} %bitcast.327), calls=%async_computation.5 | async-start | bytes 4194304 | tf_op jit(solution)/shard_map/all_to_all | solution.py:124
  743.8 655.2 %reduce-scatter.3.cloned.1.call-start = ((), (), s32[]{:S(2)}) async-start(), calls=%async_computation.12 | async-start | bytes 18874368 | tf_op jit(solution)/shard_map/reduce_scatter | solution.py:128
  762.4 5.4 copy-start.30
  841.9 19.3 %copy-start.34 = (bf16[8,256,512]{2,1,0:T(8,128)(2,1)}, bf16[8,256,512]{2,1,0:T(8,128)(2,1)S(1)}, u32[]{:S(2)}) copy-start(bf16[8,256,512]{2,1,0:T(8,128)(2,1)S(1)} %all-to-all-done.5) | copy-start | bytes 6291460
  844.6 5.5 copy-start.80
  863.2 5.4 copy-start.55
  863.2 5.4 copy-start.57
  880.9 5.6 copy-start.7
  880.9 5.6 copy-start.31
  896.5 5.7 copy-start.27
  896.5 5.7 copy-start.29
  902.2 15.4 %copy-start.69 = (f32[256]{0:T(256)S(1)}, f32[256]{0:T(256)}, u32[]{:S(2)}) copy-start(f32[256]{0:T(256)} %copy-done.68) | copy-start | bytes 3076
  902.2 15.4 %copy-start.71 = (f32[256]{0:T(256)S(1)}, f32[256]{0:T(256)}, u32[]{:S(2)}) copy-start(f32[256]{0:T(256)} %copy-done.70) | copy-start | bytes 3076
  902.2 15.4 %copy-start.74 = (f32[256]{0:T(256)S(1)}, f32[256]{0:T(256)}, u32[]{:S(2)}) copy-start(f32[256]{0:T(256)} %copy-done.73) | copy-start | bytes 3076
  931.9 10.8 copy-start.33
  931.9 10.8 copy-start.72
  946.7 51.3 %copy-start.60 = (bf16[8,256,512]{2,1,0:T(8,128)(2,1)S(1)}, bf16[8,256,512]{2,1,0:T(8,128)(2,1)}, u32[]{:S(2)}) copy-start(bf16[8,256,512]{2,1,0:T(8,128)(2,1)} %copy.303) | copy-start | bytes 6291460
  1015.9 383.1 %copy-start.76 = (f32[256]{0:T(256)S(1)}, f32[256]{0:T(256)}, u32[]{:S(2)}) copy-start(f32[256]{0:T(256)} %param.24) | copy-start | bytes 3076
  1015.9 383.7 %copy-start.78 = (f32[256]{0:T(256)S(1)}, f32[256]{0:T(256)}, u32[]{:S(2)}) copy-start(f32[256]{0:T(256)} %param.23) | copy-start | bytes 3076
  1015.9 384.3 %all-to-all-start.7 = ((bf16[8,256,512]{1,2,0:T(8,128)(2,1)}), bf16[8,256,512]{1,2,0:T(8,128)(2,1)S(1)}, u32[]{:S(2)}, u32[]{:S(2)}) async-start(bf16[8,256,512]{1,2,0:T(8,128)(2,1)} %bitcast.325), calls=%async_computation.7 | async-start | bytes 4194304 | tf_op jit(solution)/shard_map/all_to_all | solution.py:124
  1019.7 466.4 %all-reduce.7.cloned.1.call-start = ((), (), s32[]{:S(2)}) async-start(), calls=%async_computation.14 | async-start | bytes 8388608 | tf_op jit(solution)/shard_map/psum | solution.py:134
  1402.6 5.9 copy-start.59
  (30 other events, 114.0 us)
Sparse Core Ops, SparseCore 0:
  10.1 165.3 all-gather.2
  177.6 160.6 all-gather.4
  727.3 385.3 reduce-scatter.4
  1116.7 282.1 reduce-scatter.2
  1401.3 84.7 all-reduce.6
where the time goes:
time: 1500 us
  waiting for transfers between devices  733 us (49%)
  matrix products  410 us (27%)
  blocking collectives  130 us (9%)
  local copies, waits for them, and re-layouts  96.5 us (6%)
  other arithmetic  81.3 us (5%)
  starting transfers between devices  26.5 us (2%)
  between operations  16 us (1%)
    reduce_scatter x2, waiting for transfers between devices, layer_backward(): lax.psum_scatter(jnp.einsum('ot,it->oi', grad_rows, frames_in, preferred_...  379 us
    dot_general x28, matrix products, linear_scan(): jnp.dot(running, mover, precision=lax.Precision.HIGHEST, preferred_elemen...  224 us
    dot_general x28, matrix products, linear_scan(): jnp.dot(factor, mover, precision=lax.Precision.HIGHEST, preferred_element...  132 us
    all_to_all x2, blocking collectives, layer_backward(): lax.all_to_all(proj_grad.astype(jnp.bfloat16), 'neur', split_axis=1, conc...  103 us
    all_to_all x2, waiting for transfers between devices, layer_forward(): lax.all_to_all(layer_input, 'neur', split_axis=1, concat_axis=0, tiled=True)  89.6 us
    psum x1, waiting for transfers between devices, layer_backward(): weight_grad, decay_sum = lax.psum((weight_rows, decay_part), 'seq')  72.7 us
    all_gather x2, waiting for transfers between devices, layer_forward(): lax.all_gather(weight, 'neur', axis=0, tiled=True)  71.9 us
    all_to_all x2, waiting for transfers between devices, layer_backward(): lax.all_to_all(input_frames.astype(jnp.bfloat16), 'neur', split_axis=0, c...  62.9 us
  transfers between devices with their start and end apart: 11, of which 9 were waited for; matrix products, arithmetic and copies ran while one was open for 25% of the time, Pallas kernels for 0%

commit v1 on v0

--- a/solution.py
+++ b/solution.py
@@ -1,10 +1,1077 @@
+import functools
+
 import jax
 import jax.numpy as jnp
 from jax import lax
+from jax.experimental import pallas as pl
+from jax.experimental.pallas import tpu as pltpu
 from jax.sharding import PartitionSpec as P
 
 epsilon = 1e-05
 block_span = 128
+valid_frames = 3584
+f32 = jnp.float32
+bf16 = jnp.bfloat16
+MESH = pl.DeviceIdType.MESH
+
+
+def wide(tile, width):
+    return jnp.concatenate([tile] * (width // 128), axis=1)
+
+
+def at(index, size):
+    if isinstance(index, int):
+        return pl.ds(index * size, size)
+    return pl.ds(pl.multiple_of(index * size, size), size)
+
+
+def power(base, exponent):
+    result = None
+    while exponent:
+        if exponent % 2:
+            result = base if result is None else result * base
+        exponent //= 2
+        base = base * base
+    return result
+
+
+def log_of(rate):
+    u = 1.0 - rate
+    series = jnp.full_like(u, 1.0 / 8)
+    for order in range(7, 0, -1):
+        series = series * u + 1.0 / order
+    return -u * series
+
+
+GAIN, BIAS, DECAY = 0, 2, 4
+
+
+class Sizes:
+    def __init__(self, n, seqs, H, fb, tok_dev):
+        self.n, self.seqs, self.H, self.fb, self.tok_dev = n, seqs, H, fb, tok_dev
+        self.T = valid_frames // n
+        self.steps = self.T // 8
+        self.valid = valid_frames
+        self.qc = H // seqs
+        self.Z = n // 2
+        self.odd = self.T % 128
+        self.win = self.T + self.odd
+        self.L = min(512, H)
+
+
+def fits(n, seqs, H, fb, tok_dev):
+    if valid_frames % n or n % 2 or n > 8 or seqs != 4 or fb * n != H or fb % 128 or H % 512:
+        return False
+    T = valid_frames // n
+    return T % 64 == 0 and valid_frames % 128 == 0 and tok_dev >= valid_frames
+
+
+class Gather:
+    def __init__(self, env, source, full, sends, recvs, first, second):
+        self.env, self.full, self.sends, self.recvs = env, full, sends, recvs
+        self.first, self.second = first, second
+        z = env.z
+        Z = env.sz.Z
+        self.source = source.at[:, at(env.s, env.sz.qc)]
+        self.events = [(0, 0, 0)]
+        for dz in range(1, Z):
+            self.events += [(dz, 0, 0), (dz - 1, 1, 0)]
+        self.events.append((Z - 1, 1, 0))
+        self.events += [(dz, a, 1) for dz, a, _ in self.events]
+        self.done = 0
+
+    def block(self, dz, a, b, flip=0):
+        env = self.env
+        coords = {"x": env.x, "y": env.y}
+        coords[self.first] = (coords[self.first] + a) % 2
+        coords[self.second] = (coords[self.second] + b) % 2
+        zz = (env.z + env.sz.Z - dz) % env.sz.Z
+        cc = (env.c + flip) % 2
+        return self.full.at[
+            at(2 * zz + coords["x"], env.sz.fb), at(2 * coords["y"] + cc, env.sz.qc)
+        ]
+
+    def index(self, stage, dz, a, b):
+        Z = self.env.sz.Z
+        if stage == "z":
+            return dz - 1
+        if stage == "first":
+            return Z - 1 + dz
+        if stage == "second":
+            return 2 * Z - 1 + 2 * dz + a
+        return 4 * Z - 1 + 4 * dz + 2 * a + b
+
+    def copy(self, stage, source, dest, dz, a, b, target):
+        k = self.index(stage, dz, a, b)
+        return pltpu.make_async_remote_copy(
+            src_ref=source,
+            dst_ref=dest,
+            send_sem=self.sends.at[k],
+            recv_sem=self.recvs.at[k],
+            device_id=target,
+            device_id_type=MESH,
+        )
+
+    def arrival(self, dz, a, b):
+        stage = "second" if b else "first" if a else "z"
+        block = self.block(dz, a, b)
+        self.copy(stage, block, block, dz, a, b, self.env.across("x")).wait_recv()
+
+    def start(self):
+        env = self.env
+        own = self.block(0, 0, 0)
+        for dz in range(1, env.sz.Z):
+            target = {"neur": 2 * ((env.z + dz) % env.sz.Z) + env.x}
+            self.copy("z", self.source, own, dz, 0, 0, target).start()
+        self.relay(self.source, 0, 0, 0)
+        self.done = 1
+
+    def relay(self, source, dz, a, b):
+        env = self.env
+        dest = self.block(dz, a, b)
+        if not a and not b:
+            self.copy("first", source, dest, dz, a, b, env.across(self.first)).start()
+        if not b:
+            self.copy("second", source, dest, dz, a, b, env.across(self.second)).start()
+        self.copy("core", source, dest, dz, a, b, env.across("core")).start()
+
+    def advance(self, count=None):
+        last = len(self.events) if count is None else min(len(self.events), self.done + count)
+        for dz, a, b in self.events[self.done : last]:
+            self.arrival(dz, a, b)
+            self.relay(self.block(dz, a, b), dz, a, b)
+        self.done = last
+
+    def finish(self):
+        self.advance()
+        for dz, a, b in self.events:
+            block = self.block(dz, a, b, 1)
+            self.copy("core", block, block, dz, a, b, self.env.across("core")).wait_recv()
+
+    def drain(self):
+        block = self.block(0, 0, 0)
+        for k in range(8 * self.env.sz.Z - 1):
+            pltpu.make_async_remote_copy(
+                src_ref=block,
+                dst_ref=block,
+                send_sem=self.sends.at[k],
+                recv_sem=self.recvs.at[k],
+                device_id=self.env.across("x"),
+                device_id_type=MESH,
+            ).wait_send()
+
+
+class Reduce:
+    def __init__(self, env, grads, frames, land, stage, sends, recvs, first, second):
+        self.env, self.grads, self.frames, self.land, self.stage = env, grads, frames, land, stage
+        self.sends, self.recvs, self.first, self.second = sends, recvs, first, second
+
+    def place(self, p):
+        env, Z = self.env, self.env.sz.Z
+        coords = {"x": env.x, "y": env.y}
+        coords[self.first] = (coords[self.first] + 1 - p // (2 * Z)) % 2
+        coords[self.second] = (coords[self.second] + 1 - (p // Z) % 2) % 2
+        zz = (env.z + p % Z + 1) % Z
+        return zz, coords["x"], coords["y"]
+
+    def tile(self, p, cc):
+        sz = self.env.sz
+        zz, xx, yy = self.place(p)
+        return jnp.dot(
+            self.grads[at(2 * zz + xx, sz.fb), :],
+            self.frames[:, at(2 * yy + cc, sz.qc)],
+            preferred_element_type=f32,
+        )
+
+    def copy(self, k, target):
+        return pltpu.make_async_remote_copy(
+            src_ref=self.stage.at[k],
+            dst_ref=self.land(k),
+            send_sem=self.sends.at[k],
+            recv_sem=self.recvs.at[k],
+            device_id=target,
+            device_id_type=MESH,
+        )
+
+    def landed(self, k):
+        self.copy(k, self.env.across("x")).wait_recv()
+        return self.land(k)[...].astype(f32)
+
+    def send(self, k, tile, target):
+        self.stage[k] = tile.astype(bf16)
+        self.copy(k, target).start()
+
+    def cores(self):
+        env, Z = self.env, self.env.sz.Z
+
+        def one(p, _):
+            self.send(p, self.tile(p, (env.c + 1) % 2), env.across("core"))
+            return 0
+
+        lax.fori_loop(0, 4 * Z, one, 0)
+
+    def firsts(self, low=0, high=None):
+        env, Z = self.env, self.env.sz.Z
+
+        def one(p, _):
+            tile = self.tile(p, env.c) + self.landed(p)
+            self.send(4 * Z + p, tile, env.across(self.first))
+            return 0
+
+        lax.fori_loop(low, 2 * Z if high is None else high, one, 0)
+
+    def seconds(self):
+        env, Z = self.env, self.env.sz.Z
+
+        def one(p, _):
+            tile = self.tile(p, env.c) + self.landed(p) + self.landed(p + 2 * Z)
+            self.send(4 * Z + p, tile, env.across(self.second))
+            return 0
+
+        lax.fori_loop(2 * Z, 3 * Z, one, 0)
+
+    def lines(self):
+        env, Z = self.env, self.env.sz.Z
+
+        def one(p, _):
+            tile = self.tile(p, env.c) + self.landed(p) + self.landed(p + 2 * Z)
+            tile = tile + self.landed(p + 3 * Z)
+            target = {"neur": 2 * ((env.z + p % Z + 1) % Z) + env.x}
+            self.send(4 * Z + p, tile, target)
+            return 0
+
+        lax.fori_loop(3 * Z, 4 * Z - 1, one, 0)
+
+    def total(self):
+        env, Z = self.env, self.env.sz.Z
+        p = 4 * Z - 1
+        tile = self.tile(p, env.c) + self.landed(p) + self.landed(p + 2 * Z)
+        tile = tile + self.landed(p + 3 * Z)
+        for k in range(7 * Z, 8 * Z - 1):
+            tile = tile + self.landed(k)
+        return tile
+
+    def drain(self):
+        for k in range(8 * self.env.sz.Z - 1):
+            self.copy(k, self.env.across("x")).wait_send()
+
+
+class Result:
+    def __init__(self, env, whole, block, sends, recvs, local):
+        self.env, self.whole, self.block = env, whole, block
+        self.sends, self.recvs, self.local = sends, recvs, local
+
+    def part(self, flip_y, flip_c):
+        env = self.env
+        s = 2 * ((env.y + flip_y) % 2) + (env.c + flip_c) % 2
+        return self.whole.at[:, at(s, env.sz.qc)]
+
+    def copy(self, k, source, dest, target):
+        return pltpu.make_async_remote_copy(
+            src_ref=source,
+            dst_ref=dest,
+            send_sem=self.sends.at[k],
+            recv_sem=self.recvs.at[k],
+            device_id=target,
+            device_id_type=MESH,
+        )
+
+    def start(self):
+        env, own = self.env, self.part(0, 0)
+        self.copy(0, self.block, own, env.across("y")).start()
+        self.copy(1, self.block, own, env.across("core")).start()
+        pltpu.make_async_copy(self.block, own, self.local).start()
+
+    def finish(self):
+        env = self.env
+        other = self.part(1, 0)
+        self.copy(0, self.block, other, env.across("y")).wait_recv()
+        forward = self.copy(2, other, other, env.across("core"))
+        forward.start()
+        own = self.part(0, 0)
+        pltpu.make_async_copy(self.block, own, self.local).wait()
+        self.copy(0, self.block, own, env.across("y")).wait_send()
+        self.copy(1, self.block, self.part(0, 1), env.across("core")).wait()
+        forward.wait_send()
+        self.copy(2, other, self.part(1, 1), env.across("core")).wait_recv()
+
+
+class Env:
+    def across(self, axis):
+        if axis == "x":
+            return {"neur": 2 * self.z + 1 - self.x}
+        if axis == "y":
+            return {"seq": 2 * (1 - self.y) + self.c}
+        return {"seq": 2 * self.y + 1 - self.c}
+
+
+def network(
+    sz,
+    x_hbm,
+    g_hbm,
+    w_one,
+    w_two,
+    own_par,
+    cont,
+    counted,
+    aux,
+    out_land,
+    dx_land,
+    dw_one,
+    dw_two,
+    small,
+    raw,
+    perm,
+    eye,
+    xs,
+    gs,
+    xr,
+    gr,
+    p_one,
+    p_two,
+    x_two,
+    dp,
+    dpt,
+    s_one,
+    s_two,
+    wf_one,
+    wf_two,
+    land,
+    stage,
+    fin,
+    par,
+    ends,
+    work,
+    pay,
+    arrive,
+    seqpay,
+    seqland,
+    back,
+    backland,
+    local_sems,
+    par_sends,
+    par_recvs,
+    frame_sends,
+    frame_recvs,
+    gather_sends,
+    gather_recvs,
+    hop_sends,
+    hop_recvs,
+    seq_sends,
+    seq_recvs,
+    reduce_sends,
+    reduce_recvs,
+    final_sends,
+    final_recvs,
+):
+    n, seqs, H, fb, T, steps, L = sz.n, sz.seqs, sz.H, sz.fb, sz.T, sz.steps, sz.L
+    env = Env()
+    env.sz = sz
+    me = lax.axis_index("neur")
+    mine = lax.axis_index("seq")
+    env.j, env.s = me, mine
+    env.z, env.x, env.y, env.c = me // 2, me % 2, mine // 2, mine % 2
+
+    barrier = pltpu.get_barrier_semaphore()
+    for o in range(1, n):
+        pl.semaphore_signal(
+            barrier, inc=1, device_id={"neur": (me + o) % n}, device_id_type=MESH
+        )
+    for o in range(1, seqs):
+        pl.semaphore_signal(
+            barrier, inc=1, device_id={"seq": (mine + o) % seqs}, device_id_type=MESH
+        )
+    load_x = pltpu.make_async_copy(x_hbm.at[:, pl.ds(0, sz.valid)], raw, local_sems.at[0])
+    load_x.start()
+    pl.semaphore_wait(barrier, n - 1 + seqs - 1)
+
+    def neur_copy(source, dest, send, recv, i):
+        return pltpu.make_async_remote_copy(
+            src_ref=source,
+            dst_ref=dest,
+            send_sem=send,
+            recv_sem=recv,
+            device_id={"neur": i},
+            device_id_type=MESH,
+        )
+
+    def seq_copy(source, dest, send, recv, i):
+        return pltpu.make_async_remote_copy(
+            src_ref=source,
+            dst_ref=dest,
+            send_sem=send,
+            recv_sem=recv,
+            device_id={"seq": i},
+            device_id_type=MESH,
+        )
+
+    def others(body, count=n, own=me):
+        def one(o, _):
+            body((own + o) % count)
+            return 0
+
+        lax.fori_loop(1, count, one, 0)
+
+    own_lanes = at(me, fb)
+
+    def par_copy(i):
+        return neur_copy(own_par, par.at[:, own_lanes], par_sends.at[i], par_recvs.at[me], i)
+
+    def par_wait(i):
+        neur_copy(own_par, par.at[:, at(i, fb)], par_sends.at[i], par_recvs.at[i], i).wait()
+
+    others(lambda i: par_copy(i).start())
+    par[:, own_lanes] = own_par[...]
+
+    gather_one = Gather(env, w_one, wf_one, gather_sends.at[0], gather_recvs.at[0], "x", "y")
+    gather_two = Gather(env, w_two, wf_two, gather_sends.at[1], gather_recvs.at[1], "y", "x")
+    own_one = pltpu.make_async_copy(gather_one.source, gather_one.block(0, 0, 0), local_sems.at[2])
+    own_two = pltpu.make_async_copy(gather_two.source, gather_two.block(0, 0, 0), local_sems.at[3])
+    own_one.start()
+    own_two.start()
+    gather_one.start()
+
+    row = lax.broadcasted_iota(jnp.int32, (T, sz.win), 0)
+    column = lax.broadcasted_iota(jnp.int32, (T, sz.win), 1)
+    frame = (row % 8) * steps + row // 8
+    perm[0] = jnp.where(column == frame, 1.0, 0.0).astype(bf16)
+    perm[1] = jnp.where(column == frame + sz.odd, 1.0, 0.0).astype(bf16)
+    row = lax.broadcasted_iota(jnp.int32, (fb, fb), 0)
+    column = lax.broadcasted_iota(jnp.int32, (fb, fb), 1)
+    eye[...] = jnp.where(row == column, 1.0, 0.0).astype(bf16)
+
+    def window(i):
+        start = (i // 2) * (2 * T) + (i % 2) * (T - sz.odd)
+        return pl.ds(pl.multiple_of(start, 128), sz.win)
+
+    def turned(i):
+        return lax.dot_general(
+            perm[i % 2], raw[:, window(i)], (((1,), (1,)), ((), ())), preferred_element_type=f32
+        ).astype(bf16)
+
+    def frames_copy(a, source, dest, i):
+        return neur_copy(source, dest, frame_sends.at[a, i], frame_recvs.at[a, me], i)
+
+    def frames_wait(a, ref, i):
+        part = ref.at[:, at(i, fb)]
+        neur_copy(part, part, frame_sends.at[a, i], frame_recvs.at[a, i], i).wait_recv()
+
+    def frames_sent(a, ref, i):
+        part = ref.at[:, at(i, fb)]
+        neur_copy(part, part, frame_sends.at[a, i], frame_recvs.at[a, i], i).wait_send()
+
+    load_x.wait()
+
+    def send_x(i):
+        xs[:, at(i, fb)] = turned(i)
+        frames_copy(0, xs.at[:, at(i, fb)], xr.at[:, own_lanes], i).start()
+
+    others(send_x)
+    xr[:, own_lanes] = turned(me)
+    load_g = pltpu.make_async_copy(g_hbm.at[:, pl.ds(0, sz.valid)], raw, local_sems.at[1])
+    load_g.start()
+    gather_one.advance(2)
+    load_g.wait()
+
+    def turn_g(i):
+        gs[:, at(i, fb)] = turned(i)
+
+    others(turn_g)
+    gr[:, own_lanes] = turned(me)
+    gather_one.finish()
+    gather_two.start()
+    others(lambda i: frames_copy(1, gs.at[:, at(i, fb)], gr.at[:, own_lanes], i).start())
+    own_one.wait()
+    own_two.wait()
+    others(lambda i: frames_wait(0, xr, i))
+    others(par_wait)
+
+    def blocks(body):
+        def one(b, _):
+            body(at(b, L))
+            return 0
+
+        lax.fori_loop(0, H // L, one, 0)
+
+    def project(frames, weight, result):
+        def one(b, _):
+            result[:, at(b, fb)] = lax.dot_general(
+                frames[...],
+                weight[at(b, fb), :],
+                (((1,), (1,)), ((), ())),
+                preferred_element_type=f32,
+            ).astype(bf16)
+            return 0
+
+        lax.fori_loop(0, n, one, 0)
+
+    def flags(t):
+        tile = pl.ds(pl.multiple_of(8 * t, 8), 8)
+        return wide(cont[tile, :], L), wide(counted[tile, :], L)
+
+    def spread8(ref, r, cols, width=L):
+        return jnp.broadcast_to(ref[r : r + 1, cols], (8, width))
+
+    zero = jnp.zeros((8, L), f32)
+
+    def down(value):
+        return jnp.sum(value, axis=0, keepdims=True)
+
+    def exchange(e, gathered, totalled):
+        def out_copy(i):
+            return neur_copy(
+                pay.at[e, :, at(i, fb)],
+                arrive.at[e, me],
+                hop_sends.at[2 * e, i],
+                hop_recvs.at[2 * e, me],
+                i,
+            )
+
+        others(lambda i: out_copy(i).start())
+        arrive[e, me] = pay[e, :, own_lanes]
+
+        def out_wait(i):
+            neur_copy(
+                pay.at[e, :, at(i, fb)],
+                arrive.at[e, i],
+                hop_sends.at[2 * e, i],
+                hop_recvs.at[2 * e, i],
+                i,
+            ).wait()
+
+        others(out_wait)
+        gathered()
+
+        def along_copy(i):
+            return seq_copy(
+                seqpay.at[e],
+                seqland.at[e, mine],
+                seq_sends.at[e, i],
+                seq_recvs.at[e, mine],
+                i,
+            )
+
+        def along_wait(i):
+            seq_copy(
+                seqpay.at[e], seqland.at[e, i], seq_sends.at[e, i], seq_recvs.at[e, i], i
+            ).wait()
+
+        others(lambda i: along_copy(i).start(), seqs, mine)
+        seqland[e, mine] = seqpay[e]
+        others(along_wait, seqs, mine)
+        sums = seqland[e, 0]
+        for i in range(1, seqs):
+            sums = sums + seqland[e, i]
+        totalled(sums)
+
+        def back_copy(i):
+            return neur_copy(
+                back.at[e, i],
+                backland.at[e, :, own_lanes],
+                hop_sends.at[2 * e + 1, i],
+                hop_recvs.at[2 * e + 1, me],
+                i,
+            )
+
+        def back_wait(i):
+            neur_copy(
+                back.at[e, i],
+                backland.at[e, :, at(i, fb)],
+                hop_sends.at[2 * e + 1, i],
+                hop_recvs.at[2 * e + 1, i],
+                i,
+            ).wait()
+
+        others(lambda i: back_copy(i).start())
+        backland[e, :, own_lanes] = back[e, me]
+        others(back_wait)
+
+    def layer_forward(layer, frames, weight, projected, states, store, meanwhile):
+        e = layer
+        decay_row, gain_row, bias_row = DECAY + layer, GAIN + layer, BIAS + layer
+        project(frames, weight, projected)
+        meanwhile(0)
+
+        def local_ends(cols):
+            decay = spread8(par, decay_row, cols)
+
+            def step(i, carry):
+                state, first, second = carry
+                pair = projected[pl.ds(pl.multiple_of(16 * i, 16), 16), cols].astype(f32)
+                for h in range(2):
+                    value = pair[8 * h : 8 * h + 8, :]
+                    goes, count = flags(2 * i + h)
+                    state = (decay * goes) * state + value
+                    held = count * value
+                    first = first + held
+                    second = second + held * value
+                return state, first, second
+
+            state, first, second = lax.fori_loop(0, T // 16, step, (zero, zero, zero))
+            ends[:, cols] = state
+            pay[e, 1:2, cols] = down(first)
+            pay[e, 2:3, cols] = down(second)
+
+        blocks(local_ends)
+        run_power = power(par[decay_row : decay_row + 1, :], steps)
+        total = jnp.zeros((1, H), f32)
+        for k in range(8):
+            total = run_power * wide(aux[16 + k : 17 + k, :], H) * total + ends[k : k + 1, :]
+        pay[e, 0:1, :] = total
+        pay[e, 3:8, :] = jnp.zeros((5, H), f32)
+        meanwhile(1)
+
+        own_decay = own_par[decay_row : decay_row + 1, :]
+
+        def gathered():
+            whole_power = power(own_decay, T)
+            carried = jnp.zeros((1, fb), f32)
+            sums = jnp.zeros((8, fb), f32)
+            for i in range(n):
+                rows = arrive[e, i]
+                back[e, i, 0:1, :] = carried
+                carried = whole_power * wide(aux[8 + i : 9 + i, :], fb) * carried + rows[0:1, :]
+                sums = sums + rows
+            seqpay[e] = sums
+            seqpay[e, 0:1, :] = wide(aux[24:25, :], fb)
+
+        def totalled(sums):
+            frames_all = sums[0:1, :]
+            average = sums[1:2, :] / frames_all
+            inv_std = lax.rsqrt(sums[2:3, :] / frames_all - average * average + epsilon)
+            for i in range(n):
+                back[e, i, 1:2, :] = average
+                back[e, i, 2:3, :] = inv_std
+                back[e, i, 3:4, :] = frames_all
+                back[e, i, 4:8, :] = jnp.zeros((4, fb), f32)
+
+        exchange(e, gathered, totalled)
+        meanwhile(2)
+
+        total = backland[e, 0:1, :]
+        for k in range(8):
+            work[k : k + 1, :] = total
+            total = run_power * wide(aux[16 + k : 17 + k, :], H) * total + ends[k : k + 1, :]
+
+        def full_scan(cols):
+            decay = spread8(par, decay_row, cols)
+            average = spread8(backland.at[e], 1, cols)
+            inv_std = spread8(backland.at[e], 2, cols)
+            bias = spread8(par, bias_row, cols)
+            scale = jnp.sqrt(1.0 - decay * decay) * spread8(par, gain_row, cols) * inv_std
+            ones = (1.0 - jnp.exp(wide(aux[0:8, :], L) * log_of(decay))) / (1.0 - decay)
+            state = scale * (work[0:8, cols] - average * ones)
+            states[0:8, cols] = state
+
+            def step(i, state):
+                pair = projected[pl.ds(pl.multiple_of(16 * i, 16), 16), cols].astype(f32)
+                outs = []
+                for h in range(2):
+                    goes, count = flags(2 * i + h)
+                    state = (decay * goes) * state + scale * (pair[8 * h : 8 * h + 8, :] - average)
+                    states[pl.ds(pl.multiple_of(16 * i + 8 * h + 8, 8), 8), cols] = state
+                    v = state + bias
+                    soft = jnp.maximum(v, 0.0) + jnp.log(1.0 + jnp.exp(-jnp.abs(v)))
+                    outs.append(count * soft)
+                store[pl.ds(pl.multiple_of(16 * i, 16), 16), cols] = jnp.concatenate(
+                    outs, axis=0
+                ).astype(bf16)
+                return state
+
+            lax.fori_loop(0, T // 16, step, state)
+
+        blocks(full_scan)
+        meanwhile(3)
+
+    def layer_backward(layer, upstream, projected, states, meanwhile):
+        e = 2 + (1 - layer)
+        decay_row, gain_row, bias_row = DECAY + layer, GAIN + layer, BIAS + layer
+        run_power = power(par[decay_row : decay_row + 1, :], steps)
+
+        def local_ends(cols):
+            decay = spread8(par, decay_row, cols)
+            average = spread8(backland.at[layer], 1, cols)
+            inv_std = spread8(backland.at[layer], 2, cols)
+            bias = spread8(par, bias_row, cols)
+
+            def step(o, carry):
+                i = T // 16 - 1 - o
+                rows = pl.ds(pl.multiple_of(16 * i, 16), 16)
+                pair = projected[rows, cols].astype(f32)
+                ups = upstream[rows, cols].astype(f32)
+                for h in (1, 0):
+                    run, reach, U, V, UN, VN, B, D, DA = carry
+                    goes, count = flags(2 * i + h)
+                    here = pl.ds(pl.multiple_of(16 * i + 8 * h + 8, 8), 8)
+                    state = states[here, cols]
+                    before = states[pl.ds(pl.multiple_of(16 * i + 8 * h, 8), 8), cols]
+                    local = ups[8 * h : 8 * h + 8, :] * count / (1.0 + jnp.exp(-(state + bias)))
+                    states[here, cols] = local
+                    normed = (pair[8 * h : 8 * h + 8, :] - average) * inv_std
+                    run = local + run
+                    kept = goes * before
+                    link = decay * goes
+                    carry = (
+                        link * run,
+                        link * reach,
+                        U + run,
+                        V + reach,
+                        UN + run * normed,
+                        VN + reach * normed,
+                        B + local,
+                        D + run * kept,
+                        DA + reach * kept,
+                    )
+                return carry
+
+            one = jnp.ones((8, L), f32)
+            run, _, U, V, UN, VN, B, D, DA = lax.fori_loop(
+                0, T // 16, step, (zero, one, zero, zero, zero, zero, zero, zero, zero)
+            )
+            ends[:, cols] = run
+            decay_run = power(par[decay_row : decay_row + 1, cols], steps)
+            part, factor = jnp.zeros((1, L), f32), jnp.ones((1, L), f32)
+            for k in range(7, -1, -1):
+                work[k : k + 1, cols] = part
+                work[8 + k : 9 + k, cols] = factor
+                through = decay_run * wide(aux[16 + k : 17 + k, :], L)
+                part = through * part + ends[k : k + 1, cols]
+                factor = through * factor
+            pay[e, 0:1, cols] = part
+            entering, scaled = work[0:8, cols], work[8:16, cols]
+            pay[e, 1:2, cols] = down(U + V * entering)
+            pay[e, 2:3, cols] = down(V * scaled)
+            pay[e, 3:4, cols] = down(UN + VN * entering)
+            pay[e, 4:5, cols] = down(VN * scaled)
+            pay[e, 5:6, cols] = down(B)
+            pay[e, 6:7, cols] = down(D + DA * entering)
+            pay[e, 7:8, cols] = down(DA * scaled)
+
+        blocks(local_ends)
+        meanwhile(0)
+        own_decay = own_par[decay_row : decay_row + 1, :]
+        own_gain = own_par[gain_row : gain_row + 1, :]
+
+        def gathered():
+            whole_power = power(own_decay, T)
+            carried = jnp.zeros((1, fb), f32)
+            sums = [jnp.zeros((1, fb), f32)] * 4
+            for i in range(n - 1, -1, -1):
+                rows = arrive[e, i]
+                back[e, i, 0:1, :] = carried
+                for a, (plain, times) in enumerate(((1, 2), (3, 4), (5, None), (6, 7))):
+                    term = rows[plain : plain + 1, :]
+                    if times is not None:
+                        term = term + rows[times : times + 1, :] * carried
+                    sums[a] = sums[a] + term
+                carried = whole_power * wide(aux[8 + i : 9 + i, :], fb) * carried + rows[0:1, :]
+            for a in range(4):
+                seqpay[e, a : a + 1, :] = sums[a]
+            seqpay[e, 4:8, :] = jnp.zeros((4, fb), f32)
+
+        def totalled(sums):
+            rec, rec_norm = sums[0:1, :], sums[1:2, :]
+            for i in range(n):
+                back[e, i, 1:2, :] = rec
+                back[e, i, 2:3, :] = rec_norm
+                back[e, i, 3:8, :] = jnp.zeros((5, fb), f32)
+            spread = jnp.sqrt(1.0 - own_decay * own_decay)
+            small[3 * layer : 3 * layer + 1, :] = spread * rec_norm
+            small[3 * layer + 1 : 3 * layer + 2, :] = sums[2:3, :]
+            small[3 * layer + 2 : 3 * layer + 3, :] = (
+                sums[3:4, :] - own_decay / spread * own_gain * rec_norm
+            )
+
+        exchange(e, gathered, totalled)
+        meanwhile(1)
+        total = backland[e, 0:1, :]
+        for k in range(7, -1, -1):
+            work[k : k + 1, :] = total
+            total = run_power * wide(aux[16 + k : 17 + k, :], H) * total + ends[k : k + 1, :]
+
+        def full_scan(cols):
+            decay = spread8(par, decay_row, cols)
+            average = spread8(backland.at[layer], 1, cols)
+            inv_std = spread8(backland.at[layer], 2, cols)
+            frames_all = spread8(backland.at[layer], 3, cols)
+            scale = jnp.sqrt(1.0 - decay * decay) * spread8(par, gain_row, cols) * inv_std
+            rec = spread8(backland.at[e], 1, cols) / frames_all
+            rec_norm = spread8(backland.at[e], 2, cols) / frames_all * inv_std
+
+            def step(o, carry):
+                i = T // 16 - 1 - o
+                rows = pl.ds(pl.multiple_of(16 * i, 16), 16)
+                pair = projected[rows, cols].astype(f32)
+                outs = [None, None]
+                for h in (1, 0):
+                    goes, count = flags(2 * i + h)
+                    here = pl.ds(pl.multiple_of(16 * i + 8 * h + 8, 8), 8)
+                    run = states[here, cols] + carry
+                    centred = pair[8 * h : 8 * h + 8, :] - average
+                    outs[h] = scale * (run - count * (rec + rec_norm * centred))
+                    carry = (decay * goes) * run
+                dp[rows, cols] = jnp.concatenate(outs, axis=0).astype(bf16)
+                return carry
+
+            lax.fori_loop(0, T // 16, step, work[0:8, cols])
+
+        blocks(full_scan)
+        meanwhile(2)
+
+        def turn(b, _):
+            dpt[at(b, fb), :] = lax.dot_general(
+                eye[...], dp[:, at(b, fb)], (((1,), (1,)), ((), ())), preferred_element_type=f32
+            ).astype(bf16)
+            return 0
+
+        lax.fori_loop(0, n, turn, 0)
+
+    def input_gradient(weight, result):
+        def one(b, _):
+            result[:, at(b, fb)] = jnp.dot(
+                dp[...], weight[:, at(b, fb)], preferred_element_type=f32
+            ).astype(bf16)
+            return 0
+
+        lax.fori_loop(0, n, one, 0)
+
+    def relay_two(step):
+        if step == 0:
+            gather_two.advance(2)
+        elif step < 3:
+            gather_two.advance(3)
+
+    layer_forward(0, xr, wf_one, p_one, s_one, x_two, relay_two)
+    gather_two.finish()
+    others(lambda i: frames_sent(0, xs, i))
+    layer_forward(1, x_two, wf_two, p_two, s_two, xs, lambda step: None)
+
+    def place_out(a, ref, dest, i):
+        return neur_copy(
+            ref.at[:, at(i, fb)], dest.at[me], frame_sends.at[a, i], frame_recvs.at[a, me], i
+        )
+
+    def out_arrived(a, ref, dest, i):
+        neur_copy(
+            ref.at[:, at(i, fb)], dest.at[i], frame_sends.at[a, i], frame_recvs.at[a, i], i
+        ).wait()
+
+    others(lambda i: place_out(2, xs, out_land, i).start())
+    keep_out = pltpu.make_async_copy(xs.at[:, own_lanes], out_land.at[me], local_sems.at[4])
+    keep_out.start()
+    others(lambda i: frames_wait(1, gr, i))
+    others(lambda i: frames_sent(1, gs, i))
+
+    gather_two.drain()
+    layer_backward(1, gr, p_two, s_two, lambda step: None)
+    input_gradient(wf_two, gr)
+    reduce_two = Reduce(
+        env, dpt, x_two, lambda k: land.at[k], stage, reduce_sends.at[0], reduce_recvs.at[0], "y", "x"
+    )
+    reduce_one = Reduce(
+        env,
+        dpt,
+        xr,
+        lambda k: wf_two.at[at(k // 4, fb), at(k % 4, sz.qc)],
+        stage,
+        reduce_sends.at[1],
+        reduce_recvs.at[1],
+        "x",
+        "y",
+    )
+    result_two = Result(
+        env, dw_two, fin.at[0], final_sends.at[0], final_recvs.at[0], local_sems.at[6]
+    )
+    result_one = Result(
+        env, dw_one, fin.at[1], final_sends.at[1], final_recvs.at[1], local_sems.at[7]
+    )
+    reduce_two.cores()
+
+    def meanwhile(step):
+        if step == 0:
+            reduce_two.firsts()
+        if step == 1:
+            reduce_two.seconds()
+            reduce_two.lines()
+            fin[0] = reduce_two.total()
+            result_two.start()
+
+    layer_backward(0, gr, p_one, s_one, meanwhile)
+    input_gradient(wf_one, gs)
+    others(lambda i: place_out(3, gs, dx_land, i).start())
+    keep_dx = pltpu.make_async_copy(gs.at[:, own_lanes], dx_land.at[me], local_sems.at[5])
+    keep_dx.start()
+    result_two.finish()
+    reduce_two.drain()
+    reduce_one.cores()
+    reduce_one.firsts()
+    reduce_one.seconds()
+    reduce_one.lines()
+    fin[1] = reduce_one.total()
+    result_one.start()
+    others(lambda i: out_arrived(2, xs, out_land, i))
+    others(lambda i: out_arrived(3, gs, dx_land, i))
+    keep_out.wait()
+    keep_dx.wait()
+    result_one.finish()
+    reduce_one.drain()
+    gather_one.drain()
+    small[6:8, :] = jnp.zeros((2, fb), f32)
+
+
+def turn_back(sz, x_ref, g_ref, out_ref, dx_ref, output, input_grad):
+    step = pl.program_id(0)
+    T, fb, win, odd = sz.T, sz.fb, sz.win, sz.odd
+    output[...] = x_ref[...].astype(f32)
+    input_grad[...] = g_ref[...].astype(f32)
+
+    @pl.when(step < sz.n // 2)
+    def _():
+        row = lax.broadcasted_iota(jnp.int32, (T, win), 0)
+        column = lax.broadcasted_iota(jnp.int32, (T, win), 1)
+        frame = (row % 8) * sz.steps + row // 8
+        row = lax.broadcasted_iota(jnp.int32, (fb, fb), 0)
+        eye = jnp.where(row == lax.broadcasted_iota(jnp.int32, (fb, fb), 1), 1.0, 0.0).astype(bf16)
+        for half in range(2):
+            perm = jnp.where(column == frame + odd * half, 1.0, 0.0).astype(bf16)
+            lanes = pl.ds((T - odd) * half, win)
+            for source, result in ((out_ref, output), (dx_ref, input_grad)):
+                turned = lax.dot_general(
+                    eye, source[half], (((1,), (1,)), ((), ())), preferred_element_type=f32
+                ).astype(bf16)
+                result[:, lanes] += jnp.dot(turned, perm, preferred_element_type=f32)
+
+
+def frame_rows(sz, lengths, frame_mask):
+    T, steps = sz.T, sz.steps
+    me = lax.axis_index("neur")
+    starts = jnp.cumsum(lengths[0]) - lengths[0]
+    row = jnp.arange(T, dtype=jnp.int32)
+    slots = me * T + (row % 8) * steps + row // 8
+    goes = jnp.where(jnp.any(slots[:, None] == starts[None, :], axis=1), 0.0, 1.0)
+    part = lax.dynamic_slice(frame_mask, (me * T,), (T,)).reshape(8, steps).T.reshape(T)
+    inside = slots < jnp.sum(lengths[0])
+    count = jnp.where((part > 0) & inside, 1.0, 0.0)
+    places = jnp.arange(frame_mask.shape[0], dtype=jnp.int32)
+    block = jnp.sum(jnp.where((places < jnp.sum(lengths[0])) & (frame_mask > 0), 1.0, 0.0))
+    run = jnp.arange(8, dtype=jnp.int32)
+    first = me * T + run * steps
+    behind = jnp.where(starts[None, :] < first[:, None], starts[None, :], 0)
+    since = (first - jnp.max(behind, axis=1)).astype(f32)
+
+    def unbroken(begin, length):
+        inside = (starts[None, :] >= begin[:, None]) & (starts[None, :] < begin[:, None] + length)
+        return jnp.where(jnp.any(inside, axis=1), 0.0, 1.0)
+
+    whole = unbroken(run * T, T)
+    own = unbroken(first, steps)
+    aux = jnp.concatenate([since, whole, own, jnp.full((8,), 1.0) * block]).astype(f32)
+
+    def lanes(values):
+        return jnp.broadcast_to(values.astype(f32)[:, None], (values.shape[0], 128))
+
+    return lanes(goes), lanes(count), lanes(aux)
+
+
+def frames_apart(sz, inputs, weight_one, weight_two, params, lengths, frame_mask, out_grad):
+    n, seqs, H, fb, T, Z, qc = sz.n, sz.seqs, sz.H, sz.fb, sz.T, sz.Z, sz.qc
+    goes, count, aux = frame_rows(sz, lengths, frame_mask)
+    own_par = jnp.concatenate([jnp.stack(params), jnp.zeros((2, fb), f32)], axis=0)
+    whole = pl.BlockSpec(memory_space=pltpu.VMEM)
+    anywhere = pl.BlockSpec(memory_space=pl.ANY)
+    vmem, sem = pltpu.VMEM, pltpu.SemaphoreType.DMA
+    frames_shape = (T, H)
+    matmul = 2 * T * H * H
+    out_land, dx_land, dw_one, dw_two, small = pl.pallas_call(
+        functools.partial(network, sz),
+        out_shape=(
+            jax.ShapeDtypeStruct((n, T, fb), bf16),
+            jax.ShapeDtypeStruct((n, T, fb), bf16),
+            jax.ShapeDtypeStruct((fb, H), f32),
+            jax.ShapeDtypeStruct((fb, H), f32),
+            jax.ShapeDtypeStruct((8, fb), f32),
+        ),
+        in_specs=[anywhere] * 4 + [whole] * 4,
+        out_specs=(anywhere, anywhere, anywhere, anywhere, whole),
+        scratch_shapes=[
+            vmem((fb, sz.valid), bf16),
+            vmem((2, T, sz.win), bf16),
+            vmem((fb, fb), bf16),
+            vmem(frames_shape, bf16),
+            vmem(frames_shape, bf16),
+            vmem(frames_shape, bf16),
+            vmem(frames_shape, bf16),
+            vmem(frames_shape, bf16),
+            vmem(frames_shape, bf16),
+            vmem(frames_shape, bf16),
+            vmem(frames_shape, bf16),
+            vmem((H, T), bf16),
+            vmem((T + 8, H), f32),
+            vmem((T + 8, H), f32),
+            vmem((H, H), bf16),
+            vmem((H, H), bf16),
+            vmem((8 * Z, fb, qc), bf16),
+            vmem((8 * Z, fb, qc), bf16),
+            vmem((2, fb, qc), f32),
+            vmem((8, H), f32),
+            vmem((8, H), f32),
+            vmem((16, H), f32),
+            vmem((4, 8, H), f32),
+            vmem((4, n, 8, fb), f32),
+            vmem((4, 8, fb), f32),
+            vmem((4, seqs, 8, fb), f32),
+            vmem((4, n, 8, fb), f32),
+            vmem((4, 8, H), f32),
+            sem((8,)),
+            sem((n,)),
+            sem((n,)),
+            sem((4, n)),
+            sem((4, n)),
+            sem((2, 8 * Z)),
+            sem((2, 8 * Z)),
+            sem((8, n)),
+            sem((8, n)),
+            sem((4, seqs)),
+            sem((4, seqs)),
+            sem((2, 8 * Z)),
+            sem((2, 8 * Z)),
+            sem((2, 3)),
+            sem((2, 3)),
+        ],
+        compiler_params=pltpu.CompilerParams(
+            collective_id=0, has_side_effects=True, vmem_limit_bytes=63 * 1024 * 1024
+        ),
+        cost_estimate=pl.CostEstimate(
+            flops=6 * matmul, bytes_accessed=16 * fb * H, transcendentals=6 * T * H
+        ),
+        name="network",
+    )(inputs, out_grad, weight_one, weight_two, own_par, goes, count, aux)
+    tok = inputs.shape[1]
+    pairs = n // 2
+    steps = pl.cdiv(tok, 2 * T)
+    frames_spec = pl.BlockSpec((fb, 2 * T), lambda p: (0, p))
+    land_spec = pl.BlockSpec((2, T, fb), lambda p: (jnp.minimum(p, pairs - 1), 0, 0))
+    output, input_grad = pl.pallas_call(
+        functools.partial(turn_back, sz),
+        grid=(steps,),
+        out_shape=(jax.ShapeDtypeStruct((fb, tok), f32),) * 2,
+        in_specs=[frames_spec, frames_spec, land_spec, land_spec],
+        out_specs=(frames_spec, frames_spec),
+        compiler_params=pltpu.CompilerParams(vmem_limit_bytes=48 * 1024 * 1024),
+        name="turn_back",
+    )(inputs, out_grad, out_land, dx_land)
+    return (
+        output,
+        input_grad,
+        dw_one,
+        small[0],
+        small[1],
+        small[2],
+        dw_two,
+        small[3],
+        small[4],
+        small[5],
+    )
 
 
 def frame_tables(lengths, frame_mask):
@@ -150,6 +1217,20 @@
     frame_mask,
     out_grad,
 ):
+    seqs, n = lax.axis_size("seq"), lax.axis_size("neur")
+    H, (fb, tok) = weight_one.shape[1], inputs.shape
+    if fits(n, seqs, H, fb, tok):
+        params = (gain_one, gain_two, bias_one, bias_two, decay_one, decay_two)
+        return frames_apart(
+            Sizes(n, seqs, H, fb, tok),
+            inputs,
+            weight_one,
+            weight_two,
+            params,
+            lengths,
+            frame_mask,
+            out_grad,
+        )
     continues, counted = frame_tables(lengths, frame_mask)
     first_out, first_kept = layer_forward(
         inputs, weight_one, gain_one, bias_one, decay_one, continues, counted

time: 1500 us -> 471 us (0.31)
  waiting for transfers between devices: 733 us -> 0 us
  Pallas kernels: 0 us -> 448 us
  matrix products: 410 us -> 0 us
  blocking collectives: 130 us -> 0 us
  local copies, waits for them, and re-layouts: 96.5 us -> 14.4 us
  other arithmetic: 81.3 us -> 6.13 us
  starting transfers between devices: 26.5 us -> 0 us
  between operations: 16 us -> 0.71 us
    pallas_call x0 -> x2, Pallas kernels: none -> 448 us  [the longest x1 439 us: frames_apart(): pl.pallas_call(functools.partial(network, sz), out_shape=(jax.ShapeDtypeS...]
    dot_general x62 -> x0, matrix products: 410 us -> none  [the longest x28 224 us: linear_scan(): jnp.dot(running, mover, precision=lax.Precision.HIGHEST, preferred_elemen...]
    reduce_scatter x2 -> x0, waiting for transfers between devices: 379 us -> none  [layer_backward(): lax.psum_scatter(jnp.einsum('ot,it->oi', grad_rows, frames_in, preferred_...]
    all_to_all x6 -> x0, waiting for transfers between devices: 208 us -> none  [the longest x2 89.6 us: layer_forward(): lax.all_to_all(layer_input, 'neur', split_axis=1, concat_axis=0, tiled=True)]
    all_to_all x2 -> x0, blocking collectives: 103 us -> none  [layer_backward(): lax.all_to_all(proj_grad.astype(jnp.bfloat16), 'neur', split_axis=1, conc...]
    psum x1 -> x0, waiting for transfers between devices: 72.7 us -> none  [layer_backward(): weight_grad, decay_sum = lax.psum((weight_rows, decay_part), 'seq')]
    all_gather x2 -> x0, waiting for transfers between devices: 71.9 us -> none  [layer_forward(): lax.all_gather(weight, 'neur', axis=0, tiled=True)]
    reduce_sum x8 -> x2, other arithmetic: 33.4 us -> 3.26 us  [the longest x1 1.97 us: frame_rows(): jnp.sum(jnp.where((places < jnp.sum(lengths[0])) & (frame_mask > 0), 1.0,...]
  transfers between devices with their start and end apart: 11 -> 0, of which waited for: 9 -> 0; matrix products, arithmetic and copies ran while one was open for 25% -> 0% of each run, Pallas kernels for 0% -> 0%
where the time goes in v1:
time: 471 us; the launch traced here: 469 us
  Pallas kernels  448 us (95%)
  local copies, waits for them, and re-layouts  14.4 us (3%)
  other arithmetic  6.13 us (1%)
    pallas_call x1, Pallas kernels, frames_apart(): pl.pallas_call(functools.partial(network, sz), out_shape=(jax.ShapeDtypeS...  439 us

profile of v1, /device:TPU:0, one launch (start us, length us, event | category | flops | bytes accessed | tf_op | source)
XLA Modules:
  0.0 469.2 jit_solution(13872147691978063417)
XLA Ops:
  0.6 0.8 dynamic-slice_compare_fusion
  1.4 0.1 gt.24
  1.5 0.8 reduce-window_clone.1
  2.4 1.3 fusion.10
  3.7 2.0 select_reduce_fusion
  5.6 0.6 mul.48
  6.3 0.2 select_reduce_fusion.1
  6.5 0.2 and_reduce_fusion.1
  6.7 0.1 pad_maximum_fusion
  6.8 0.1 compare_reduce_fusion
  6.9 1.4 concatenate.6.own_par
  8.3 0.1 copy.23
  8.4 0.1 gt.26
  8.5 0.7 and_select_fusion
  9.1 0.7 broadcast_in_dim.82.aux
  9.8 0.8 broadcast_in_dim.76.counted
  10.6 0.8 broadcast_in_dim.75.cont
  11.4 439.0 %network.1 = (bf16[8,448,256]{2,1,0:T(8,128)(2,1)}, bf16[8,448,256]{2,1,0:T(8,128)(2,1)}, f32[256,2048]{1,0:T(8,128)}, f32[256,2048]{1,0:T(8,128)}, f32[8,256]{1,0:T(8,128)}) custom-call(bf16[256,4096]{1,0:T(8,128)(2,1)} %x_ref.1, bf16[256,4096]{1,0:T(8,128)(2,1)} %g_ref.1, bf16[256,2048]{1,0:T(8,128)(2,1)} %w_one.1, bf16[256,2048]{1,0:T(8,128)(2,1)} %w_two.1, ...), custom_call_target="tpu_custom_call" | custom-call | flops 22548578304 | bytes 8388608 | tf_op jit(solution)/shard_map/network/pallas_call | solution.py:985
  450.5 1.5 fusion.9
  452.0 0.0 copy-start
  452.0 1.6 copy-done
  453.6 0.0 copy-start.1
  453.6 1.5 copy-done.1
  455.1 0.0 copy-start.2
  455.1 1.5 copy-done.2
  456.6 0.0 copy-start.4
  456.6 9.0 %turn_back.1 = (f32[256,4096]{1,0:T(8,128)}, f32[256,4096]{1,0:T(8,128)}) custom-call(bf16[256,4096]{1,0:T(8,128)(2,1)S(1)} %copy-done, bf16[256,4096]{1,0:T(8,128)(2,1)} %g_ref.1, bf16[8,448,256]{2,1,0:T(8,128)(2,1)S(1)} %copy-done.1, bf16[8,448,256]{2,1,0:T(8,128)(2,1)S(1)} %copy-done.2), custom_call_target="tpu_custom_call" | custom-call | tf_op jit(solution)/shard_map/turn_back/pallas_call | solution.py:1054
  465.5 0.0 copy-done.4
  465.5 0.0 copy-start.3
  465.5 1.3 copy.26
  466.9 1.0 copy-done.3
  467.9 1.3 copy.27
  (8 shorter events, 0.0 us)
Async XLA Ops:
  452.0 1.6 copy-start
  453.6 1.5 copy-start.1
  455.1 1.5 copy-start.2
  456.6 9.0 %copy-start.4 = (f32[256,2048]{1,0:T(8,128)S(1)}, f32[256,2048]{1,0:T(8,128)}, u32[]{:S(2)}) copy-start(f32[256,2048]{1,0:T(8,128)} %get-tuple-element.50) | copy-start | bytes 6291460
  465.5 2.3 copy-start.3

commit v2 on v1

--- a/solution.py
+++ b/solution.py
@@ -56,6 +56,7 @@
         self.Z = n // 2
         self.odd = self.T % 128
         self.win = self.T + self.odd
+        self.K = self.T + 16
         self.L = min(512, H)
 
 
@@ -66,43 +67,11 @@
     return T % 64 == 0 and valid_frames % 128 == 0 and tok_dev >= valid_frames
 
 
-class Gather:
-    def __init__(self, env, source, full, sends, recvs, first, second):
-        self.env, self.full, self.sends, self.recvs = env, full, sends, recvs
-        self.first, self.second = first, second
-        z = env.z
-        Z = env.sz.Z
-        self.source = source.at[:, at(env.s, env.sz.qc)]
-        self.events = [(0, 0, 0)]
-        for dz in range(1, Z):
-            self.events += [(dz, 0, 0), (dz - 1, 1, 0)]
-        self.events.append((Z - 1, 1, 0))
-        self.events += [(dz, a, 1) for dz, a, _ in self.events]
-        self.done = 0
-
-    def block(self, dz, a, b, flip=0):
-        env = self.env
-        coords = {"x": env.x, "y": env.y}
-        coords[self.first] = (coords[self.first] + a) % 2
-        coords[self.second] = (coords[self.second] + b) % 2
-        zz = (env.z + env.sz.Z - dz) % env.sz.Z
-        cc = (env.c + flip) % 2
-        return self.full.at[
-            at(2 * zz + coords["x"], env.sz.fb), at(2 * coords["y"] + cc, env.sz.qc)
-        ]
-
-    def index(self, stage, dz, a, b):
-        Z = self.env.sz.Z
-        if stage == "z":
-            return dz - 1
-        if stage == "first":
-            return Z - 1 + dz
-        if stage == "second":
-            return 2 * Z - 1 + 2 * dz + a
-        return 4 * Z - 1 + 4 * dz + 2 * a + b
-
-    def copy(self, stage, source, dest, dz, a, b, target):
-        k = self.index(stage, dz, a, b)
+class Line:
+    def __init__(self, env, sends, recvs):
+        self.env, self.sends, self.recvs = env, sends, recvs
+
+    def copy(self, k, source, dest, target):
         return pltpu.make_async_remote_copy(
             src_ref=source,
             dst_ref=dest,
@@ -112,148 +81,272 @@
             device_id_type=MESH,
         )
 
-    def arrival(self, dz, a, b):
-        stage = "second" if b else "first" if a else "z"
-        block = self.block(dz, a, b)
-        self.copy(stage, block, block, dz, a, b, self.env.across("x")).wait_recv()
+    def arrived(self, k, ref):
+        self.copy(k, ref, ref, self.env.across("x")).wait_recv()
+
+    def sent(self, k, ref):
+        self.copy(k, ref, ref, self.env.across("x")).wait_send()
+
+    def along(self, dz):
+        z, Z = self.env.z, self.env.sz.Z
+        if dz == 0:
+            return [(None, z, 0)]
+        return [(z >= dz, z - dz, 1), (z + dz < Z, z + dz, -1)]
+
+
+def if_so(condition, body):
+    if condition is None:
+        body()
+    else:
+        pl.when(condition)(body)
+
+
+class Gather(Line):
+    def __init__(self, env, source, full, sends, recvs):
+        super().__init__(env, sends, recvs)
+        self.full = full
+        self.source = source.at[:, at(env.s, env.sz.qc)]
+        Z = env.sz.Z
+        self.steps = []
+        for dz in range(1, Z):
+            self.steps.append(functools.partial(self.line, dz))
+            self.steps.append(functools.partial(self.sides, dz - 1))
+        self.steps.append(functools.partial(self.sides, Z - 1))
+        self.steps.append(self.diagonals)
+        self.steps.append(self.cores)
+
+    def block(self, zz, fx, fy, fc=0):
+        env = self.env
+        rows = at(2 * zz + (env.x + fx) % 2, env.sz.fb)
+        return self.full.at[rows, at(2 * ((env.y + fy) % 2) + (env.c + fc) % 2, env.sz.qc)]
+
+    def half(self, ref, h):
+        return ref.at[pl.ds(h * (self.env.sz.fb // 2), self.env.sz.fb // 2), :]
+
+    def spread(self, zz, source):
+        env, Z = self.env, self.env.sz.Z
+        dest = self.block(zz, 0, 0)
+        self.copy(2 * Z + zz, source, dest, env.across("x")).start()
+        self.copy(3 * Z + zz, source, dest, env.across("y")).start()
+        self.copy(6 * Z + zz, source, dest, env.across("core")).start()
+
+    def pass_on(self, zz, source, way):
+        env, Z = self.env, self.env.sz.Z
+        dest = self.block(zz, 0, 0)
+
+        def go():
+            pltpu.make_async_remote_copy(
+                src_ref=source,
+                dst_ref=dest,
+                send_sem=self.sends.at[zz if way > 0 else Z + zz],
+                recv_sem=self.recvs.at[zz],
+                device_id={"neur": 2 * (env.z + way) + env.x},
+                device_id_type=MESH,
+            ).start()
+
+        pl.when(env.z < Z - 1 if way > 0 else env.z > 0)(go)
 
     def start(self):
-        env = self.env
-        own = self.block(0, 0, 0)
-        for dz in range(1, env.sz.Z):
-            target = {"neur": 2 * ((env.z + dz) % env.sz.Z) + env.x}
-            self.copy("z", self.source, own, dz, 0, 0, target).start()
-        self.relay(self.source, 0, 0, 0)
-        self.done = 1
-
-    def relay(self, source, dz, a, b):
-        env = self.env
-        dest = self.block(dz, a, b)
-        if not a and not b:
-            self.copy("first", source, dest, dz, a, b, env.across(self.first)).start()
-        if not b:
-            self.copy("second", source, dest, dz, a, b, env.across(self.second)).start()
-        self.copy("core", source, dest, dz, a, b, env.across("core")).start()
+        z = self.env.z
+        self.pass_on(z, self.source, 1)
+        self.pass_on(z, self.source, -1)
+        self.spread(z, self.source)
+
+    def line(self, dz):
+        for condition, zz, way in self.along(dz):
+
+            def one(zz=zz, way=way):
+                block = self.block(zz, 0, 0)
+                self.arrived(zz, block)
+                self.pass_on(zz, block, way)
+                self.spread(zz, block)
+
+            if_so(condition, one)
+
+    def sides(self, dz):
+        env, Z = self.env, self.env.sz.Z
+        for condition, zz, _ in self.along(dz):
+
+            def one(zz=zz):
+                block = self.block(zz, 1, 0)
+                self.arrived(2 * Z + zz, block)
+                part = self.half(block, 1)
+                self.copy(5 * Z + zz, part, part, env.across("y")).start()
+                self.copy(7 * Z + zz, block, block, env.across("core")).start()
+                block = self.block(zz, 0, 1)
+                self.arrived(3 * Z + zz, block)
+                part = self.half(block, 0)
+                self.copy(4 * Z + zz, part, part, env.across("x")).start()
+                self.copy(8 * Z + zz, block, block, env.across("core")).start()
+
+            if_so(condition, one)
+
+    def diagonals(self):
+        env, Z = self.env, self.env.sz.Z
+        for dz in range(Z):
+            for condition, zz, _ in self.along(dz):
+
+                def one(zz=zz):
+                    block = self.block(zz, 1, 1)
+                    self.arrived(4 * Z + zz, self.half(block, 0))
+                    self.arrived(5 * Z + zz, self.half(block, 1))
+                    self.copy(9 * Z + zz, block, block, env.across("core")).start()
+
+                if_so(condition, one)
+
+    def cores(self):
+        Z = self.env.sz.Z
+        for k, (fx, fy) in enumerate(((0, 0), (1, 0), (0, 1), (1, 1))):
+            for zz in range(Z):
+                self.arrived((6 + k) * Z + zz, self.block(zz, fx, fy, 1))
 
     def advance(self, count=None):
-        last = len(self.events) if count is None else min(len(self.events), self.done + count)
-        for dz, a, b in self.events[self.done : last]:
-            self.arrival(dz, a, b)
-            self.relay(self.block(dz, a, b), dz, a, b)
-        self.done = last
+        for _ in range(len(self.steps) if count is None else min(count, len(self.steps))):
+            self.steps.pop(0)()
+
+    def drain(self):
+        env, Z = self.env, self.env.sz.Z
+        block = self.block(0, 0, 0)
+        for zz in range(Z):
+            pl.when((zz <= env.z) & (env.z < Z - 1))(lambda zz=zz: self.sent(zz, block))
+            pl.when((zz >= env.z) & (env.z > 0))(lambda zz=zz: self.sent(Z + zz, block))
+            for k in (2, 3, 6, 7, 8, 9):
+                self.sent(k * Z + zz, block)
+            for k in (4, 5):
+                self.sent(k * Z + zz, self.half(block, 0))
+
+
+class Reduce(Line):
+    kinds = ((1, 1), (1, 0), (0, 1), (0, 0))
+
+    def __init__(self, env, grads, frames, land, spare, stage, total, sends, recvs):
+        super().__init__(env, sends, recvs)
+        self.grads, self.frames, self.land, self.spare = grads, frames, land, spare
+        self.stage, self.total = stage, total
+
+    def product(self, kind, zz, fc=0):
+        env, sz = self.env, self.env.sz
+        fx, fy = self.kinds[kind]
+        rows = at(2 * zz + (env.x + fx) % 2, sz.fb)
+        columns = at(2 * ((env.y + fy) % 2) + (env.c + fc) % 2, sz.qc)
+        return jnp.dot(
+            self.grads[rows, :], self.frames[:, columns], preferred_element_type=f32
+        )
+
+    def half(self, ref, h):
+        return ref.at[pl.ds(h * (self.env.sz.fb // 2), self.env.sz.fb // 2), :]
+
+    def landed(self, k, slot):
+        self.arrived(k, self.land(slot))
+        return self.land(slot)[...].astype(f32)
+
+    def cores(self, kind):
+        env, Z = self.env, self.env.sz.Z
+
+        def one(zz, _):
+            k = kind * Z + zz
+            held = (kind % 2) * Z + zz
+            if kind >= 2:
+                self.sent(k - 2 * Z, self.stage.at[held])
+            self.stage[held] = self.product(kind, zz, 1).astype(bf16)
+            self.copy(k, self.stage.at[held], self.land(k), env.across("core")).start()
+            return 0
+
+        lax.fori_loop(0, Z, one, 0)
+
+    def diagonals(self):
+        env, Z = self.env, self.env.sz.Z
+
+        def one(zz, _):
+            held = self.stage.at[2 * Z + zz]
+            held[...] = (self.product(0, zz) + self.landed(zz, zz)).astype(bf16)
+            slot = self.land(4 * Z + zz)
+            for k, h, axis in ((4, 0, "x"), (5, 1, "y")):
+                self.copy(
+                    k * Z + zz, self.half(held, h), self.half(slot, h), env.across(axis)
+                ).start()
+            return 0
+
+        lax.fori_loop(0, Z, one, 0)
+
+    def sides(self, low=0, high=None):
+        env, Z = self.env, self.env.sz.Z
+        rows = env.sz.fb // 2
+
+        def one(zz, _):
+            slot = self.land(4 * Z + zz)
+            for kind, h, wait, k, axis in ((1, 1, 5, 6, "x"), (2, 0, 4, 7, "y")):
+                tile = self.product(kind, zz) + self.landed(kind * Z + zz, kind * Z + zz)
+                part = self.half(slot, h)
+                self.arrived(wait * Z + zz, part)
+                held = self.stage.at[(2 + kind) * Z + zz]
+                other = 1 - h
+                own = slice(h * rows, (h + 1) * rows)
+                rest = slice(other * rows, (other + 1) * rows)
+                self.half(held, h)[...] = (tile[own, :] + part[...].astype(f32)).astype(bf16)
+                self.half(held, other)[...] = tile[rest, :].astype(bf16)
+                self.copy(
+                    k * Z + zz, held, self.land((4 + kind) * Z + zz), env.across(axis)
+                ).start()
+            return 0
+
+        lax.fori_loop(low, Z if high is None else high, one, 0)
+
+    def joined(self, zz):
+        Z = self.env.sz.Z
+        tile = self.product(3, zz) + self.landed(3 * Z + zz, 3 * Z + zz)
+        tile = tile + self.landed(6 * Z + zz, 5 * Z + zz)
+        self.total[...] = tile + self.landed(7 * Z + zz, 6 * Z + zz)
+
+    def lines(self):
+        env, Z, z = self.env, self.env.sz.Z, self.env.z
+
+        def onward(zz, way):
+            k, slot = (8 if way > 0 else 9) * Z + zz, 7 * Z + zz
+            self.joined(zz)
+
+            @pl.when(z > 0 if way > 0 else z < Z - 1)
+            def _():
+                self.total[...] += self.landed(k, slot)
+
+            held = self.stage.at[2 * Z + zz]
+            self.sent(4 * Z + zz, self.half(held, 0))
+            self.sent(5 * Z + zz, self.half(held, 0))
+            held[...] = self.total[...].astype(bf16)
+            target = {"neur": 2 * (z + way) + env.x}
+            if way > 0:
+                self.copy(k, held, self.land(slot), target).start()
+            else:
+                pl.when(zz == z - 1)(lambda: self.copy(k, held, self.spare, target).start())
+                pl.when(zz != z - 1)(lambda: self.copy(k, held, self.land(slot), target).start())
+
+        for i in range(Z - 1):
+            pl.when(Z - 1 - i > z)(functools.partial(onward, Z - 1 - i, 1))
+            pl.when(i < z)(functools.partial(onward, i, -1))
 
     def finish(self):
-        self.advance()
-        for dz, a, b in self.events:
-            block = self.block(dz, a, b, 1)
-            self.copy("core", block, block, dz, a, b, self.env.across("core")).wait_recv()
+        Z, z = self.env.sz.Z, self.env.z
+        self.joined(z)
+
+        @pl.when(z > 0)
+        def _():
+            self.total[...] += self.landed(8 * Z + z, 7 * Z + z)
+
+        @pl.when(z < Z - 1)
+        def _():
+            self.arrived(9 * Z + z, self.spare)
+            self.total[...] += self.spare[...].astype(f32)
 
     def drain(self):
-        block = self.block(0, 0, 0)
-        for k in range(8 * self.env.sz.Z - 1):
-            pltpu.make_async_remote_copy(
-                src_ref=block,
-                dst_ref=block,
-                send_sem=self.sends.at[k],
-                recv_sem=self.recvs.at[k],
-                device_id=self.env.across("x"),
-                device_id_type=MESH,
-            ).wait_send()
-
-
-class Reduce:
-    def __init__(self, env, grads, frames, land, stage, sends, recvs, first, second):
-        self.env, self.grads, self.frames, self.land, self.stage = env, grads, frames, land, stage
-        self.sends, self.recvs, self.first, self.second = sends, recvs, first, second
-
-    def place(self, p):
-        env, Z = self.env, self.env.sz.Z
-        coords = {"x": env.x, "y": env.y}
-        coords[self.first] = (coords[self.first] + 1 - p // (2 * Z)) % 2
-        coords[self.second] = (coords[self.second] + 1 - (p // Z) % 2) % 2
-        zz = (env.z + p % Z + 1) % Z
-        return zz, coords["x"], coords["y"]
-
-    def tile(self, p, cc):
-        sz = self.env.sz
-        zz, xx, yy = self.place(p)
-        return jnp.dot(
-            self.grads[at(2 * zz + xx, sz.fb), :],
-            self.frames[:, at(2 * yy + cc, sz.qc)],
-            preferred_element_type=f32,
-        )
-
-    def copy(self, k, target):
-        return pltpu.make_async_remote_copy(
-            src_ref=self.stage.at[k],
-            dst_ref=self.land(k),
-            send_sem=self.sends.at[k],
-            recv_sem=self.recvs.at[k],
-            device_id=target,
-            device_id_type=MESH,
-        )
-
-    def landed(self, k):
-        self.copy(k, self.env.across("x")).wait_recv()
-        return self.land(k)[...].astype(f32)
-
-    def send(self, k, tile, target):
-        self.stage[k] = tile.astype(bf16)
-        self.copy(k, target).start()
-
-    def cores(self):
-        env, Z = self.env, self.env.sz.Z
-
-        def one(p, _):
-            self.send(p, self.tile(p, (env.c + 1) % 2), env.across("core"))
-            return 0
-
-        lax.fori_loop(0, 4 * Z, one, 0)
-
-    def firsts(self, low=0, high=None):
-        env, Z = self.env, self.env.sz.Z
-
-        def one(p, _):
-            tile = self.tile(p, env.c) + self.landed(p)
-            self.send(4 * Z + p, tile, env.across(self.first))
-            return 0
-
-        lax.fori_loop(low, 2 * Z if high is None else high, one, 0)
-
-    def seconds(self):
-        env, Z = self.env, self.env.sz.Z
-
-        def one(p, _):
-            tile = self.tile(p, env.c) + self.landed(p) + self.landed(p + 2 * Z)
-            self.send(4 * Z + p, tile, env.across(self.second))
-            return 0
-
-        lax.fori_loop(2 * Z, 3 * Z, one, 0)
-
-    def lines(self):
-        env, Z = self.env, self.env.sz.Z
-
-        def one(p, _):
-            tile = self.tile(p, env.c) + self.landed(p) + self.landed(p + 2 * Z)
-            tile = tile + self.landed(p + 3 * Z)
-            target = {"neur": 2 * ((env.z + p % Z + 1) % Z) + env.x}
-            self.send(4 * Z + p, tile, target)
-            return 0
-
-        lax.fori_loop(3 * Z, 4 * Z - 1, one, 0)
-
-    def total(self):
-        env, Z = self.env, self.env.sz.Z
-        p = 4 * Z - 1
-        tile = self.tile(p, env.c) + self.landed(p) + self.landed(p + 2 * Z)
-        tile = tile + self.landed(p + 3 * Z)
-        for k in range(7 * Z, 8 * Z - 1):
-            tile = tile + self.landed(k)
-        return tile
-
-    def drain(self):
-        for k in range(8 * self.env.sz.Z - 1):
-            self.copy(k, self.env.across("x")).wait_send()
+        Z, z = self.env.sz.Z, self.env.z
+        held = self.stage.at[0]
+        for zz in range(Z):
+            for k in (2, 3, 6, 7):
+                self.sent(k * Z + zz, held)
+            for k in (4, 5):
+                pl.when(zz == z)(lambda k=k, zz=zz: self.sent(k * Z + zz, self.half(held, 0)))
+            pl.when(zz > z)(lambda zz=zz: self.sent(8 * Z + zz, held))
+            pl.when(zz < z)(lambda zz=zz: self.sent(9 * Z + zz, held))
 
 
 class Result:
@@ -331,13 +424,15 @@
     p_two,
     x_two,
     dp,
-    dpt,
+    dpt_one,
+    dpt_two,
     s_one,
     s_two,
     wf_one,
     wf_two,
     land,
     stage,
+    spare,
     fin,
     par,
     ends,
@@ -348,6 +443,10 @@
     seqland,
     back,
     backland,
+    sumpay,
+    sumland,
+    sumseq,
+    sumseqland,
     local_sems,
     par_sends,
     par_recvs,
@@ -363,6 +462,8 @@
     reduce_recvs,
     final_sends,
     final_recvs,
+    sum_sends,
+    sum_recvs,
 ):
     n, seqs, H, fb, T, steps, L = sz.n, sz.seqs, sz.H, sz.fb, sz.T, sz.steps, sz.L
     env = Env()
@@ -423,10 +524,10 @@
     others(lambda i: par_copy(i).start())
     par[:, own_lanes] = own_par[...]
 
-    gather_one = Gather(env, w_one, wf_one, gather_sends.at[0], gather_recvs.at[0], "x", "y")
-    gather_two = Gather(env, w_two, wf_two, gather_sends.at[1], gather_recvs.at[1], "y", "x")
-    own_one = pltpu.make_async_copy(gather_one.source, gather_one.block(0, 0, 0), local_sems.at[2])
-    own_two = pltpu.make_async_copy(gather_two.source, gather_two.block(0, 0, 0), local_sems.at[3])
+    gather_one = Gather(env, w_one, wf_one, gather_sends.at[0], gather_recvs.at[0])
+    gather_two = Gather(env, w_two, wf_two, gather_sends.at[1], gather_recvs.at[1])
+    own_one = pltpu.make_async_copy(gather_one.source, gather_one.block(env.z, 0, 0), local_sems.at[2])
+    own_two = pltpu.make_async_copy(gather_two.source, gather_two.block(env.z, 0, 0), local_sems.at[3])
     own_one.start()
     own_two.start()
     gather_one.start()
@@ -453,21 +554,21 @@
         return neur_copy(source, dest, frame_sends.at[a, i], frame_recvs.at[a, me], i)
 
     def frames_wait(a, ref, i):
-        part = ref.at[:, at(i, fb)]
+        part = ref.at[pl.ds(0, T), at(i, fb)]
         neur_copy(part, part, frame_sends.at[a, i], frame_recvs.at[a, i], i).wait_recv()
 
     def frames_sent(a, ref, i):
-        part = ref.at[:, at(i, fb)]
+        part = ref.at[pl.ds(0, T), at(i, fb)]
         neur_copy(part, part, frame_sends.at[a, i], frame_recvs.at[a, i], i).wait_send()
 
     load_x.wait()
 
     def send_x(i):
         xs[:, at(i, fb)] = turned(i)
-        frames_copy(0, xs.at[:, at(i, fb)], xr.at[:, own_lanes], i).start()
+        frames_copy(0, xs.at[:, at(i, fb)], xr.at[pl.ds(0, T), own_lanes], i).start()
 
     others(send_x)
-    xr[:, own_lanes] = turned(me)
+    xr[0:T, own_lanes] = turned(me)
     load_g = pltpu.make_async_copy(g_hbm.at[:, pl.ds(0, sz.valid)], raw, local_sems.at[1])
     load_g.start()
     gather_one.advance(2)
@@ -478,9 +579,9 @@
 
     others(turn_g)
     gr[:, own_lanes] = turned(me)
-    gather_one.finish()
+    gather_one.advance(len(gather_one.steps) - 1)
     gather_two.start()
-    others(lambda i: frames_copy(1, gs.at[:, at(i, fb)], gr.at[:, own_lanes], i).start())
+    gather_one.advance()
     own_one.wait()
     own_two.wait()
     others(lambda i: frames_wait(0, xr, i))
@@ -496,7 +597,7 @@
     def project(frames, weight, result):
         def one(b, _):
             result[:, at(b, fb)] = lax.dot_general(
-                frames[...],
+                frames[0:T, :],
                 weight[at(b, fb), :],
                 (((1,), (1,)), ((), ())),
                 preferred_element_type=f32,
@@ -517,7 +618,7 @@
     def down(value):
         return jnp.sum(value, axis=0, keepdims=True)
 
-    def exchange(e, gathered, totalled):
+    def exchange(e, gathered, totalled, gap):
         def out_copy(i):
             return neur_copy(
                 pay.at[e, :, at(i, fb)],
@@ -529,6 +630,7 @@
 
         others(lambda i: out_copy(i).start())
         arrive[e, me] = pay[e, :, own_lanes]
+        gap()
 
         def out_wait(i):
             neur_copy(
@@ -558,6 +660,7 @@
 
         others(lambda i: along_copy(i).start(), seqs, mine)
         seqland[e, mine] = seqpay[e]
+        gap()
         others(along_wait, seqs, mine)
         sums = seqland[e, 0]
         for i in range(1, seqs):
@@ -584,19 +687,20 @@
 
         others(lambda i: back_copy(i).start())
         backland[e, :, own_lanes] = back[e, me]
+        gap()
         others(back_wait)
 
-    def layer_forward(layer, frames, weight, projected, states, store, meanwhile):
+    def layer_forward(layer, frames, weight, projected, states, store, gap):
         e = layer
         decay_row, gain_row, bias_row = DECAY + layer, GAIN + layer, BIAS + layer
         project(frames, weight, projected)
-        meanwhile(0)
+        gap()
 
         def local_ends(cols):
             decay = spread8(par, decay_row, cols)
 
             def step(i, carry):
-                state, first, second = carry
+                state, first, second, inward = carry
                 pair = projected[pl.ds(pl.multiple_of(16 * i, 16), 16), cols].astype(f32)
                 for h in range(2):
                     value = pair[8 * h : 8 * h + 8, :]
@@ -605,12 +709,16 @@
                     held = count * value
                     first = first + held
                     second = second + held * value
-                return state, first, second
-
-            state, first, second = lax.fori_loop(0, T // 16, step, (zero, zero, zero))
+                ins = frames[pl.ds(pl.multiple_of(16 * i, 16), 16), cols].astype(f32)
+                return state, first, second, inward + ins[0:8, :] + ins[8:16, :]
+
+            state, first, second, inward = lax.fori_loop(
+                0, T // 16, step, (zero, zero, zero, zero)
+            )
             ends[:, cols] = state
             pay[e, 1:2, cols] = down(first)
             pay[e, 2:3, cols] = down(second)
+            pay[e, 3:4, cols] = down(inward)
 
         blocks(local_ends)
         run_power = power(par[decay_row : decay_row + 1, :], steps)
@@ -618,8 +726,8 @@
         for k in range(8):
             total = run_power * wide(aux[16 + k : 17 + k, :], H) * total + ends[k : k + 1, :]
         pay[e, 0:1, :] = total
-        pay[e, 3:8, :] = jnp.zeros((5, H), f32)
-        meanwhile(1)
+        pay[e, 4:8, :] = jnp.zeros((4, H), f32)
+        gap()
 
         own_decay = own_par[decay_row : decay_row + 1, :]
 
@@ -639,14 +747,19 @@
             frames_all = sums[0:1, :]
             average = sums[1:2, :] / frames_all
             inv_std = lax.rsqrt(sums[2:3, :] / frames_all - average * average + epsilon)
+            centre = sums[3:4, :] / (sz.valid * seqs)
             for i in range(n):
                 back[e, i, 1:2, :] = average
                 back[e, i, 2:3, :] = inv_std
                 back[e, i, 3:4, :] = frames_all
-                back[e, i, 4:8, :] = jnp.zeros((4, fb), f32)
-
-        exchange(e, gathered, totalled)
-        meanwhile(2)
+                back[e, i, 4:5, :] = centre
+                back[e, i, 5:8, :] = jnp.zeros((3, fb), f32)
+
+        exchange(e, gathered, totalled, gap)
+        centre = backland[e, 4:5, :]
+        frames[T : T + 16, :] = jnp.concatenate(
+            [-centre, -centre, -centre, jnp.zeros((13, H), f32)], axis=0
+        ).astype(bf16)
 
         total = backland[e, 0:1, :]
         for k in range(8):
@@ -681,9 +794,9 @@
             lax.fori_loop(0, T // 16, step, state)
 
         blocks(full_scan)
-        meanwhile(3)
-
-    def layer_backward(layer, upstream, projected, states, meanwhile):
+        gap()
+
+    def layer_backward(layer, upstream, projected, states, turned_grads, gap):
         e = 2 + (1 - layer)
         decay_row, gain_row, bias_row = DECAY + layer, GAIN + layer, BIAS + layer
         run_power = power(par[decay_row : decay_row + 1, :], steps)
@@ -748,7 +861,7 @@
             pay[e, 7:8, cols] = down(DA * scaled)
 
         blocks(local_ends)
-        meanwhile(0)
+        gap()
         own_decay = own_par[decay_row : decay_row + 1, :]
         own_gain = own_par[gain_row : gain_row + 1, :]
 
@@ -782,8 +895,7 @@
                 sums[3:4, :] - own_decay / spread * own_gain * rec_norm
             )
 
-        exchange(e, gathered, totalled)
-        meanwhile(1)
+        exchange(e, gathered, totalled, gap)
         total = backland[e, 0:1, :]
         for k in range(7, -1, -1):
             work[k : k + 1, :] = total
@@ -799,6 +911,7 @@
             rec_norm = spread8(backland.at[e], 2, cols) / frames_all * inv_std
 
             def step(o, carry):
+                carry, added = carry
                 i = T // 16 - 1 - o
                 rows = pl.ds(pl.multiple_of(16 * i, 16), 16)
                 pair = projected[rows, cols].astype(f32)
@@ -810,41 +923,103 @@
                     centred = pair[8 * h : 8 * h + 8, :] - average
                     outs[h] = scale * (run - count * (rec + rec_norm * centred))
                     carry = (decay * goes) * run
-                dp[rows, cols] = jnp.concatenate(outs, axis=0).astype(bf16)
-                return carry
-
-            lax.fori_loop(0, T // 16, step, work[0:8, cols])
+                rounded = jnp.concatenate(outs, axis=0).astype(bf16)
+                dp[rows, cols] = rounded
+                rounded = rounded.astype(f32)
+                return carry, added + rounded[0:8, :] + rounded[8:16, :]
+
+            _, added = lax.fori_loop(0, T // 16, step, (work[0:8, cols], zero))
+            whole = down(added)
+            sumpay[layer, 0:1, cols] = whole
+            high = whole.astype(bf16).astype(f32)
+            middle = (whole - high).astype(bf16).astype(f32)
+            low = whole - high - middle
+            dp[T : T + 16, cols] = jnp.concatenate(
+                [high, middle, low, jnp.zeros((13, L), f32)], axis=0
+            ).astype(bf16)
 
         blocks(full_scan)
-        meanwhile(2)
+        sumpay[layer, 1:8, :] = jnp.zeros((7, H), f32)
+        gap()
 
         def turn(b, _):
-            dpt[at(b, fb), :] = lax.dot_general(
+            turned_grads[at(b, fb), :] = lax.dot_general(
                 eye[...], dp[:, at(b, fb)], (((1,), (1,)), ((), ())), preferred_element_type=f32
             ).astype(bf16)
             return 0
 
         lax.fori_loop(0, n, turn, 0)
 
-    def input_gradient(weight, result):
-        def one(b, _):
-            result[:, at(b, fb)] = jnp.dot(
-                dp[...], weight[:, at(b, fb)], preferred_element_type=f32
-            ).astype(bf16)
-            return 0
-
-        lax.fori_loop(0, n, one, 0)
-
-    def relay_two(step):
-        if step == 0:
-            gather_two.advance(2)
-        elif step < 3:
-            gather_two.advance(3)
-
-    layer_forward(0, xr, wf_one, p_one, s_one, x_two, relay_two)
-    gather_two.finish()
-    others(lambda i: frames_sent(0, xs, i))
-    layer_forward(1, x_two, wf_two, p_two, s_two, xs, lambda step: None)
+    def input_gradient(weight, result, i):
+        result[:, at(i, fb)] = jnp.dot(
+            dp[0:T, :], weight[:, at(i, fb)], preferred_element_type=f32
+        ).astype(bf16)
+
+    def sum_copy(layer, i):
+        return neur_copy(
+            sumpay.at[layer, :, at(i, fb)],
+            sumland.at[layer, me],
+            sum_sends.at[layer, i],
+            sum_recvs.at[layer, me],
+            i,
+        )
+
+    def sum_along(layer, i):
+        return seq_copy(
+            sumseq.at[layer],
+            sumseqland.at[layer, mine],
+            sum_sends.at[layer, n + i],
+            sum_recvs.at[layer, n + mine],
+            i,
+        )
+
+    def sum_start(layer):
+        others(lambda i: sum_copy(layer, i).start())
+        sumland[layer, me] = sumpay[layer, :, own_lanes]
+
+    def sum_middle(layer):
+        def wait(i):
+            neur_copy(
+                sumpay.at[layer, :, at(i, fb)],
+                sumland.at[layer, i],
+                sum_sends.at[layer, i],
+                sum_recvs.at[layer, i],
+                i,
+            ).wait()
+
+        others(wait)
+        total = sumland[layer, 0]
+        for i in range(1, n):
+            total = total + sumland[layer, i]
+        sumseq[layer] = total
+        sumseqland[layer, mine] = total
+        others(lambda i: sum_along(layer, i).start(), seqs, mine)
+
+    def sum_finish(layer, frames, total):
+        def wait(i):
+            seq_copy(
+                sumseq.at[layer],
+                sumseqland.at[layer, i],
+                sum_sends.at[layer, n + i],
+                sum_recvs.at[layer, n + i],
+                i,
+            ).wait()
+
+        others(wait, seqs, mine)
+        whole = sumseqland[layer, 0]
+        for i in range(1, seqs):
+            whole = whole + sumseqland[layer, i]
+        whole = whole[0:1, :]
+        high = whole.astype(bf16).astype(f32)
+        middle = (whole - high).astype(bf16).astype(f32)
+        low = whole - high - middle
+        rows = jnp.concatenate([high, middle, low, jnp.zeros((13, fb), f32)], axis=0).astype(bf16)
+        columns = lax.dot_general(
+            eye[...], rows, (((1,), (1,)), ((), ())), preferred_element_type=f32
+        ).astype(bf16)
+        total[...] -= jnp.dot(
+            columns, frames[T : T + 16, at(mine, sz.qc)], preferred_element_type=f32
+        )
 
     def place_out(a, ref, dest, i):
         return neur_copy(
@@ -855,59 +1030,104 @@
         neur_copy(
             ref.at[:, at(i, fb)], dest.at[i], frame_sends.at[a, i], frame_recvs.at[a, i], i
         ).wait()
+
+    def run_next(steps):
+        if steps:
+            steps.pop(0)()
+
+    def send_g():
+        others(lambda i: frames_copy(1, gs.at[:, at(i, fb)], gr.at[:, own_lanes], i).start())
+
+    gather_two.steps.insert(2 * sz.Z - 3, send_g)
+    layer_forward(0, xr, wf_one, p_one, s_one, x_two, lambda: gather_two.advance(1))
+    gather_two.advance()
+    others(lambda i: frames_sent(0, xs, i))
+    layer_forward(1, x_two, wf_two, p_two, s_two, xs, lambda: None)
 
     others(lambda i: place_out(2, xs, out_land, i).start())
     keep_out = pltpu.make_async_copy(xs.at[:, own_lanes], out_land.at[me], local_sems.at[4])
     keep_out.start()
     others(lambda i: frames_wait(1, gr, i))
     others(lambda i: frames_sent(1, gs, i))
-
     gather_two.drain()
-    layer_backward(1, gr, p_two, s_two, lambda step: None)
-    input_gradient(wf_two, gr)
+
+    layer_backward(1, gr, p_two, s_two, dpt_two, lambda: None)
+    lax.fori_loop(0, n, lambda i, _: (input_gradient(wf_two, gr, i), 0)[1], 0)
+    sum_start(1)
     reduce_two = Reduce(
-        env, dpt, x_two, lambda k: land.at[k], stage, reduce_sends.at[0], reduce_recvs.at[0], "y", "x"
+        env,
+        dpt_two,
+        x_two,
+        lambda k: land.at[k],
+        spare.at[1],
+        stage,
+        fin.at[1],
+        reduce_sends.at[1],
+        reduce_recvs.at[1],
     )
     reduce_one = Reduce(
         env,
-        dpt,
+        dpt_one,
         xr,
-        lambda k: wf_two.at[at(k // 4, fb), at(k % 4, sz.qc)],
+        lambda k: wf_two.at[at(k // seqs, fb), at(k % seqs, sz.qc)],
+        spare.at[0],
         stage,
-        reduce_sends.at[1],
-        reduce_recvs.at[1],
-        "x",
-        "y",
+        fin.at[0],
+        reduce_sends.at[0],
+        reduce_recvs.at[0],
     )
     result_two = Result(
-        env, dw_two, fin.at[0], final_sends.at[0], final_recvs.at[0], local_sems.at[6]
+        env, dw_two, fin.at[1], final_sends.at[1], final_recvs.at[1], local_sems.at[6]
     )
     result_one = Result(
-        env, dw_one, fin.at[1], final_sends.at[1], final_recvs.at[1], local_sems.at[7]
-    )
-    reduce_two.cores()
-
-    def meanwhile(step):
-        if step == 0:
-            reduce_two.firsts()
-        if step == 1:
-            reduce_two.seconds()
-            reduce_two.lines()
-            fin[0] = reduce_two.total()
-            result_two.start()
-
-    layer_backward(0, gr, p_one, s_one, meanwhile)
-    input_gradient(wf_one, gs)
-    others(lambda i: place_out(3, gs, dx_land, i).start())
+        env, dw_one, fin.at[0], final_sends.at[0], final_recvs.at[0], local_sems.at[7]
+    )
+    for kind in range(4):
+        reduce_two.cores(kind)
+
+    half = sz.Z // 2
+    layer_backward(
+        0,
+        gr,
+        p_one,
+        s_one,
+        dpt_one,
+        functools.partial(
+            run_next,
+            [
+                reduce_two.diagonals,
+                functools.partial(sum_middle, 1),
+                functools.partial(reduce_two.sides, 0, half),
+                functools.partial(reduce_two.sides, half, sz.Z),
+            ],
+        ),
+    )
+    sum_start(0)
+    reduce_two.lines()
+    reduce_two.finish()
+    sum_finish(1, x_two, fin.at[1])
+    result_two.start()
+    reduce_two.drain()
+    for kind in range(2):
+        reduce_one.cores(kind)
+    reduce_one.diagonals()
+
+    def send_dx(i):
+        input_gradient(wf_one, gs, i)
+        place_out(3, gs, dx_land, i).start()
+
+    others(send_dx)
+    input_gradient(wf_one, gs, me)
     keep_dx = pltpu.make_async_copy(gs.at[:, own_lanes], dx_land.at[me], local_sems.at[5])
     keep_dx.start()
+    for kind in range(2, 4):
+        reduce_one.cores(kind)
+    sum_middle(0)
     result_two.finish()
-    reduce_two.drain()
-    reduce_one.cores()
-    reduce_one.firsts()
-    reduce_one.seconds()
+    reduce_one.sides()
     reduce_one.lines()
-    fin[1] = reduce_one.total()
+    reduce_one.finish()
+    sum_finish(0, xr, fin.at[0])
     result_one.start()
     others(lambda i: out_arrived(2, xs, out_land, i))
     others(lambda i: out_arrived(3, gs, dx_land, i))
@@ -980,7 +1200,7 @@
     whole = pl.BlockSpec(memory_space=pltpu.VMEM)
     anywhere = pl.BlockSpec(memory_space=pl.ANY)
     vmem, sem = pltpu.VMEM, pltpu.SemaphoreType.DMA
-    frames_shape = (T, H)
+    frames_shape, longer_shape = (T, H), (sz.K, H)
     matmul = 2 * T * H * H
     out_land, dx_land, dw_one, dw_two, small = pl.pallas_call(
         functools.partial(network, sz),
@@ -999,19 +1219,21 @@
             vmem((fb, fb), bf16),
             vmem(frames_shape, bf16),
             vmem(frames_shape, bf16),
+            vmem(longer_shape, bf16),
             vmem(frames_shape, bf16),
             vmem(frames_shape, bf16),
             vmem(frames_shape, bf16),
-            vmem(frames_shape, bf16),
-            vmem(frames_shape, bf16),
-            vmem(frames_shape, bf16),
-            vmem((H, T), bf16),
+            vmem(longer_shape, bf16),
+            vmem(longer_shape, bf16),
+            vmem((H, sz.K), bf16),
+            vmem((H, sz.K), bf16),
             vmem((T + 8, H), f32),
             vmem((T + 8, H), f32),
             vmem((H, H), bf16),
             vmem((H, H), bf16),
             vmem((8 * Z, fb, qc), bf16),
-            vmem((8 * Z, fb, qc), bf16),
+            vmem((5 * Z, fb, qc), bf16),
+            vmem((2, fb, qc), bf16),
             vmem((2, fb, qc), f32),
             vmem((8, H), f32),
             vmem((8, H), f32),
@@ -1022,21 +1244,27 @@
             vmem((4, seqs, 8, fb), f32),
             vmem((4, n, 8, fb), f32),
             vmem((4, 8, H), f32),
+            vmem((2, 8, H), f32),
+            vmem((2, n, 8, fb), f32),
+            vmem((2, 8, fb), f32),
+            vmem((2, seqs, 8, fb), f32),
             sem((8,)),
             sem((n,)),
             sem((n,)),
             sem((4, n)),
             sem((4, n)),
-            sem((2, 8 * Z)),
-            sem((2, 8 * Z)),
+            sem((2, 10 * Z)),
+            sem((2, 10 * Z)),
             sem((8, n)),
             sem((8, n)),
             sem((4, seqs)),
             sem((4, seqs)),
-            sem((2, 8 * Z)),
-            sem((2, 8 * Z)),
+            sem((2, 10 * Z)),
+            sem((2, 10 * Z)),
             sem((2, 3)),
             sem((2, 3)),
+            sem((2, n + seqs)),
+            sem((2, n + seqs)),
         ],
         compiler_params=pltpu.CompilerParams(
             collective_id=0, has_side_effects=True, vmem_limit_bytes=63 * 1024 * 1024

time: 471 us -> 434 us (0.921)
  Pallas kernels: 448 us -> 412 us
    pallas_call x1, Pallas kernels: 439 us -> 403 us  [frames_apart(): pl.pallas_call(functools.partial(network, sz), out_shape=(jax.ShapeDtypeS...]
where the time goes in v2:
time: 434 us; the launch traced here: 433 us
  Pallas kernels  412 us (95%)
  local copies, waits for them, and re-layouts  14.4 us (3%)
  other arithmetic  6.13 us (1%)
    pallas_call x1, Pallas kernels, frames_apart(): pl.pallas_call(functools.partial(network, sz), out_shape=(jax.ShapeDtypeS...  403 us
    pallas_call x1, Pallas kernels, frames_apart(): pl.pallas_call(functools.partial(turn_back, sz), grid=(steps,), out_shape...  8.97 us

profile of v2, /device:TPU:0, one launch (start us, length us, event | category | flops | bytes accessed | tf_op | source)
XLA Modules:
  0.0 433.2 jit_solution(3430820743015179167)
XLA Ops:
  0.6 0.8 dynamic-slice_compare_fusion
  1.4 0.1 gt.24
  1.5 0.8 reduce-window_clone.1
  2.4 1.3 fusion.10
  3.7 2.0 select_reduce_fusion
  5.6 0.6 mul.48
  6.3 0.2 select_reduce_fusion.1
  6.5 0.2 and_reduce_fusion.1
  6.7 0.1 pad_maximum_fusion
  6.8 0.1 compare_reduce_fusion
  6.9 1.4 concatenate.6.own_par
  8.3 0.1 copy.23
  8.4 0.1 gt.26
  8.5 0.7 and_select_fusion
  9.1 0.7 broadcast_in_dim.82.aux
  9.8 0.8 broadcast_in_dim.76.counted
  10.6 0.8 broadcast_in_dim.75.cont
  11.4 403.0 %network.1 = (bf16[8,448,256]{2,1,0:T(8,128)(2,1)}, bf16[8,448,256]{2,1,0:T(8,128)(2,1)}, f32[256,2048]{1,0:T(8,128)}, f32[256,2048]{1,0:T(8,128)}, f32[8,256]{1,0:T(8,128)}) custom-call(bf16[256,4096]{1,0:T(8,128)(2,1)} %x_ref.1, bf16[256,4096]{1,0:T(8,128)(2,1)} %g_ref.1, bf16[256,2048]{1,0:T(8,128)(2,1)} %w_one.1, bf16[256,2048]{1,0:T(8,128)(2,1)} %w_two.1, ...), custom_call_target="tpu_custom_call" | custom-call | flops 22548578304 | bytes 8388608 | tf_op jit(solution)/shard_map/network/pallas_call | solution.py:1205
  414.4 1.5 fusion.9
  415.9 0.0 copy-start
  415.9 1.6 copy-done
  417.5 0.0 copy-start.1
  417.5 1.5 copy-done.1
  419.0 0.0 copy-start.2
  419.0 1.5 copy-done.2
  420.5 0.0 copy-start.4
  420.5 9.0 %turn_back.1 = (f32[256,4096]{1,0:T(8,128)}, f32[256,4096]{1,0:T(8,128)}) custom-call(bf16[256,4096]{1,0:T(8,128)(2,1)S(1)} %copy-done, bf16[256,4096]{1,0:T(8,128)(2,1)} %g_ref.1, bf16[8,448,256]{2,1,0:T(8,128)(2,1)S(1)} %copy-done.1, bf16[8,448,256]{2,1,0:T(8,128)(2,1)S(1)} %copy-done.2), custom_call_target="tpu_custom_call" | custom-call | tf_op jit(solution)/shard_map/turn_back/pallas_call | solution.py:1282
  429.5 0.0 copy-done.4
  429.5 0.0 copy-start.3
  429.5 1.3 copy.26
  430.8 1.0 copy-done.3
  431.9 1.3 copy.27
  (8 shorter events, 0.0 us)
Async XLA Ops:
  415.9 1.6 copy-start
  417.5 1.5 copy-start.1
  419.0 1.5 copy-start.2
  420.5 9.0 %copy-start.4 = (f32[256,2048]{1,0:T(8,128)S(1)}, f32[256,2048]{1,0:T(8,128)}, u32[]{:S(2)}) copy-start(f32[256,2048]{1,0:T(8,128)} %get-tuple-element.50) | copy-start | bytes 6291460
  429.5 2.3 copy-start.3

commit v3 on v2

--- a/solution.py
+++ b/solution.py
@@ -102,18 +102,11 @@
 
 
 class Gather(Line):
-    def __init__(self, env, source, full, sends, recvs):
+    def __init__(self, env, source, full, sends, recvs, cut):
         super().__init__(env, sends, recvs)
+        self.cut = cut
         self.full = full
         self.source = source.at[:, at(env.s, env.sz.qc)]
-        Z = env.sz.Z
-        self.steps = []
-        for dz in range(1, Z):
-            self.steps.append(functools.partial(self.line, dz))
-            self.steps.append(functools.partial(self.sides, dz - 1))
-        self.steps.append(functools.partial(self.sides, Z - 1))
-        self.steps.append(self.diagonals)
-        self.steps.append(self.cores)
 
     def block(self, zz, fx, fy, fc=0):
         env = self.env
@@ -121,7 +114,9 @@
         return self.full.at[rows, at(2 * ((env.y + fy) % 2) + (env.c + fc) % 2, env.sz.qc)]
 
     def half(self, ref, h):
-        return ref.at[pl.ds(h * (self.env.sz.fb // 2), self.env.sz.fb // 2), :]
+        if h == 0:
+            return ref.at[pl.ds(0, self.cut), :]
+        return ref.at[pl.ds(self.cut, self.env.sz.fb - self.cut), :]
 
     def spread(self, zz, source):
         env, Z = self.env, self.env.sz.Z
@@ -200,10 +195,6 @@
             for zz in range(Z):
                 self.arrived((6 + k) * Z + zz, self.block(zz, fx, fy, 1))
 
-    def advance(self, count=None):
-        for _ in range(len(self.steps) if count is None else min(count, len(self.steps))):
-            self.steps.pop(0)()
-
     def drain(self):
         env, Z = self.env, self.env.sz.Z
         block = self.block(0, 0, 0)
@@ -212,15 +203,16 @@
             pl.when((zz >= env.z) & (env.z > 0))(lambda zz=zz: self.sent(Z + zz, block))
             for k in (2, 3, 6, 7, 8, 9):
                 self.sent(k * Z + zz, block)
-            for k in (4, 5):
-                self.sent(k * Z + zz, self.half(block, 0))
+            self.sent(4 * Z + zz, self.half(block, 0))
+            self.sent(5 * Z + zz, self.half(block, 1))
 
 
 class Reduce(Line):
     kinds = ((1, 1), (1, 0), (0, 1), (0, 0))
 
-    def __init__(self, env, grads, frames, land, spare, stage, total, sends, recvs):
+    def __init__(self, env, grads, frames, land, spare, stage, held, total, sends, recvs, relay):
         super().__init__(env, sends, recvs)
+        self.relay, self.held = relay, held
         self.grads, self.frames, self.land, self.spare = grads, frames, land, spare
         self.stage, self.total = stage, total
 
@@ -258,7 +250,7 @@
         env, Z = self.env, self.env.sz.Z
 
         def one(zz, _):
-            held = self.stage.at[2 * Z + zz]
+            held = self.held(zz)
             held[...] = (self.product(0, zz) + self.landed(zz, zz)).astype(bf16)
             slot = self.land(4 * Z + zz)
             for k, h, axis in ((4, 0, "x"), (5, 1, "y")):
@@ -300,6 +292,10 @@
 
     def lines(self):
         env, Z, z = self.env, self.env.sz.Z, self.env.z
+        if not self.relay:
+            for dz in range(1, Z):
+                self.straight((z + dz) % Z)
+            return
 
         def onward(zz, way):
             k, slot = (8 if way > 0 else 9) * Z + zz, 7 * Z + zz
@@ -309,9 +305,9 @@
             def _():
                 self.total[...] += self.landed(k, slot)
 
-            held = self.stage.at[2 * Z + zz]
+            held = self.held(zz)
             self.sent(4 * Z + zz, self.half(held, 0))
-            self.sent(5 * Z + zz, self.half(held, 0))
+            self.sent(5 * Z + zz, self.half(held, 1))
             held[...] = self.total[...].astype(bf16)
             target = {"neur": 2 * (z + way) + env.x}
             if way > 0:
@@ -324,9 +320,30 @@
             pl.when(Z - 1 - i > z)(functools.partial(onward, Z - 1 - i, 1))
             pl.when(i < z)(functools.partial(onward, i, -1))
 
+    def straight(self, zz):
+        env, Z, z = self.env, self.env.sz.Z, self.env.z
+        self.joined(zz)
+        held = self.held(zz)
+        self.sent(4 * Z + zz, self.half(held, 0))
+        self.sent(5 * Z + zz, self.half(held, 1))
+        held[...] = self.total[...].astype(bf16)
+        pltpu.make_async_remote_copy(
+            src_ref=held,
+            dst_ref=self.land(7 * Z + z),
+            send_sem=self.sends.at[8 * Z + zz],
+            recv_sem=self.recvs.at[8 * Z + z],
+            device_id={"neur": 2 * zz + env.x},
+            device_id_type=MESH,
+        ).start()
+
     def finish(self):
         Z, z = self.env.sz.Z, self.env.z
         self.joined(z)
+        if not self.relay:
+            for dz in range(1, Z):
+                zz = (z + dz) % Z
+                self.total[...] += self.landed(8 * Z + zz, 7 * Z + zz)
+            return
 
         @pl.when(z > 0)
         def _():
@@ -337,16 +354,27 @@
             self.arrived(9 * Z + z, self.spare)
             self.total[...] += self.spare[...].astype(f32)
 
+    def drain_cores(self):
+        for k in range(2 * self.env.sz.Z, 4 * self.env.sz.Z):
+            self.sent(k, self.stage.at[0])
+
+    def drain_sides(self):
+        for k in range(6 * self.env.sz.Z, 8 * self.env.sz.Z):
+            self.sent(k, self.stage.at[0])
+
     def drain(self):
         Z, z = self.env.sz.Z, self.env.z
         held = self.stage.at[0]
         for zz in range(Z):
-            for k in (2, 3, 6, 7):
-                self.sent(k * Z + zz, held)
             for k in (4, 5):
-                pl.when(zz == z)(lambda k=k, zz=zz: self.sent(k * Z + zz, self.half(held, 0)))
-            pl.when(zz > z)(lambda zz=zz: self.sent(8 * Z + zz, held))
-            pl.when(zz < z)(lambda zz=zz: self.sent(9 * Z + zz, held))
+                pl.when(zz == z)(
+                    lambda k=k, zz=zz: self.sent(k * Z + zz, self.half(held, k - 4))
+                )
+            if self.relay:
+                pl.when(zz > z)(lambda zz=zz: self.sent(8 * Z + zz, held))
+                pl.when(zz < z)(lambda zz=zz: self.sent(9 * Z + zz, held))
+            else:
+                pl.when(zz != z)(lambda zz=zz: self.sent(8 * Z + zz, held))
 
 
 class Result:
@@ -524,17 +552,19 @@
     others(lambda i: par_copy(i).start())
     par[:, own_lanes] = own_par[...]
 
-    gather_one = Gather(env, w_one, wf_one, gather_sends.at[0], gather_recvs.at[0])
-    gather_two = Gather(env, w_two, wf_two, gather_sends.at[1], gather_recvs.at[1])
+    cuts = (fb // 4, fb // 4)
+    gather_one = Gather(env, w_one, wf_one, gather_sends.at[0], gather_recvs.at[0], cuts[0])
+    gather_two = Gather(env, w_two, wf_two, gather_sends.at[1], gather_recvs.at[1], cuts[1])
     own_one = pltpu.make_async_copy(gather_one.source, gather_one.block(env.z, 0, 0), local_sems.at[2])
     own_two = pltpu.make_async_copy(gather_two.source, gather_two.block(env.z, 0, 0), local_sems.at[3])
     own_one.start()
     own_two.start()
     gather_one.start()
+    gather_two.start()
 
     row = lax.broadcasted_iota(jnp.int32, (T, sz.win), 0)
     column = lax.broadcasted_iota(jnp.int32, (T, sz.win), 1)
-    frame = (row % 8) * steps + row // 8
+    frame = (row & 7) * steps + (row >> 3)
     perm[0] = jnp.where(column == frame, 1.0, 0.0).astype(bf16)
     perm[1] = jnp.where(column == frame + sz.odd, 1.0, 0.0).astype(bf16)
     row = lax.broadcasted_iota(jnp.int32, (fb, fb), 0)
@@ -563,25 +593,44 @@
 
     load_x.wait()
 
+    def turn_x(i):
+        xs[:, at(i, fb)] = turned(i)
+
     def send_x(i):
-        xs[:, at(i, fb)] = turned(i)
         frames_copy(0, xs.at[:, at(i, fb)], xr.at[pl.ds(0, T), own_lanes], i).start()
 
-    others(send_x)
+    def send_all_x():
+        others(send_x)
+
+    others(turn_x)
     xr[0:T, own_lanes] = turned(me)
     load_g = pltpu.make_async_copy(g_hbm.at[:, pl.ds(0, sz.valid)], raw, local_sems.at[1])
     load_g.start()
-    gather_one.advance(2)
+    ends_of_line = (env.z == 0) | (env.z == sz.Z - 1)
+    pl.when(ends_of_line)(send_all_x)
+    for dz in range(1, sz.Z):
+        gather_one.line(dz)
+        gather_two.line(dz)
+        if dz == max(1, sz.Z - 2):
+            pl.when(jnp.logical_not(ends_of_line))(send_all_x)
+        gather_one.sides(dz - 1)
     load_g.wait()
 
     def turn_g(i):
         gs[:, at(i, fb)] = turned(i)
 
+    def send_g(i):
+        frames_copy(1, gs.at[:, at(i, fb)], gr.at[:, own_lanes], i).start()
+
     others(turn_g)
     gr[:, own_lanes] = turned(me)
-    gather_one.advance(len(gather_one.steps) - 1)
-    gather_two.start()
-    gather_one.advance()
+    gather_one.sides(sz.Z - 1)
+    others(send_g)
+    gather_one.diagonals()
+    for dz in range(sz.Z):
+        gather_two.sides(dz)
+    gather_two.diagonals()
+    gather_one.cores()
     own_one.wait()
     own_two.wait()
     others(lambda i: frames_wait(0, xr, i))
@@ -630,7 +679,7 @@
 
         others(lambda i: out_copy(i).start())
         arrive[e, me] = pay[e, :, own_lanes]
-        gap()
+        gap("hop_a")
 
         def out_wait(i):
             neur_copy(
@@ -660,7 +709,7 @@
 
         others(lambda i: along_copy(i).start(), seqs, mine)
         seqland[e, mine] = seqpay[e]
-        gap()
+        gap("hop_b")
         others(along_wait, seqs, mine)
         sums = seqland[e, 0]
         for i in range(1, seqs):
@@ -687,14 +736,14 @@
 
         others(lambda i: back_copy(i).start())
         backland[e, :, own_lanes] = back[e, me]
-        gap()
+        gap("hop_c")
         others(back_wait)
 
     def layer_forward(layer, frames, weight, projected, states, store, gap):
         e = layer
         decay_row, gain_row, bias_row = DECAY + layer, GAIN + layer, BIAS + layer
         project(frames, weight, projected)
-        gap()
+        gap("ends")
 
         def local_ends(cols):
             decay = spread8(par, decay_row, cols)
@@ -727,7 +776,6 @@
             total = run_power * wide(aux[16 + k : 17 + k, :], H) * total + ends[k : k + 1, :]
         pay[e, 0:1, :] = total
         pay[e, 4:8, :] = jnp.zeros((4, H), f32)
-        gap()
 
         own_decay = own_par[decay_row : decay_row + 1, :]
 
@@ -794,7 +842,6 @@
             lax.fori_loop(0, T // 16, step, state)
 
         blocks(full_scan)
-        gap()
 
     def layer_backward(layer, upstream, projected, states, turned_grads, gap):
         e = 2 + (1 - layer)
@@ -861,7 +908,6 @@
             pay[e, 7:8, cols] = down(DA * scaled)
 
         blocks(local_ends)
-        gap()
         own_decay = own_par[decay_row : decay_row + 1, :]
         own_gain = own_par[gain_row : gain_row + 1, :]
 
@@ -896,6 +942,7 @@
             )
 
         exchange(e, gathered, totalled, gap)
+        gap("scan")
         total = backland[e, 0:1, :]
         for k in range(7, -1, -1):
             work[k : k + 1, :] = total
@@ -940,7 +987,6 @@
 
         blocks(full_scan)
         sumpay[layer, 1:8, :] = jnp.zeros((7, H), f32)
-        gap()
 
         def turn(b, _):
             turned_grads[at(b, fb), :] = lax.dot_general(
@@ -1031,29 +1077,35 @@
             ref.at[:, at(i, fb)], dest.at[i], frame_sends.at[a, i], frame_recvs.at[a, i], i
         ).wait()
 
-    def run_next(steps):
-        if steps:
-            steps.pop(0)()
-
-    def send_g():
-        others(lambda i: frames_copy(1, gs.at[:, at(i, fb)], gr.at[:, own_lanes], i).start())
-
-    gather_two.steps.insert(2 * sz.Z - 3, send_g)
-    layer_forward(0, xr, wf_one, p_one, s_one, x_two, lambda: gather_two.advance(1))
-    gather_two.advance()
+    def nothing(name):
+        return None
+
+    layer_forward(0, xr, wf_one, p_one, s_one, x_two, nothing)
+    gather_two.cores()
     others(lambda i: frames_sent(0, xs, i))
-    layer_forward(1, x_two, wf_two, p_two, s_two, xs, lambda: None)
-
-    others(lambda i: place_out(2, xs, out_land, i).start())
+    layer_forward(1, x_two, wf_two, p_two, s_two, xs, nothing)
+
+    def send_out(low, high):
+        def one(o, _):
+            place_out(2, xs, out_land, (me + o) % n).start()
+            return 0
+
+        lax.fori_loop(low, high, one, 0)
+
     keep_out = pltpu.make_async_copy(xs.at[:, own_lanes], out_land.at[me], local_sems.at[4])
     keep_out.start()
     others(lambda i: frames_wait(1, gr, i))
     others(lambda i: frames_sent(1, gs, i))
     gather_two.drain()
 
-    layer_backward(1, gr, p_two, s_two, dpt_two, lambda: None)
+    send_out(1, 2)
+    layer_backward(
+        1, gr, p_two, s_two, dpt_two, lambda name: send_out(2, 3) if name == "scan" else None
+    )
+    send_out(3, 4)
     lax.fori_loop(0, n, lambda i, _: (input_gradient(wf_two, gr, i), 0)[1], 0)
     sum_start(1)
+    send_out(4, 5)
     reduce_two = Reduce(
         env,
         dpt_two,
@@ -1061,9 +1113,11 @@
         lambda k: land.at[k],
         spare.at[1],
         stage,
+        lambda k: stage.at[2 * sz.Z + k],
         fin.at[1],
         reduce_sends.at[1],
         reduce_recvs.at[1],
+        False,
     )
     reduce_one = Reduce(
         env,
@@ -1072,9 +1126,11 @@
         lambda k: wf_two.at[at(k // seqs, fb), at(k % seqs, sz.qc)],
         spare.at[0],
         stage,
+        lambda k: raw.at[:, at(k, sz.qc)],
         fin.at[0],
         reduce_sends.at[0],
         reduce_recvs.at[0],
+        True,
     )
     result_two = Result(
         env, dw_two, fin.at[1], final_sends.at[1], final_recvs.at[1], local_sems.at[6]
@@ -1084,56 +1140,51 @@
     )
     for kind in range(4):
         reduce_two.cores(kind)
-
-    half = sz.Z // 2
-    layer_backward(
-        0,
-        gr,
-        p_one,
-        s_one,
-        dpt_one,
-        functools.partial(
-            run_next,
-            [
-                reduce_two.diagonals,
-                functools.partial(sum_middle, 1),
-                functools.partial(reduce_two.sides, 0, half),
-                functools.partial(reduce_two.sides, half, sz.Z),
-            ],
-        ),
-    )
+    reduce_two.diagonals()
+
+    def meanwhile(name):
+        if name == "hop_b":
+            sum_middle(1)
+        if name == "scan":
+            reduce_two.sides()
+            send_out(5, 6)
+
+    layer_backward(0, gr, p_one, s_one, dpt_one, meanwhile)
+    reduce_two.drain_cores()
+    for kind in range(4):
+        reduce_one.cores(kind)
+    reduce_one.diagonals()
     sum_start(0)
+
+    def send_dx(i):
+        input_gradient(wf_one, gs, i)
+        place_out(3, gs, dx_land, i).start()
+
+    others(send_dx)
+    input_gradient(wf_one, gs, me)
+    send_out(6, n)
+    keep_dx = pltpu.make_async_copy(gs.at[:, own_lanes], dx_land.at[me], local_sems.at[5])
+    keep_dx.start()
     reduce_two.lines()
+    reduce_two.drain_sides()
+    sum_middle(0)
+    reduce_one.sides()
     reduce_two.finish()
     sum_finish(1, x_two, fin.at[1])
     result_two.start()
-    reduce_two.drain()
-    for kind in range(2):
-        reduce_one.cores(kind)
-    reduce_one.diagonals()
-
-    def send_dx(i):
-        input_gradient(wf_one, gs, i)
-        place_out(3, gs, dx_land, i).start()
-
-    others(send_dx)
-    input_gradient(wf_one, gs, me)
-    keep_dx = pltpu.make_async_copy(gs.at[:, own_lanes], dx_land.at[me], local_sems.at[5])
-    keep_dx.start()
-    for kind in range(2, 4):
-        reduce_one.cores(kind)
-    sum_middle(0)
-    result_two.finish()
-    reduce_one.sides()
     reduce_one.lines()
     reduce_one.finish()
     sum_finish(0, xr, fin.at[0])
     result_one.start()
+    result_two.finish()
     others(lambda i: out_arrived(2, xs, out_land, i))
     others(lambda i: out_arrived(3, gs, dx_land, i))
     keep_out.wait()
     keep_dx.wait()
     result_one.finish()
+    reduce_two.drain()
+    reduce_one.drain_cores()
+    reduce_one.drain_sides()
     reduce_one.drain()
     gather_one.drain()
     small[6:8, :] = jnp.zeros((2, fb), f32)
@@ -1149,7 +1200,7 @@
     def _():
         row = lax.broadcasted_iota(jnp.int32, (T, win), 0)
         column = lax.broadcasted_iota(jnp.int32, (T, win), 1)
-        frame = (row % 8) * sz.steps + row // 8
+        frame = (row & 7) * sz.steps + (row >> 3)
         row = lax.broadcasted_iota(jnp.int32, (fb, fb), 0)
         eye = jnp.where(row == lax.broadcasted_iota(jnp.int32, (fb, fb), 1), 1.0, 0.0).astype(bf16)
         for half in range(2):

time: 434 us -> 375 us (0.86)
  Pallas kernels: 412 us -> 353 us
    pallas_call x1, Pallas kernels: 403 us -> 344 us  [frames_apart(): pl.pallas_call(functools.partial(network, sz), out_shape=(jax.ShapeDtypeS...]
where the time goes in v3:
time: 375 us; the launch traced here: 374 us
  Pallas kernels  353 us (94%)
  local copies, waits for them, and re-layouts  14.4 us (4%)
  other arithmetic  6.13 us (2%)
    pallas_call x1, Pallas kernels, frames_apart(): pl.pallas_call(functools.partial(network, sz), out_shape=(jax.ShapeDtypeS...  344 us
    pallas_call x1, Pallas kernels, frames_apart(): pl.pallas_call(functools.partial(turn_back, sz), grid=(steps,), out_shape...  8.97 us
    unnamed x12, local copies, waits for them, and re-layouts  8.26 us

profile of v3, /device:TPU:0, one launch (start us, length us, event | category | flops | bytes accessed | tf_op | source)
XLA Modules:
  0.0 374.0 jit_solution(8563517792485063807)
XLA Ops:
  0.6 0.8 dynamic-slice_compare_fusion
  1.4 0.1 gt.24
  1.5 0.8 reduce-window_clone.1
  2.4 1.3 fusion.10
  3.7 2.0 select_reduce_fusion
  5.6 0.6 mul.48
  6.3 0.2 select_reduce_fusion.1
  6.5 0.2 and_reduce_fusion.1
  6.7 0.1 pad_maximum_fusion
  6.8 0.1 compare_reduce_fusion
  6.9 1.4 concatenate.6.own_par
  8.3 0.1 copy.23
  8.4 0.1 gt.26
  8.5 0.7 and_select_fusion
  9.1 0.7 broadcast_in_dim.82.aux
  9.8 0.8 broadcast_in_dim.76.counted
  10.6 0.8 broadcast_in_dim.75.cont
  11.4 343.8 %network.1 = (bf16[8,448,256]{2,1,0:T(8,128)(2,1)}, bf16[8,448,256]{2,1,0:T(8,128)(2,1)}, f32[256,2048]{1,0:T(8,128)}, f32[256,2048]{1,0:T(8,128)}, f32[8,256]{1,0:T(8,128)}) custom-call(bf16[256,4096]{1,0:T(8,128)(2,1)} %x_ref.1, bf16[256,4096]{1,0:T(8,128)(2,1)} %g_ref.1, bf16[256,2048]{1,0:T(8,128)(2,1)} %w_one.1, bf16[256,2048]{1,0:T(8,128)(2,1)} %w_two.1, ...), custom_call_target="tpu_custom_call" | custom-call | flops 22548578304 | bytes 8388608 | tf_op jit(solution)/shard_map/network/pallas_call | solution.py:1256
  355.3 1.5 fusion.9
  356.8 0.0 copy-start
  356.8 1.6 copy-done
  358.4 0.0 copy-start.1
  358.4 1.5 copy-done.1
  359.9 0.0 copy-start.2
  359.9 1.5 copy-done.2
  361.4 0.0 copy-start.4
  361.4 9.0 %turn_back.1 = (f32[256,4096]{1,0:T(8,128)}, f32[256,4096]{1,0:T(8,128)}) custom-call(bf16[256,4096]{1,0:T(8,128)(2,1)S(1)} %copy-done, bf16[256,4096]{1,0:T(8,128)(2,1)} %g_ref.1, bf16[8,448,256]{2,1,0:T(8,128)(2,1)S(1)} %copy-done.1, bf16[8,448,256]{2,1,0:T(8,128)(2,1)S(1)} %copy-done.2), custom_call_target="tpu_custom_call" | custom-call | tf_op jit(solution)/shard_map/turn_back/pallas_call | solution.py:1333
  370.4 0.0 copy-done.4
  370.4 0.0 copy-start.3
  370.4 1.3 copy.26
  371.7 1.0 copy-done.3
  372.7 1.3 copy.27
  (8 shorter events, 0.0 us)
Async XLA Ops:
  356.8 1.6 copy-start
  358.4 1.5 copy-start.1
  359.9 1.5 copy-start.2
  361.4 9.0 %copy-start.4 = (f32[256,2048]{1,0:T(8,128)S(1)}, f32[256,2048]{1,0:T(8,128)}, u32[]{:S(2)}) copy-start(f32[256,2048]{1,0:T(8,128)} %get-tuple-element.50) | copy-start | bytes 6291460
  370.4 2.3 copy-start.3

commit v4 on v3

--- a/solution.py
+++ b/solution.py
@@ -61,7 +61,7 @@
 
 
 def fits(n, seqs, H, fb, tok_dev):
-    if valid_frames % n or n % 2 or n > 8 or seqs != 4 or fb * n != H or fb % 128 or H % 512:
+    if n not in (4, 8) or valid_frames % n or seqs != 4 or fb * n != H or fb % 128 or H % 512:
         return False
     T = valid_frames // n
     return T % 64 == 0 and valid_frames % 128 == 0 and tok_dev >= valid_frames
@@ -210,9 +210,9 @@
 class Reduce(Line):
     kinds = ((1, 1), (1, 0), (0, 1), (0, 0))
 
-    def __init__(self, env, grads, frames, land, spare, stage, held, total, sends, recvs, relay):
+    def __init__(self, env, grads, frames, land, spare, stage, held, total, sends, recvs, cut):
         super().__init__(env, sends, recvs)
-        self.relay, self.held = relay, held
+        self.cut, self.held = cut, held
         self.grads, self.frames, self.land, self.spare = grads, frames, land, spare
         self.stage, self.total = stage, total
 
@@ -226,16 +226,25 @@
         )
 
     def half(self, ref, h):
-        return ref.at[pl.ds(h * (self.env.sz.fb // 2), self.env.sz.fb // 2), :]
+        if h == 0:
+            return ref.at[pl.ds(0, self.cut), :]
+        return ref.at[pl.ds(self.cut, self.env.sz.fb - self.cut), :]
 
     def landed(self, k, slot):
         self.arrived(k, self.land(slot))
         return self.land(slot)[...].astype(f32)
 
+    def turn(self, i):
+        z, Z = self.env.z, self.env.sz.Z
+        low = jnp.where(i < Z - 1 - z, Z - 1 - i, i - (Z - 1 - z))
+        high = jnp.where(i < z, i, Z - 1 - (i - z))
+        return jnp.where(i == Z - 1, z, jnp.where(z < Z // 2, low, high))
+
     def cores(self, kind):
         env, Z = self.env, self.env.sz.Z
 
-        def one(zz, _):
+        def one(i, _):
+            zz = self.turn(i)
             k = kind * Z + zz
             held = (kind % 2) * Z + zz
             if kind >= 2:
@@ -249,7 +258,8 @@
     def diagonals(self):
         env, Z = self.env, self.env.sz.Z
 
-        def one(zz, _):
+        def one(i, _):
+            zz = self.turn(i)
             held = self.held(zz)
             held[...] = (self.product(0, zz) + self.landed(zz, zz)).astype(bf16)
             slot = self.land(4 * Z + zz)
@@ -263,9 +273,10 @@
 
     def sides(self, low=0, high=None):
         env, Z = self.env, self.env.sz.Z
-        rows = env.sz.fb // 2
-
-        def one(zz, _):
+        spans = slice(0, self.cut), slice(self.cut, env.sz.fb)
+
+        def one(i, _):
+            zz = self.turn(i)
             slot = self.land(4 * Z + zz)
             for kind, h, wait, k, axis in ((1, 1, 5, 6, "x"), (2, 0, 4, 7, "y")):
                 tile = self.product(kind, zz) + self.landed(kind * Z + zz, kind * Z + zz)
@@ -273,10 +284,9 @@
                 self.arrived(wait * Z + zz, part)
                 held = self.stage.at[(2 + kind) * Z + zz]
                 other = 1 - h
-                own = slice(h * rows, (h + 1) * rows)
-                rest = slice(other * rows, (other + 1) * rows)
-                self.half(held, h)[...] = (tile[own, :] + part[...].astype(f32)).astype(bf16)
-                self.half(held, other)[...] = tile[rest, :].astype(bf16)
+                summed = tile[spans[h], :] + part[...].astype(f32)
+                self.half(held, h)[...] = summed.astype(bf16)
+                self.half(held, other)[...] = tile[spans[other], :].astype(bf16)
                 self.copy(
                     k * Z + zz, held, self.land((4 + kind) * Z + zz), env.across(axis)
                 ).start()
@@ -290,13 +300,8 @@
         tile = tile + self.landed(6 * Z + zz, 5 * Z + zz)
         self.total[...] = tile + self.landed(7 * Z + zz, 6 * Z + zz)
 
-    def lines(self):
+    def lines(self, low=0, high=None):
         env, Z, z = self.env, self.env.sz.Z, self.env.z
-        if not self.relay:
-            for dz in range(1, Z):
-                self.straight((z + dz) % Z)
-            return
-
         def onward(zz, way):
             k, slot = (8 if way > 0 else 9) * Z + zz, 7 * Z + zz
             self.joined(zz)
@@ -316,35 +321,14 @@
                 pl.when(zz == z - 1)(lambda: self.copy(k, held, self.spare, target).start())
                 pl.when(zz != z - 1)(lambda: self.copy(k, held, self.land(slot), target).start())
 
-        for i in range(Z - 1):
-            pl.when(Z - 1 - i > z)(functools.partial(onward, Z - 1 - i, 1))
-            pl.when(i < z)(functools.partial(onward, i, -1))
-
-    def straight(self, zz):
-        env, Z, z = self.env, self.env.sz.Z, self.env.z
-        self.joined(zz)
-        held = self.held(zz)
-        self.sent(4 * Z + zz, self.half(held, 0))
-        self.sent(5 * Z + zz, self.half(held, 1))
-        held[...] = self.total[...].astype(bf16)
-        pltpu.make_async_remote_copy(
-            src_ref=held,
-            dst_ref=self.land(7 * Z + z),
-            send_sem=self.sends.at[8 * Z + zz],
-            recv_sem=self.recvs.at[8 * Z + z],
-            device_id={"neur": 2 * zz + env.x},
-            device_id_type=MESH,
-        ).start()
+        for i in range(low, Z - 1 if high is None else high):
+            zz = self.turn(i)
+            pl.when(zz > z)(functools.partial(onward, zz, 1))
+            pl.when(zz < z)(functools.partial(onward, zz, -1))
 
     def finish(self):
         Z, z = self.env.sz.Z, self.env.z
         self.joined(z)
-        if not self.relay:
-            for dz in range(1, Z):
-                zz = (z + dz) % Z
-                self.total[...] += self.landed(8 * Z + zz, 7 * Z + zz)
-            return
-
         @pl.when(z > 0)
         def _():
             self.total[...] += self.landed(8 * Z + z, 7 * Z + z)
@@ -370,11 +354,8 @@
                 pl.when(zz == z)(
                     lambda k=k, zz=zz: self.sent(k * Z + zz, self.half(held, k - 4))
                 )
-            if self.relay:
-                pl.when(zz > z)(lambda zz=zz: self.sent(8 * Z + zz, held))
-                pl.when(zz < z)(lambda zz=zz: self.sent(9 * Z + zz, held))
-            else:
-                pl.when(zz != z)(lambda zz=zz: self.sent(8 * Z + zz, held))
+            pl.when(zz > z)(lambda zz=zz: self.sent(8 * Z + zz, held))
+            pl.when(zz < z)(lambda zz=zz: self.sent(9 * Z + zz, held))
 
 
 class Result:
@@ -432,15 +413,23 @@
     g_hbm,
     w_one,
     w_two,
-    own_par,
-    cont,
-    counted,
-    aux,
+    gain_one,
+    gain_two,
+    bias_one,
+    bias_two,
+    decay_one,
+    decay_two,
+    lengths,
+    frame_mask,
     out_land,
     dx_land,
     dw_one,
     dw_two,
     small,
+    own_par,
+    cont,
+    counted,
+    aux,
     raw,
     perm,
     eye,
@@ -512,6 +501,9 @@
         )
     load_x = pltpu.make_async_copy(x_hbm.at[:, pl.ds(0, sz.valid)], raw, local_sems.at[0])
     load_x.start()
+    for r, values in enumerate((gain_one, gain_two, bias_one, bias_two, decay_one, decay_two)):
+        own_par[r : r + 1, :] = values[...]
+    own_par[6:8, :] = jnp.zeros((2, fb), f32)
     pl.semaphore_wait(barrier, n - 1 + seqs - 1)
 
     def neur_copy(source, dest, send, recv, i):
@@ -533,6 +525,19 @@
             device_id={"seq": i},
             device_id_type=MESH,
         )
+
+    def part(body, low, high):
+        def one(o, _):
+            body((me + o) % n)
+            return 0
+
+        lax.fori_loop(low, high, one, 0)
+
+    def straight(body):
+        lax.fori_loop(1, n // 2, lambda o, _: (body((me + 2 * o) % n), 0)[1], 0)
+
+    def crossing(body):
+        lax.fori_loop(0, n // 2, lambda o, _: (body((me + 2 * o + 1) % n), 0)[1], 0)
 
     def others(body, count=n, own=me):
         def one(o, _):
@@ -614,7 +619,10 @@
         if dz == max(1, sz.Z - 2):
             pl.when(jnp.logical_not(ends_of_line))(send_all_x)
         gather_one.sides(dz - 1)
+    frame_tables_of(sz, me, lengths, frame_mask, perm, window(me), cont, counted, aux)
     load_g.wait()
+
+    g_first, g_second = max(2, n - 3), max(2, n - 1)
 
     def turn_g(i):
         gs[:, at(i, fb)] = turned(i)
@@ -625,11 +633,10 @@
     others(turn_g)
     gr[:, own_lanes] = turned(me)
     gather_one.sides(sz.Z - 1)
-    others(send_g)
+    part(send_g, 1, g_first)
     gather_one.diagonals()
-    for dz in range(sz.Z):
+    for dz in range(sz.Z - 1):
         gather_two.sides(dz)
-    gather_two.diagonals()
     gather_one.cores()
     own_one.wait()
     own_two.wait()
@@ -813,6 +820,8 @@
         for k in range(8):
             work[k : k + 1, :] = total
             total = run_power * wide(aux[16 + k : 17 + k, :], H) * total + ends[k : k + 1, :]
+
+        gap("scan")
 
         def full_scan(cols):
             decay = spread8(par, decay_row, cols)
@@ -1080,17 +1089,24 @@
     def nothing(name):
         return None
 
-    layer_forward(0, xr, wf_one, p_one, s_one, x_two, nothing)
+    def during_one(name):
+        if name == "ends":
+            gather_two.sides(sz.Z - 1)
+            gather_two.diagonals()
+        if name == "scan":
+            part(send_g, g_first, g_second)
+
+    def during_two(name):
+        if name == "scan":
+            part(send_g, g_second, n)
+
+    layer_forward(0, xr, wf_one, p_one, s_one, x_two, during_one)
     gather_two.cores()
     others(lambda i: frames_sent(0, xs, i))
-    layer_forward(1, x_two, wf_two, p_two, s_two, xs, nothing)
+    layer_forward(1, x_two, wf_two, p_two, s_two, xs, during_two)
 
     def send_out(low, high):
-        def one(o, _):
-            place_out(2, xs, out_land, (me + o) % n).start()
-            return 0
-
-        lax.fori_loop(low, high, one, 0)
+        part(lambda i: place_out(2, xs, out_land, i).start(), min(low, n), min(high, n))
 
     keep_out = pltpu.make_async_copy(xs.at[:, own_lanes], out_land.at[me], local_sems.at[4])
     keep_out.start()
@@ -1117,7 +1133,7 @@
         fin.at[1],
         reduce_sends.at[1],
         reduce_recvs.at[1],
-        False,
+        fb // 2,
     )
     reduce_one = Reduce(
         env,
@@ -1130,7 +1146,7 @@
         fin.at[0],
         reduce_sends.at[0],
         reduce_recvs.at[0],
-        True,
+        fb // 2,
     )
     result_two = Result(
         env, dw_two, fin.at[1], final_sends.at[1], final_recvs.at[1], local_sems.at[6]
@@ -1140,39 +1156,51 @@
     )
     for kind in range(4):
         reduce_two.cores(kind)
-    reduce_two.diagonals()
+    send_out(5, 6)
 
     def meanwhile(name):
         if name == "hop_b":
             sum_middle(1)
         if name == "scan":
-            reduce_two.sides()
-            send_out(5, 6)
+            reduce_two.diagonals()
+            send_out(6, n)
 
     layer_backward(0, gr, p_one, s_one, dpt_one, meanwhile)
     reduce_two.drain_cores()
-    for kind in range(4):
+    reduce_one.cores(0)
+    reduce_two.sides()
+    reduce_one.diagonals()
+    for kind in range(1, 4):
         reduce_one.cores(kind)
-    reduce_one.diagonals()
     sum_start(0)
 
     def send_dx(i):
+        place_out(3, gs, dx_land, i).start()
+
+    def make_dx(i):
         input_gradient(wf_one, gs, i)
-        place_out(3, gs, dx_land, i).start()
-
-    others(send_dx)
-    input_gradient(wf_one, gs, me)
-    send_out(6, n)
+
+    def make_and_send_dx(i):
+        make_dx(i)
+        send_dx(i)
+
+    straight(make_and_send_dx)
+    crossing(make_dx)
+    make_dx(me)
     keep_dx = pltpu.make_async_copy(gs.at[:, own_lanes], dx_land.at[me], local_sems.at[5])
     keep_dx.start()
     reduce_two.lines()
+    sum_middle(0)
     reduce_two.drain_sides()
-    sum_middle(0)
-    reduce_one.sides()
+    reduce_one.sides(0, 2)
     reduce_two.finish()
     sum_finish(1, x_two, fin.at[1])
     result_two.start()
-    reduce_one.lines()
+    for i in range(2, sz.Z):
+        reduce_one.lines(i - 2, i - 1)
+        reduce_one.sides(i, i + 1)
+    crossing(send_dx)
+    reduce_one.lines(sz.Z - 2, sz.Z - 1)
     reduce_one.finish()
     sum_finish(0, xr, fin.at[0])
     result_one.start()
@@ -1190,64 +1218,115 @@
     small[6:8, :] = jnp.zeros((2, fb), f32)
 
 
-def turn_back(sz, x_ref, g_ref, out_ref, dx_ref, output, input_grad):
+def frame_tables_of(sz, me, lengths, frame_mask, perm, window, cont, counted, aux):
+    T, steps = sz.T, sz.steps
+    starts, filled = [], 0
+    for k in range(lengths.shape[1]):
+        starts.append(filled)
+        filled = filled + lengths[0, k]
+    row = lax.broadcasted_iota(jnp.int32, (T, 128), 0)
+    slot = me * T + (row & 7) * steps + (row >> 3)
+    goes = jnp.ones((T, 128), f32)
+    for start in starts:
+        goes = jnp.where(slot == start, 0.0, goes)
+    cont[...] = goes
+    kept = jnp.where(frame_mask[0:1, window] > 0, 1.0, 0.0)
+    kept = jnp.broadcast_to(kept, (128, sz.win)).astype(bf16)
+    kept = lax.dot_general(
+        perm[me % 2], kept, (((1,), (1,)), ((), ())), preferred_element_type=f32
+    )
+    counted[...] = jnp.where(slot < filled, kept, 0.0)
+    run = lax.broadcasted_iota(jnp.int32, (8, 128), 0)
+    first = me * T + run * steps
+    behind = jnp.zeros((8, 128), jnp.int32)
+    whole, own = jnp.ones((8, 128), f32), jnp.ones((8, 128), f32)
+    for start in starts:
+        behind = jnp.where(first > start, jnp.maximum(behind, start), behind)
+        whole = jnp.where((run * T <= start) & (start < run * T + T), 0.0, whole)
+        own = jnp.where((first <= start) & (start < first + steps), 0.0, own)
+    aux[0:8, :] = (first - behind).astype(f32)
+    aux[8:16, :] = whole
+    aux[16:24, :] = own
+    place = lax.broadcasted_iota(jnp.int32, (1, sz.tok_dev), 1)
+    block = jnp.where((place < filled) & (frame_mask[...] > 0), 1.0, 0.0)
+    block = jnp.sum(block, axis=1, keepdims=True)
+    aux[24:32, :] = jnp.broadcast_to(block, (8, 128))
+
+
+def turn_back(
+    sz,
+    steps,
+    x_ref,
+    g_ref,
+    out_ref,
+    dx_ref,
+    one_ref,
+    two_ref,
+    small,
+    output,
+    input_grad,
+    dw_one,
+    dw_two,
+    gain_one,
+    bias_one,
+    decay_one,
+    gain_two,
+    bias_two,
+    decay_two,
+    perm,
+    eye,
+    held,
+    sems,
+):
     step = pl.program_id(0)
     T, fb, win, odd = sz.T, sz.fb, sz.win, sz.odd
-    output[...] = x_ref[...].astype(f32)
-    input_grad[...] = g_ref[...].astype(f32)
-
-    @pl.when(step < sz.n // 2)
+    pairs = ((one_ref, dw_one), (two_ref, dw_two))
+    reads = [pltpu.make_async_copy(a, held.at[k], sems.at[k]) for k, (a, _) in enumerate(pairs)]
+    writes = [pltpu.make_async_copy(held.at[k], b, sems.at[k]) for k, (_, b) in enumerate(pairs)]
+
+    @pl.when(step == 0)
     def _():
+        for move in reads:
+            move.start()
         row = lax.broadcasted_iota(jnp.int32, (T, win), 0)
         column = lax.broadcasted_iota(jnp.int32, (T, win), 1)
         frame = (row & 7) * sz.steps + (row >> 3)
+        perm[0] = jnp.where(column == frame, 1.0, 0.0).astype(bf16)
+        perm[1] = jnp.where(column == frame + odd, 1.0, 0.0).astype(bf16)
         row = lax.broadcasted_iota(jnp.int32, (fb, fb), 0)
-        eye = jnp.where(row == lax.broadcasted_iota(jnp.int32, (fb, fb), 1), 1.0, 0.0).astype(bf16)
+        column = lax.broadcasted_iota(jnp.int32, (fb, fb), 1)
+        eye[...] = jnp.where(row == column, 1.0, 0.0).astype(bf16)
+        rows = (gain_one, bias_one, decay_one, gain_two, bias_two, decay_two)
+        for r, ref in enumerate(rows):
+            ref[...] = small[r : r + 1, :]
+
+    output[...] = x_ref[...].astype(f32)
+    input_grad[...] = g_ref[...].astype(f32)
+
+    @pl.when(step < sz.n // 2)
+    def _():
         for half in range(2):
-            perm = jnp.where(column == frame + odd * half, 1.0, 0.0).astype(bf16)
             lanes = pl.ds((T - odd) * half, win)
             for source, result in ((out_ref, output), (dx_ref, input_grad)):
                 turned = lax.dot_general(
-                    eye, source[half], (((1,), (1,)), ((), ())), preferred_element_type=f32
+                    eye[...], source[half], (((1,), (1,)), ((), ())), preferred_element_type=f32
                 ).astype(bf16)
-                result[:, lanes] += jnp.dot(turned, perm, preferred_element_type=f32)
-
-
-def frame_rows(sz, lengths, frame_mask):
-    T, steps = sz.T, sz.steps
-    me = lax.axis_index("neur")
-    starts = jnp.cumsum(lengths[0]) - lengths[0]
-    row = jnp.arange(T, dtype=jnp.int32)
-    slots = me * T + (row % 8) * steps + row // 8
-    goes = jnp.where(jnp.any(slots[:, None] == starts[None, :], axis=1), 0.0, 1.0)
-    part = lax.dynamic_slice(frame_mask, (me * T,), (T,)).reshape(8, steps).T.reshape(T)
-    inside = slots < jnp.sum(lengths[0])
-    count = jnp.where((part > 0) & inside, 1.0, 0.0)
-    places = jnp.arange(frame_mask.shape[0], dtype=jnp.int32)
-    block = jnp.sum(jnp.where((places < jnp.sum(lengths[0])) & (frame_mask > 0), 1.0, 0.0))
-    run = jnp.arange(8, dtype=jnp.int32)
-    first = me * T + run * steps
-    behind = jnp.where(starts[None, :] < first[:, None], starts[None, :], 0)
-    since = (first - jnp.max(behind, axis=1)).astype(f32)
-
-    def unbroken(begin, length):
-        inside = (starts[None, :] >= begin[:, None]) & (starts[None, :] < begin[:, None] + length)
-        return jnp.where(jnp.any(inside, axis=1), 0.0, 1.0)
-
-    whole = unbroken(run * T, T)
-    own = unbroken(first, steps)
-    aux = jnp.concatenate([since, whole, own, jnp.full((8,), 1.0) * block]).astype(f32)
-
-    def lanes(values):
-        return jnp.broadcast_to(values.astype(f32)[:, None], (values.shape[0], 128))
-
-    return lanes(goes), lanes(count), lanes(aux)
+                result[:, lanes] += jnp.dot(turned, perm[half], preferred_element_type=f32)
+
+    @pl.when(step == 1)
+    def _():
+        for read, write in zip(reads, writes, strict=True):
+            read.wait()
+            write.start()
+
+    @pl.when(step == steps - 1)
+    def _():
+        for move in writes:
+            move.wait()
 
 
 def frames_apart(sz, inputs, weight_one, weight_two, params, lengths, frame_mask, out_grad):
     n, seqs, H, fb, T, Z, qc = sz.n, sz.seqs, sz.H, sz.fb, sz.T, sz.Z, sz.qc
-    goes, count, aux = frame_rows(sz, lengths, frame_mask)
-    own_par = jnp.concatenate([jnp.stack(params), jnp.zeros((2, fb), f32)], axis=0)
     whole = pl.BlockSpec(memory_space=pltpu.VMEM)
     anywhere = pl.BlockSpec(memory_space=pl.ANY)
     vmem, sem = pltpu.VMEM, pltpu.SemaphoreType.DMA
@@ -1262,9 +1341,13 @@
             jax.ShapeDtypeStruct((fb, H), f32),
             jax.ShapeDtypeStruct((8, fb), f32),
         ),
-        in_specs=[anywhere] * 4 + [whole] * 4,
+        in_specs=[anywhere] * 4 + [whole] * 6 + [pl.BlockSpec(memory_space=pltpu.SMEM), whole],
         out_specs=(anywhere, anywhere, anywhere, anywhere, whole),
         scratch_shapes=[
+            vmem((8, fb), f32),
+            vmem((T, 128), f32),
+            vmem((T, 128), f32),
+            vmem((32, 128), f32),
             vmem((fb, sz.valid), bf16),
             vmem((2, T, sz.win), bf16),
             vmem((fb, fb), bf16),
@@ -1324,21 +1407,41 @@
             flops=6 * matmul, bytes_accessed=16 * fb * H, transcendentals=6 * T * H
         ),
         name="network",
-    )(inputs, out_grad, weight_one, weight_two, own_par, goes, count, aux)
+    )(
+        inputs,
+        out_grad,
+        weight_one,
+        weight_two,
+        *(values.reshape(1, fb) for values in params),
+        lengths,
+        frame_mask.reshape(1, -1),
+    )
     tok = inputs.shape[1]
     pairs = n // 2
     steps = pl.cdiv(tok, 2 * T)
     frames_spec = pl.BlockSpec((fb, 2 * T), lambda p: (0, p))
     land_spec = pl.BlockSpec((2, T, fb), lambda p: (jnp.minimum(p, pairs - 1), 0, 0))
-    output, input_grad = pl.pallas_call(
-        functools.partial(turn_back, sz),
+    row_spec = pl.BlockSpec((1, fb), lambda p: (0, 0))
+    results = pl.pallas_call(
+        functools.partial(turn_back, sz, steps),
         grid=(steps,),
-        out_shape=(jax.ShapeDtypeStruct((fb, tok), f32),) * 2,
-        in_specs=[frames_spec, frames_spec, land_spec, land_spec],
-        out_specs=(frames_spec, frames_spec),
-        compiler_params=pltpu.CompilerParams(vmem_limit_bytes=48 * 1024 * 1024),
+        out_shape=(jax.ShapeDtypeStruct((fb, tok), f32),) * 2
+        + (jax.ShapeDtypeStruct((fb, H), f32),) * 2
+        + (jax.ShapeDtypeStruct((1, fb), f32),) * 6,
+        in_specs=[frames_spec, frames_spec, land_spec, land_spec, anywhere, anywhere]
+        + [pl.BlockSpec((8, fb), lambda p: (0, 0))],
+        out_specs=(frames_spec, frames_spec, anywhere, anywhere) + (row_spec,) * 6,
+        scratch_shapes=[
+            vmem((2, T, sz.win), bf16),
+            vmem((fb, fb), bf16),
+            vmem((2, fb, H), f32),
+            sem((2,)),
+        ],
+        compiler_params=pltpu.CompilerParams(vmem_limit_bytes=60 * 1024 * 1024),
         name="turn_back",
-    )(inputs, out_grad, out_land, dx_land)
+    )(inputs, out_grad, out_land, dx_land, dw_one, dw_two, small)
+    output, input_grad, dw_one, dw_two = results[:4]
+    small = [row.reshape(fb) for row in results[4:]]
     return (
         output,
         input_grad,

time: 375 us -> 333 us (0.89)
  Pallas kernels: 353 us -> 332 us
  local copies, waits for them, and re-layouts: 14.4 us -> 0 us
  other arithmetic: 6.13 us -> 0 us
    pallas_call x1, Pallas kernels: 344 us -> 321 us  [frames_apart(): pl.pallas_call(functools.partial(network, sz), out_shape=(jax.ShapeDtypeS...]
    unnamed x12 -> x0, local copies, waits for them, and re-layouts: 8.26 us -> none
where the time goes in v4:
time: 333 us
  Pallas kernels  332 us (100%)
    pallas_call x1, Pallas kernels, frames_apart(): pl.pallas_call(functools.partial(network, sz), out_shape=(jax.ShapeDtypeS...  321 us
    pallas_call x1, Pallas kernels, frames_apart(): pl.pallas_call(functools.partial(turn_back, sz, steps), grid=(steps,), ou...  10.7 us

profile of v4, /device:TPU:0, one launch (start us, length us, event | category | flops | bytes accessed | tf_op | source)
XLA Modules:
  0.0 332.8 jit_solution(17024977135448846952)
XLA Ops:
  0.6 321.3 %network.1 = (bf16[8,448,256]{2,1,0:T(8,128)(2,1)}, bf16[8,448,256]{2,1,0:T(8,128)(2,1)}, f32[256,2048]{1,0:T(8,128)}, f32[256,2048]{1,0:T(8,128)}, f32[8,256]{1,0:T(8,128)}) custom-call(bf16[256,4096]{1,0:T(8,128)(2,1)} %x_ref.1, bf16[256,4096]{1,0:T(8,128)(2,1)} %g_ref.1, bf16[256,2048]{1,0:T(8,128)(2,1)} %w_one.1, bf16[256,2048]{1,0:T(8,128)(2,1)} %w_two.1, ...), custom_call_target="tpu_custom_call" | custom-call | flops 22548578304 | bytes 8388608 | tf_op jit(solution)/shard_map/network/pallas_call | solution.py:1335
  321.9 10.7 %turn_back.1 = (f32[256,4096]{1,0:T(8,128)}, f32[256,4096]{1,0:T(8,128)}, f32[256,2048]{1,0:T(8,128)}, f32[256,2048]{1,0:T(8,128)}, f32[1,256]{1,0:T(1,128)}, /*...) custom-call(bf16[256,4096]{1,0:T(8,128)(2,1)} %x_ref.1, ...), custom_call_target="tpu_custom_call" | custom-call | tf_op jit(solution)/shard_map/turn_back/pallas_call | solution.py:1425

commit v5 on v4

--- a/solution.py
+++ b/solution.py
@@ -526,18 +526,11 @@
             device_id_type=MESH,
         )
 
-    def part(body, low, high):
-        def one(o, _):
-            body((me + o) % n)
-            return 0
-
-        lax.fori_loop(low, high, one, 0)
-
     def straight(body):
         lax.fori_loop(1, n // 2, lambda o, _: (body((me + 2 * o) % n), 0)[1], 0)
 
-    def crossing(body):
-        lax.fori_loop(0, n // 2, lambda o, _: (body((me + 2 * o + 1) % n), 0)[1], 0)
+    def crossing(body, low=0, high=n // 2):
+        lax.fori_loop(low, high, lambda o, _: (body((me + 2 * o + 1) % n), 0)[1], 0)
 
     def others(body, count=n, own=me):
         def one(o, _):
@@ -605,7 +598,8 @@
         frames_copy(0, xs.at[:, at(i, fb)], xr.at[pl.ds(0, T), own_lanes], i).start()
 
     def send_all_x():
-        others(send_x)
+        crossing(send_x)
+        straight(send_x)
 
     others(turn_x)
     xr[0:T, own_lanes] = turned(me)
@@ -622,8 +616,6 @@
     frame_tables_of(sz, me, lengths, frame_mask, perm, window(me), cont, counted, aux)
     load_g.wait()
 
-    g_first, g_second = max(2, n - 3), max(2, n - 1)
-
     def turn_g(i):
         gs[:, at(i, fb)] = turned(i)
 
@@ -633,7 +625,7 @@
     others(turn_g)
     gr[:, own_lanes] = turned(me)
     gather_one.sides(sz.Z - 1)
-    part(send_g, 1, g_first)
+    straight(send_g)
     gather_one.diagonals()
     for dz in range(sz.Z - 1):
         gather_two.sides(dz)
@@ -1094,19 +1086,19 @@
             gather_two.sides(sz.Z - 1)
             gather_two.diagonals()
         if name == "scan":
-            part(send_g, g_first, g_second)
+            crossing(send_g, 0, n // 4)
 
     def during_two(name):
         if name == "scan":
-            part(send_g, g_second, n)
+            crossing(send_g, n // 4, n // 2)
 
     layer_forward(0, xr, wf_one, p_one, s_one, x_two, during_one)
     gather_two.cores()
     others(lambda i: frames_sent(0, xs, i))
     layer_forward(1, x_two, wf_two, p_two, s_two, xs, during_two)
 
-    def send_out(low, high):
-        part(lambda i: place_out(2, xs, out_land, i).start(), min(low, n), min(high, n))
+    def send_out(i):
+        place_out(2, xs, out_land, i).start()
 
     keep_out = pltpu.make_async_copy(xs.at[:, own_lanes], out_land.at[me], local_sems.at[4])
     keep_out.start()
@@ -1114,14 +1106,21 @@
     others(lambda i: frames_sent(1, gs, i))
     gather_two.drain()
 
-    send_out(1, 2)
+    crossing(send_out, 0, 1)
     layer_backward(
-        1, gr, p_two, s_two, dpt_two, lambda name: send_out(2, 3) if name == "scan" else None
-    )
-    send_out(3, 4)
+        1,
+        gr,
+        p_two,
+        s_two,
+        dpt_two,
+        lambda name: crossing(send_out, 1, 2) if name == "scan" else None,
+    )
+    if n > 4:
+        crossing(send_out, 2, 3)
     lax.fori_loop(0, n, lambda i, _: (input_gradient(wf_two, gr, i), 0)[1], 0)
     sum_start(1)
-    send_out(4, 5)
+    if n > 4:
+        crossing(send_out, 3, 4)
     reduce_two = Reduce(
         env,
         dpt_two,
@@ -1149,21 +1148,20 @@
         fb // 2,
     )
     result_two = Result(
-        env, dw_two, fin.at[1], final_sends.at[1], final_recvs.at[1], local_sems.at[6]
+        env, dw_two, land.at[1], final_sends.at[1], final_recvs.at[1], local_sems.at[6]
     )
     result_one = Result(
-        env, dw_one, fin.at[0], final_sends.at[0], final_recvs.at[0], local_sems.at[7]
+        env, dw_one, land.at[0], final_sends.at[0], final_recvs.at[0], local_sems.at[7]
     )
     for kind in range(4):
         reduce_two.cores(kind)
-    send_out(5, 6)
 
     def meanwhile(name):
         if name == "hop_b":
             sum_middle(1)
         if name == "scan":
             reduce_two.diagonals()
-            send_out(6, n)
+            straight(send_out)
 
     layer_backward(0, gr, p_one, s_one, dpt_one, meanwhile)
     reduce_two.drain_cores()
@@ -1193,16 +1191,18 @@
     sum_middle(0)
     reduce_two.drain_sides()
     reduce_one.sides(0, 2)
-    reduce_two.finish()
-    sum_finish(1, x_two, fin.at[1])
-    result_two.start()
     for i in range(2, sz.Z):
         reduce_one.lines(i - 2, i - 1)
         reduce_one.sides(i, i + 1)
     crossing(send_dx)
+    reduce_two.finish()
+    sum_finish(1, x_two, fin.at[1])
+    land[1] = fin[1].astype(bf16)
+    result_two.start()
     reduce_one.lines(sz.Z - 2, sz.Z - 1)
     reduce_one.finish()
     sum_finish(0, xr, fin.at[0])
+    land[0] = fin[0].astype(bf16)
     result_one.start()
     result_two.finish()
     others(lambda i: out_arrived(2, xs, out_land, i))
@@ -1274,15 +1274,15 @@
     bias_two,
     decay_two,
     perm,
-    eye,
     held,
+    widened,
     sems,
 ):
     step = pl.program_id(0)
     T, fb, win, odd = sz.T, sz.fb, sz.win, sz.odd
     pairs = ((one_ref, dw_one), (two_ref, dw_two))
     reads = [pltpu.make_async_copy(a, held.at[k], sems.at[k]) for k, (a, _) in enumerate(pairs)]
-    writes = [pltpu.make_async_copy(held.at[k], b, sems.at[k]) for k, (_, b) in enumerate(pairs)]
+    writes = [pltpu.make_async_copy(widened.at[k], b, sems.at[k]) for k, (_, b) in enumerate(pairs)]
 
     @pl.when(step == 0)
     def _():
@@ -1293,9 +1293,6 @@
         frame = (row & 7) * sz.steps + (row >> 3)
         perm[0] = jnp.where(column == frame, 1.0, 0.0).astype(bf16)
         perm[1] = jnp.where(column == frame + odd, 1.0, 0.0).astype(bf16)
-        row = lax.broadcasted_iota(jnp.int32, (fb, fb), 0)
-        column = lax.broadcasted_iota(jnp.int32, (fb, fb), 1)
-        eye[...] = jnp.where(row == column, 1.0, 0.0).astype(bf16)
         rows = (gain_one, bias_one, decay_one, gain_two, bias_two, decay_two)
         for r, ref in enumerate(rows):
             ref[...] = small[r : r + 1, :]
@@ -1308,15 +1305,15 @@
         for half in range(2):
             lanes = pl.ds((T - odd) * half, win)
             for source, result in ((out_ref, output), (dx_ref, input_grad)):
-                turned = lax.dot_general(
-                    eye[...], source[half], (((1,), (1,)), ((), ())), preferred_element_type=f32
-                ).astype(bf16)
-                result[:, lanes] += jnp.dot(turned, perm[half], preferred_element_type=f32)
+                result[:, lanes] += lax.dot_general(
+                    source[half], perm[half], (((0,), (0,)), ((), ())), preferred_element_type=f32
+                )
 
     @pl.when(step == 1)
     def _():
-        for read, write in zip(reads, writes, strict=True):
+        for k, (read, write) in enumerate(zip(reads, writes, strict=True)):
             read.wait()
+            widened[k] = held[k].astype(f32)
             write.start()
 
     @pl.when(step == steps - 1)
@@ -1337,8 +1334,8 @@
         out_shape=(
             jax.ShapeDtypeStruct((n, T, fb), bf16),
             jax.ShapeDtypeStruct((n, T, fb), bf16),
-            jax.ShapeDtypeStruct((fb, H), f32),
-            jax.ShapeDtypeStruct((fb, H), f32),
+            jax.ShapeDtypeStruct((fb, H), bf16),
+            jax.ShapeDtypeStruct((fb, H), bf16),
             jax.ShapeDtypeStruct((8, fb), f32),
         ),
         in_specs=[anywhere] * 4 + [whole] * 6 + [pl.BlockSpec(memory_space=pltpu.SMEM), whole],
@@ -1433,7 +1430,7 @@
         out_specs=(frames_spec, frames_spec, anywhere, anywhere) + (row_spec,) * 6,
         scratch_shapes=[
             vmem((2, T, sz.win), bf16),
-            vmem((fb, fb), bf16),
+            vmem((2, fb, H), bf16),
             vmem((2, fb, H), f32),
             sem((2,)),
         ],

time: 333 us -> 316 us (0.949)
  Pallas kernels: 332 us -> 314 us
    pallas_call x1, Pallas kernels: 321 us -> 305 us  [frames_apart(): pl.pallas_call(functools.partial(network, sz), out_shape=(jax.ShapeDtypeS...]
where the time goes in v5:
time: 316 us; the launch traced here: 315 us
  Pallas kernels  314 us (99%)
    pallas_call x1, Pallas kernels, frames_apart(): pl.pallas_call(functools.partial(network, sz), out_shape=(jax.ShapeDtypeS...  305 us
    pallas_call x1, Pallas kernels, frames_apart(): pl.pallas_call(functools.partial(turn_back, sz, steps), grid=(steps,), ou...  9.5 us

profile of v5, /device:TPU:0, one launch (start us, length us, event | category | flops | bytes accessed | tf_op | source)
XLA Modules:
  0.0 315.1 jit_solution(2907205856245553186)
XLA Ops:
  0.6 304.7 %network.1 = (bf16[8,448,256]{2,1,0:T(8,128)(2,1)}, bf16[8,448,256]{2,1,0:T(8,128)(2,1)}, bf16[256,2048]{1,0:T(8,128)(2,1)}, bf16[256,2048]{1,0:T(8,128)(2,1)}, f32[8,256]{1,0:T(8,128)}) custom-call(bf16[256,4096]{1,0:T(8,128)(2,1)} %x_ref.1, bf16[256,4096]{1,0:T(8,128)(2,1)} %g_ref.1, bf16[256,2048]{1,0:T(8,128)(2,1)} %w_one.1, bf16[256,2048]{1,0:T(8,128)(2,1)} %w_two.1, ...), custom_call_target="tpu_custom_call" | custom-call | flops 22548578304 | bytes 8388608 | tf_op jit(solution)/shard_map/network/pallas_call | solution.py:1332
  305.4 9.5 %turn_back.1 = (f32[256,4096]{1,0:T(8,128)}, f32[256,4096]{1,0:T(8,128)}, f32[256,2048]{1,0:T(8,128)}, f32[256,2048]{1,0:T(8,128)}, f32[1,256]{1,0:T(1,128)}, /*...) custom-call(bf16[256,4096]{1,0:T(8,128)(2,1)} %x_ref.1, ...), custom_call_target="tpu_custom_call" | custom-call | tf_op jit(solution)/shard_map/turn_back/pallas_call | solution.py:1422

commit v6 on v5

--- a/solution.py
+++ b/solution.py
@@ -430,6 +430,7 @@
     cont,
     counted,
     aux,
+    frames_sum,
     raw,
     perm,
     eye,
@@ -550,7 +551,7 @@
     others(lambda i: par_copy(i).start())
     par[:, own_lanes] = own_par[...]
 
-    cuts = (fb // 4, fb // 4)
+    cuts = (fb // 4, 3 * fb // 8)
     gather_one = Gather(env, w_one, wf_one, gather_sends.at[0], gather_recvs.at[0], cuts[0])
     gather_two = Gather(env, w_two, wf_two, gather_sends.at[1], gather_recvs.at[1], cuts[1])
     own_one = pltpu.make_async_copy(gather_one.source, gather_one.block(env.z, 0, 0), local_sems.at[2])
@@ -625,9 +626,11 @@
     others(turn_g)
     gr[:, own_lanes] = turned(me)
     gather_one.sides(sz.Z - 1)
+    gather_two.sides(0)
     straight(send_g)
+    crossing(send_g, 0, 1)
     gather_one.diagonals()
-    for dz in range(sz.Z - 1):
+    for dz in range(1, sz.Z - 1):
         gather_two.sides(dz)
     gather_one.cores()
     own_one.wait()
@@ -644,15 +647,15 @@
 
     def project(frames, weight, result):
         def one(b, _):
-            result[:, at(b, fb)] = lax.dot_general(
+            result[:, at(b, 2 * fb)] = lax.dot_general(
                 frames[0:T, :],
-                weight[at(b, fb), :],
+                weight[at(b, 2 * fb), :],
                 (((1,), (1,)), ((), ())),
                 preferred_element_type=f32,
             ).astype(bf16)
             return 0
 
-        lax.fori_loop(0, n, one, 0)
+        lax.fori_loop(0, n // 2, one, 0)
 
     def flags(t):
         tile = pl.ds(pl.multiple_of(8 * t, 8), 8)
@@ -667,23 +670,26 @@
         return jnp.sum(value, axis=0, keepdims=True)
 
     def exchange(e, gathered, totalled, gap):
+        ahead = pl.ds(0, 4 if e < 2 else 8)
+        behind = pl.ds(0, 4)
+
         def out_copy(i):
             return neur_copy(
-                pay.at[e, :, at(i, fb)],
-                arrive.at[e, me],
+                pay.at[e, ahead, at(i, fb)],
+                arrive.at[e, me, ahead],
                 hop_sends.at[2 * e, i],
                 hop_recvs.at[2 * e, me],
                 i,
             )
 
         others(lambda i: out_copy(i).start())
-        arrive[e, me] = pay[e, :, own_lanes]
+        arrive[e, me, ahead] = pay[e, ahead, own_lanes]
         gap("hop_a")
 
         def out_wait(i):
             neur_copy(
-                pay.at[e, :, at(i, fb)],
-                arrive.at[e, i],
+                pay.at[e, ahead, at(i, fb)],
+                arrive.at[e, i, ahead],
                 hop_sends.at[2 * e, i],
                 hop_recvs.at[2 * e, i],
                 i,
@@ -717,8 +723,8 @@
 
         def back_copy(i):
             return neur_copy(
-                back.at[e, i],
-                backland.at[e, :, own_lanes],
+                back.at[e, i, behind],
+                backland.at[e, behind, own_lanes],
                 hop_sends.at[2 * e + 1, i],
                 hop_recvs.at[2 * e + 1, me],
                 i,
@@ -726,15 +732,15 @@
 
         def back_wait(i):
             neur_copy(
-                back.at[e, i],
-                backland.at[e, :, at(i, fb)],
+                back.at[e, i, behind],
+                backland.at[e, behind, at(i, fb)],
                 hop_sends.at[2 * e + 1, i],
                 hop_recvs.at[2 * e + 1, i],
                 i,
             ).wait()
 
         others(lambda i: back_copy(i).start())
-        backland[e, :, own_lanes] = back[e, me]
+        backland[e, behind, own_lanes] = back[e, me, behind]
         gap("hop_c")
         others(back_wait)
 
@@ -774,20 +780,20 @@
         for k in range(8):
             total = run_power * wide(aux[16 + k : 17 + k, :], H) * total + ends[k : k + 1, :]
         pay[e, 0:1, :] = total
-        pay[e, 4:8, :] = jnp.zeros((4, H), f32)
 
         own_decay = own_par[decay_row : decay_row + 1, :]
 
         def gathered():
             whole_power = power(own_decay, T)
             carried = jnp.zeros((1, fb), f32)
-            sums = jnp.zeros((8, fb), f32)
+            sums = jnp.zeros((4, fb), f32)
             for i in range(n):
-                rows = arrive[e, i]
+                rows = arrive[e, i, 0:4, :]
                 back[e, i, 0:1, :] = carried
                 carried = whole_power * wide(aux[8 + i : 9 + i, :], fb) * carried + rows[0:1, :]
                 sums = sums + rows
-            seqpay[e] = sums
+            seqpay[e, 0:4, :] = sums
+            seqpay[e, 4:8, :] = jnp.zeros((4, fb), f32)
             seqpay[e, 0:1, :] = wide(aux[24:25, :], fb)
 
         def totalled(sums):
@@ -798,12 +804,11 @@
             for i in range(n):
                 back[e, i, 1:2, :] = average
                 back[e, i, 2:3, :] = inv_std
-                back[e, i, 3:4, :] = frames_all
-                back[e, i, 4:5, :] = centre
-                back[e, i, 5:8, :] = jnp.zeros((3, fb), f32)
+                back[e, i, 3:4, :] = centre
+            frames_sum[...] = frames_all[:, 0:128]
 
         exchange(e, gathered, totalled, gap)
-        centre = backland[e, 4:5, :]
+        centre = backland[e, 3:4, :]
         frames[T : T + 16, :] = jnp.concatenate(
             [-centre, -centre, -centre, jnp.zeros((13, H), f32)], axis=0
         ).astype(bf16)
@@ -934,7 +939,7 @@
             for i in range(n):
                 back[e, i, 1:2, :] = rec
                 back[e, i, 2:3, :] = rec_norm
-                back[e, i, 3:8, :] = jnp.zeros((5, fb), f32)
+                back[e, i, 3:4, :] = jnp.zeros((1, fb), f32)
             spread = jnp.sqrt(1.0 - own_decay * own_decay)
             small[3 * layer : 3 * layer + 1, :] = spread * rec_norm
             small[3 * layer + 1 : 3 * layer + 2, :] = sums[2:3, :]
@@ -953,7 +958,7 @@
             decay = spread8(par, decay_row, cols)
             average = spread8(backland.at[layer], 1, cols)
             inv_std = spread8(backland.at[layer], 2, cols)
-            frames_all = spread8(backland.at[layer], 3, cols)
+            frames_all = wide(frames_sum[...], L)
             scale = jnp.sqrt(1.0 - decay * decay) * spread8(par, gain_row, cols) * inv_std
             rec = spread8(backland.at[e], 1, cols) / frames_all
             rec_norm = spread8(backland.at[e], 2, cols) / frames_all * inv_std
@@ -997,9 +1002,9 @@
 
         lax.fori_loop(0, n, turn, 0)
 
-    def input_gradient(weight, result, i):
-        result[:, at(i, fb)] = jnp.dot(
-            dp[0:T, :], weight[:, at(i, fb)], preferred_element_type=f32
+    def input_gradient(weight, result, columns):
+        result[:, columns] = jnp.dot(
+            dp[0:T, :], weight[:, columns], preferred_element_type=f32
         ).astype(bf16)
 
     def sum_copy(layer, i):
@@ -1086,11 +1091,11 @@
             gather_two.sides(sz.Z - 1)
             gather_two.diagonals()
         if name == "scan":
-            crossing(send_g, 0, n // 4)
+            crossing(send_g, 1, n // 2 - 1)
 
     def during_two(name):
         if name == "scan":
-            crossing(send_g, n // 4, n // 2)
+            crossing(send_g, max(1, n // 2 - 1), n // 2)
 
     layer_forward(0, xr, wf_one, p_one, s_one, x_two, during_one)
     gather_two.cores()
@@ -1117,7 +1122,7 @@
     )
     if n > 4:
         crossing(send_out, 2, 3)
-    lax.fori_loop(0, n, lambda i, _: (input_gradient(wf_two, gr, i), 0)[1], 0)
+    lax.fori_loop(0, n // 2, lambda i, _: (input_gradient(wf_two, gr, at(i, 2 * fb)), 0)[1], 0)
     sum_start(1)
     if n > 4:
         crossing(send_out, 3, 4)
@@ -1176,7 +1181,7 @@
         place_out(3, gs, dx_land, i).start()
 
     def make_dx(i):
-        input_gradient(wf_one, gs, i)
+        input_gradient(wf_one, gs, at(i, fb))
 
     def make_and_send_dx(i):
         make_dx(i)
@@ -1194,7 +1199,9 @@
     for i in range(2, sz.Z):
         reduce_one.lines(i - 2, i - 1)
         reduce_one.sides(i, i + 1)
-    crossing(send_dx)
+        if i == 2:
+            crossing(send_dx, 0, n // 4)
+    crossing(send_dx, n // 4 if sz.Z > 2 else 0, n // 2)
     reduce_two.finish()
     sum_finish(1, x_two, fin.at[1])
     land[1] = fin[1].astype(bf16)
@@ -1345,6 +1352,7 @@
             vmem((T, 128), f32),
             vmem((T, 128), f32),
             vmem((32, 128), f32),
+            vmem((1, 128), f32),
             vmem((fb, sz.valid), bf16),
             vmem((2, T, sz.win), bf16),
             vmem((fb, fb), bf16),

time: 316 us -> 302 us (0.956)
  Pallas kernels: 314 us -> 299 us
    pallas_call x1, Pallas kernels: 305 us -> 289 us  [frames_apart(): pl.pallas_call(functools.partial(network, sz), out_shape=(jax.ShapeDtypeS...]
where the time goes in v6:
time: 302 us; the launch traced here: 300 us
  Pallas kernels  299 us (99%)
    pallas_call x1, Pallas kernels, frames_apart(): pl.pallas_call(functools.partial(network, sz), out_shape=(jax.ShapeDtypeS...  289 us
    pallas_call x1, Pallas kernels, frames_apart(): pl.pallas_call(functools.partial(turn_back, sz, steps), grid=(steps,), ou...  9.53 us

profile of v6, /device:TPU:0, one launch (start us, length us, event | category | flops | bytes accessed | tf_op | source)
XLA Modules:
  0.0 299.6 jit_solution(1111299889505045997)
XLA Ops:
  0.6 289.2 %network.1 = (bf16[8,448,256]{2,1,0:T(8,128)(2,1)}, bf16[8,448,256]{2,1,0:T(8,128)(2,1)}, bf16[256,2048]{1,0:T(8,128)(2,1)}, bf16[256,2048]{1,0:T(8,128)(2,1)}, f32[8,256]{1,0:T(8,128)}) custom-call(bf16[256,4096]{1,0:T(8,128)(2,1)} %x_ref.1, bf16[256,4096]{1,0:T(8,128)(2,1)} %g_ref.1, bf16[256,2048]{1,0:T(8,128)(2,1)} %w_one.1, bf16[256,2048]{1,0:T(8,128)(2,1)} %w_two.1, ...), custom_call_target="tpu_custom_call" | custom-call | flops 22548578304 | bytes 8388608 | tf_op jit(solution)/shard_map/network/pallas_call | solution.py:1339
  289.9 9.5 %turn_back.1 = (f32[256,4096]{1,0:T(8,128)}, f32[256,4096]{1,0:T(8,128)}, f32[256,2048]{1,0:T(8,128)}, f32[256,2048]{1,0:T(8,128)}, f32[1,256]{1,0:T(1,128)}, /*...) custom-call(bf16[256,4096]{1,0:T(8,128)(2,1)} %x_ref.1, ...), custom_call_target="tpu_custom_call" | custom-call | tf_op jit(solution)/shard_map/turn_back/pallas_call | solution.py:1430

commit v7 on v6

--- a/solution.py
+++ b/solution.py
@@ -527,8 +527,8 @@
             device_id_type=MESH,
         )
 
-    def straight(body):
-        lax.fori_loop(1, n // 2, lambda o, _: (body((me + 2 * o) % n), 0)[1], 0)
+    def straight(body, low=1, high=n // 2):
+        lax.fori_loop(low, high, lambda o, _: (body((me + 2 * o) % n), 0)[1], 0)
 
     def crossing(body, low=0, high=n // 2):
         lax.fori_loop(low, high, lambda o, _: (body((me + 2 * o + 1) % n), 0)[1], 0)
@@ -630,7 +630,7 @@
     straight(send_g)
     crossing(send_g, 0, 1)
     gather_one.diagonals()
-    for dz in range(1, sz.Z - 1):
+    for dz in range(1, sz.Z):
         gather_two.sides(dz)
     gather_one.cores()
     own_one.wait()
@@ -1087,8 +1087,7 @@
         return None
 
     def during_one(name):
-        if name == "ends":
-            gather_two.sides(sz.Z - 1)
+        if name == "hop_c":
             gather_two.diagonals()
         if name == "scan":
             crossing(send_g, 1, n // 2 - 1)

time: 302 us -> 297 us (0.983)
  Pallas kernels: 299 us -> 295 us
    pallas_call x1, Pallas kernels: 289 us -> 285 us  [frames_apart(): pl.pallas_call(functools.partial(network, sz), out_shape=(jax.ShapeDtypeS...]
where the time goes in v7:
time: 297 us; the launch traced here: 296 us
  Pallas kernels  295 us (99%)
    pallas_call x1, Pallas kernels, frames_apart(): pl.pallas_call(functools.partial(network, sz), out_shape=(jax.ShapeDtypeS...  285 us
    pallas_call x1, Pallas kernels, frames_apart(): pl.pallas_call(functools.partial(turn_back, sz, steps), grid=(steps,), ou...  9.53 us

profile of v7, /device:TPU:0, one launch (start us, length us, event | category | flops | bytes accessed | tf_op | source)
XLA Modules:
  0.0 295.7 jit_solution(16927239624151520958)
XLA Ops:
  0.6 285.4 %network.1 = (bf16[8,448,256]{2,1,0:T(8,128)(2,1)}, bf16[8,448,256]{2,1,0:T(8,128)(2,1)}, bf16[256,2048]{1,0:T(8,128)(2,1)}, bf16[256,2048]{1,0:T(8,128)(2,1)}, f32[8,256]{1,0:T(8,128)}) custom-call(bf16[256,4096]{1,0:T(8,128)(2,1)} %x_ref.1, bf16[256,4096]{1,0:T(8,128)(2,1)} %g_ref.1, bf16[256,2048]{1,0:T(8,128)(2,1)} %w_one.1, bf16[256,2048]{1,0:T(8,128)(2,1)} %w_two.1, ...), custom_call_target="tpu_custom_call" | custom-call | flops 22548578304 | bytes 8388608 | tf_op jit(solution)/shard_map/network/pallas_call | solution.py:1338
  286.0 9.5 %turn_back.1 = (f32[256,4096]{1,0:T(8,128)}, f32[256,4096]{1,0:T(8,128)}, f32[256,2048]{1,0:T(8,128)}, f32[256,2048]{1,0:T(8,128)}, f32[1,256]{1,0:T(1,128)}, /*...) custom-call(bf16[256,4096]{1,0:T(8,128)(2,1)} %x_ref.1, ...), custom_call_target="tpu_custom_call" | custom-call | tf_op jit(solution)/shard_map/turn_back/pallas_call | solution.py:1429

commit v8 on v7

--- a/solution.py
+++ b/solution.py
@@ -606,6 +606,12 @@
     xr[0:T, own_lanes] = turned(me)
     load_g = pltpu.make_async_copy(g_hbm.at[:, pl.ds(0, sz.valid)], raw, local_sems.at[1])
     load_g.start()
+    def turn_g(i):
+        gs[:, at(i, fb)] = turned(i)
+
+    def send_g(i):
+        frames_copy(1, gs.at[:, at(i, fb)], gr.at[:, own_lanes], i).start()
+
     ends_of_line = (env.z == 0) | (env.z == sz.Z - 1)
     pl.when(ends_of_line)(send_all_x)
     for dz in range(1, sz.Z):
@@ -613,18 +619,11 @@
         gather_two.line(dz)
         if dz == max(1, sz.Z - 2):
             pl.when(jnp.logical_not(ends_of_line))(send_all_x)
+            frame_tables_of(sz, me, lengths, frame_mask, perm, window(me), cont, counted, aux)
+            load_g.wait()
+            others(turn_g)
+            gr[:, own_lanes] = turned(me)
         gather_one.sides(dz - 1)
-    frame_tables_of(sz, me, lengths, frame_mask, perm, window(me), cont, counted, aux)
-    load_g.wait()
-
-    def turn_g(i):
-        gs[:, at(i, fb)] = turned(i)
-
-    def send_g(i):
-        frames_copy(1, gs.at[:, at(i, fb)], gr.at[:, own_lanes], i).start()
-
-    others(turn_g)
-    gr[:, own_lanes] = turned(me)
     gather_one.sides(sz.Z - 1)
     gather_two.sides(0)
     straight(send_g)
@@ -1306,13 +1305,14 @@
     output[...] = x_ref[...].astype(f32)
     input_grad[...] = g_ref[...].astype(f32)
 
-    @pl.when(step < sz.n // 2)
+    @pl.when(step < sz.n // 4)
     def _():
-        for half in range(2):
-            lanes = pl.ds((T - odd) * half, win)
+        for part in range(4):
+            half = part % 2
+            lanes = pl.ds(2 * T * (part // 2) + (T - odd) * half, win)
             for source, result in ((out_ref, output), (dx_ref, input_grad)):
                 result[:, lanes] += lax.dot_general(
-                    source[half], perm[half], (((0,), (0,)), ((), ())), preferred_element_type=f32
+                    source[part], perm[half], (((0,), (0,)), ((), ())), preferred_element_type=f32
                 )
 
     @pl.when(step == 1)
@@ -1421,10 +1421,10 @@
         frame_mask.reshape(1, -1),
     )
     tok = inputs.shape[1]
-    pairs = n // 2
-    steps = pl.cdiv(tok, 2 * T)
-    frames_spec = pl.BlockSpec((fb, 2 * T), lambda p: (0, p))
-    land_spec = pl.BlockSpec((2, T, fb), lambda p: (jnp.minimum(p, pairs - 1), 0, 0))
+    groups = n // 4
+    steps = pl.cdiv(tok, 4 * T)
+    frames_spec = pl.BlockSpec((fb, 4 * T), lambda p: (0, p))
+    land_spec = pl.BlockSpec((4, T, fb), lambda p: (jnp.minimum(p, groups - 1), 0, 0))
     row_spec = pl.BlockSpec((1, fb), lambda p: (0, 0))
     results = pl.pallas_call(
         functools.partial(turn_back, sz, steps),

time: 297 us -> 296 us (level)
  no operation moved by 1% of the time
where the time goes in v8:
time: 296 us; the launch traced here: 295 us
  Pallas kernels  294 us (99%)
    pallas_call x1, Pallas kernels, frames_apart(): pl.pallas_call(functools.partial(network, sz), out_shape=(jax.ShapeDtypeS...  285 us
    pallas_call x1, Pallas kernels, frames_apart(): pl.pallas_call(functools.partial(turn_back, sz, steps), grid=(steps,), ou...  8.98 us

profile of v8, /device:TPU:0, one launch (start us, length us, event | category | flops | bytes accessed | tf_op | source)
XLA Modules:
  0.0 294.6 jit_solution(5792326747058467943)
XLA Ops:
  0.6 284.8 %network.1 = (bf16[8,448,256]{2,1,0:T(8,128)(2,1)}, bf16[8,448,256]{2,1,0:T(8,128)(2,1)}, bf16[256,2048]{1,0:T(8,128)(2,1)}, bf16[256,2048]{1,0:T(8,128)(2,1)}, f32[8,256]{1,0:T(8,128)}) custom-call(bf16[256,4096]{1,0:T(8,128)(2,1)} %x_ref.1, bf16[256,4096]{1,0:T(8,128)(2,1)} %g_ref.1, bf16[256,2048]{1,0:T(8,128)(2,1)} %w_one.1, bf16[256,2048]{1,0:T(8,128)(2,1)} %w_two.1, ...), custom_call_target="tpu_custom_call" | custom-call | flops 22548578304 | bytes 8388608 | tf_op jit(solution)/shard_map/network/pallas_call | solution.py:1338
  285.5 9.0 %turn_back.1 = (f32[256,4096]{1,0:T(8,128)}, f32[256,4096]{1,0:T(8,128)}, f32[256,2048]{1,0:T(8,128)}, f32[256,2048]{1,0:T(8,128)}, f32[1,256]{1,0:T(1,128)}, /*...) custom-call(bf16[256,4096]{1,0:T(8,128)(2,1)} %x_ref.1, ...), custom_call_target="tpu_custom_call" | custom-call | tf_op jit(solution)/shard_map/turn_back/pallas_call | solution.py:1429

commit v9 on v8

--- a/solution.py
+++ b/solution.py
@@ -551,7 +551,7 @@
     others(lambda i: par_copy(i).start())
     par[:, own_lanes] = own_par[...]
 
-    cuts = (fb // 4, 3 * fb // 8)
+    cuts = (fb // 4, 7 * fb // 16)
     gather_one = Gather(env, w_one, wf_one, gather_sends.at[0], gather_recvs.at[0], cuts[0])
     gather_two = Gather(env, w_two, wf_two, gather_sends.at[1], gather_recvs.at[1], cuts[1])
     own_one = pltpu.make_async_copy(gather_one.source, gather_one.block(env.z, 0, 0), local_sems.at[2])
@@ -1200,11 +1200,11 @@
         if i == 2:
             crossing(send_dx, 0, n // 4)
     crossing(send_dx, n // 4 if sz.Z > 2 else 0, n // 2)
+    reduce_one.lines(sz.Z - 2, sz.Z - 1)
     reduce_two.finish()
     sum_finish(1, x_two, fin.at[1])
     land[1] = fin[1].astype(bf16)
     result_two.start()
-    reduce_one.lines(sz.Z - 2, sz.Z - 1)
     reduce_one.finish()
     sum_finish(0, xr, fin.at[0])
     land[0] = fin[0].astype(bf16)

time: 296 us -> 296 us (level)
  no operation moved by 1% of the time
where the time goes in v9:
time: 296 us; the launch traced here: 295 us
  Pallas kernels  294 us (99%)
    pallas_call x1, Pallas kernels, frames_apart(): pl.pallas_call(functools.partial(network, sz), out_shape=(jax.ShapeDtypeS...  285 us
    pallas_call x1, Pallas kernels, frames_apart(): pl.pallas_call(functools.partial(turn_back, sz, steps), grid=(steps,), ou...  8.98 us

profile of v9, /device:TPU:0, one launch (start us, length us, event | category | flops | bytes accessed | tf_op | source)
XLA Modules:
  0.0 294.6 jit_solution(5669742896109393404)
XLA Ops:
  0.6 284.8 %network.1 = (bf16[8,448,256]{2,1,0:T(8,128)(2,1)}, bf16[8,448,256]{2,1,0:T(8,128)(2,1)}, bf16[256,2048]{1,0:T(8,128)(2,1)}, bf16[256,2048]{1,0:T(8,128)(2,1)}, f32[8,256]{1,0:T(8,128)}) custom-call(bf16[256,4096]{1,0:T(8,128)(2,1)} %x_ref.1, bf16[256,4096]{1,0:T(8,128)(2,1)} %g_ref.1, bf16[256,2048]{1,0:T(8,128)(2,1)} %w_one.1, bf16[256,2048]{1,0:T(8,128)(2,1)} %w_two.1, ...), custom_call_target="tpu_custom_call" | custom-call | flops 22548578304 | bytes 8388608 | tf_op jit(solution)/shard_map/network/pallas_call | solution.py:1338
  285.5 9.0 %turn_back.1 = (f32[256,4096]{1,0:T(8,128)}, f32[256,4096]{1,0:T(8,128)}, f32[256,2048]{1,0:T(8,128)}, f32[256,2048]{1,0:T(8,128)}, f32[1,256]{1,0:T(1,128)}, /*...) custom-call(bf16[256,4096]{1,0:T(8,128)(2,1)} %x_ref.1, ...), custom_call_target="tpu_custom_call" | custom-call | tf_op jit(solution)/shard_map/turn_back/pallas_call | solution.py:1429
